TPU v7x, 32 devices: a whole 2x2x4 slice. The times are simulated.
32 devices in a mesh: tm: 2 (over core), space: 16 (over z, y, x).
Axes of the slice: x: 2, y: 2, z: 4, core: 2. Of those that a mesh axis runs over, the one named last changes fastest.
Arguments:
- initial: float32 [64, 64, 128], P('space'), may hold values from -6 to 6
- guess: float32 [8, 64, 64, 128], P('tm', 'space'), may hold values from -6 to 6
- conduct: float32 [64, 64, 128], P('space'), may hold values from 0.3 to 3
- source: float32 [64, 64, 128], P('space'), may hold values from -6 to 6
- profile: float32 [64], P('tm'), may hold values from -1 to 1
Outputs:
- corrected: float32 [8, 64, 64, 128], P('tm', 'space')
- residual: float32 [8, 64, 64, 128], P('tm', 'space')
All inputs are finite; a program needn't handle non-finite values.
Results may differ from a plain program's by a relative error of at most 0.000048.
Values sent between devices are 32-bit elements; how exact they have to be, the bound alone decides.
No kernel may reach another device: no remote copies, remote signals or barrier semaphores. Data moves between devices by JAX's collectives and lax.ppermute only.
A program may use at most 64 MiB of HBM per device.

v0:
```python
from functools import partial

import jax
import jax.numpy as jnp
from jax import lax
from jax.sharding import PartitionSpec as P

COARSEN = 8
SWEEPS = 3


KAPPA_TOP = 3.0


def extended_2(cells, sides, width):
    for axis, dim in sides:
        count = lax.axis_size(axis)
        ends = count - 1
        head = lax.slice_in_dim(cells, 0, width, axis=dim)
        tail = lax.slice_in_dim(cells, cells.shape[dim] - width, cells.shape[dim], axis=dim)
        cells = jnp.concatenate(
            [
                lax.ppermute(tail, axis, [(i, (i + 1) % count) for i in range(ends)]),
                cells,
                lax.ppermute(head, axis, [((i + 1) % count, i) for i in range(ends)]),
            ],
            axis=dim,
        )
    return cells


def passed_along(value, axis, by):
    size = lax.axis_size(axis)
    pairs = [(i, i + by) for i in range(size) if 0 <= i + by < size]
    return lax.ppermute(value, axis, pairs)


def laplace(padded):
    framed = jnp.pad(padded, ((0, 0), (0, 0), (1, 1), (1, 1)))
    centre = framed[:, 1:-1, 1:-1, 1:-1]
    beside = framed[:, 2:, 1:-1, 1:-1] + framed[:, :-2, 1:-1, 1:-1]
    beside = beside + framed[:, 1:-1, 2:, 1:-1] + framed[:, 1:-1, :-2, 1:-1]
    beside = beside + framed[:, 1:-1, 1:-1, 2:] + framed[:, 1:-1, 1:-1, :-2]
    return 6.0 * centre - beside


def factors(top):
    middle = (top + 1.0) / 2.0
    spread = (top - 1.0) / 2.0
    return (middle, spread, middle / spread)


def advance_deep(start, amount, scale, top, extended):
    middle, spread, relative = factors(top)
    height = start.shape[1]
    depth = SWEEPS

    def window_coef(array, margin):
        return array[depth - margin : depth - margin + height + 2 * margin]

    widened = extended_2(start, (("space", 1),), SWEEPS)
    conduct_wide = extended[0]
    source_wide = extended[1]
    margin = depth - 1
    ratio_now = 1.0 / relative
    remain = amount * window_coef(source_wide, margin) - scale * window_coef(
        conduct_wide, margin
    ) * laplace(widened)
    update = remain / middle
    iterate = widened[:, depth - margin : depth - margin + height + 2 * margin] + update
    for sweep in range(SWEEPS - 1):
        margin = margin - 1
        applied = update[:, 1:-1] + scale * window_coef(conduct_wide, margin) * laplace(update)
        remain = remain[:, 1:-1] - applied
        ratio_next = 1.0 / (2.0 * relative - ratio_now)
        update = ratio_next * ratio_now * update[:, 1:-1] + 2.0 * ratio_next / spread * remain
        iterate = iterate[:, 1:-1] + update
        ratio_now = ratio_next
    return iterate


def body(initial, guess, conduct, source, profile):
    position = lax.axis_index("tm")
    first = position == 0
    local_count = guess.shape[0]
    amounts = profile.reshape(local_count, COARSEN)
    fine_top = 1.0 + 12.0 * KAPPA_TOP
    coarse_top = 1.0 + 12.0 * KAPPA_TOP * COARSEN
    extended = extended_2(jnp.stack([conduct, source], axis=0), (("space", 1),), SWEEPS)
    stepper = partial(advance_deep, extended=extended)

    def sweep_interval(entry):
        state = entry
        for inner in range(COARSEN):
            state = stepper(state, amounts[:, inner][:, None, None, None], 1.0, fine_top)
        return state

    def coarse_step(state):
        return stepper(state[None], 0.0, float(COARSEN), coarse_top)[0]

    previous = passed_along(guess[-1], "tm", 1)
    entry = jnp.concatenate([jnp.where(first, initial, previous)[None], guess[:-1]], axis=0)
    relaxed = sweep_interval(entry)
    carried = passed_along(relaxed[-1], "tm", 1)
    again = jnp.concatenate([jnp.where(first, initial, carried)[None], relaxed[:-1]], axis=0)
    residual = sweep_interval(again) - relaxed
    blank = jnp.zeros_like(residual)
    groups = lax.axis_size("tm")

    def chain_round(section, errors):
        incoming = passed_along(errors[-1], "tm", 1)
        running = incoming
        collected = []
        for slot in range(local_count):
            running = coarse_step(running) + residual[slot]
            collected.append(running)
        return jnp.stack(collected, axis=0)

    error = lax.fori_loop(0, groups, chain_round, blank)
    corrected = relaxed + error
    return (corrected, residual)


def solution(mesh):
    return jax.shard_map(
        body,
        mesh=mesh,
        in_specs=(
            P("space", None, None),
            P("tm", "space", None, None),
            P("space", None, None),
            P("space", None, None),
            P("tm"),
        ),
        out_specs=(P("tm", "space", None, None), P("tm", "space", None, None)),
        check_vma=False,
    )
```

profile of v0, /device:TPU:24, one launch (start us, length us, event | category | flops | bytes accessed | tf_op | source)
XLA Modules:
  0.0 507.2 jit_solution(4891732310906638419)
XLA Ops:
  21.6 5.8 %collective-permute-done.10 = f32[4,3,64,128]{3,2,1,0:T(8,128)S(1)} collective-permute-done((f32[4,3,64,128]{3,2,1,0:T(8,128)S(1)}, f32[4,3,64,128]{3,2,1,0:T(8,128)S(1)}, u32[]{:S(2)}, u32[]{:S(2)}) %collective-permute-start.10) | collective-permute-done | bytes 393248 | tf_op jit(solution)/shard_map/ppermute | solution.py:23
  27.4 7.3 %collective-permute-done.11 = f32[4,3,64,128]{3,2,1,0:T(8,128)S(1)} collective-permute-done((f32[4,3,64,128]{3,2,1,0:T(8,128)S(1)}, f32[4,3,64,128]{3,2,1,0:T(8,128)S(1)}, u32[]{:S(2)}, u32[]{:S(2)}) %collective-permute-start.11) | collective-permute-done | bytes 393248 | tf_op jit(solution)/shard_map/ppermute | solution.py:25
  51.0 9.0 %collective-permute-done.15 = f32[4,3,64,128]{3,2,1,0:T(8,128)S(1)} collective-permute-done((f32[4,3,64,128]{3,2,1,0:T(8,128)S(1)}, f32[4,3,64,128]{3,2,1,0:T(8,128)S(1)}, u32[]{:S(2)}, u32[]{:S(2)}) %collective-permute-start.15) | collective-permute-done | bytes 393248 | tf_op jit(solution)/shard_map/ppermute | solution.py:25
  70.6 6.3 %collective-permute-done.16 = f32[4,3,64,128]{3,2,1,0:T(8,128)S(1)} collective-permute-done((f32[4,3,64,128]{3,2,1,0:T(8,128)S(1)}, f32[4,3,64,128]{3,2,1,0:T(8,128)S(1)}, u32[]{:S(2)}, u32[]{:S(2)}) %collective-permute-start.16) | collective-permute-done | bytes 393248 | tf_op jit(solution)/shard_map/ppermute | solution.py:23
  76.9 6.7 %collective-permute-done.17 = f32[4,3,64,128]{3,2,1,0:T(8,128)S(1)} collective-permute-done((f32[4,3,64,128]{3,2,1,0:T(8,128)S(1)}, f32[4,3,64,128]{3,2,1,0:T(8,128)S(1)}, u32[]{:S(2)}, u32[]{:S(2)}) %collective-permute-start.17) | collective-permute-done | bytes 393248 | tf_op jit(solution)/shard_map/ppermute | solution.py:25
  94.1 6.3 %collective-permute-done.18 = f32[4,3,64,128]{3,2,1,0:T(8,128)S(1)} collective-permute-done((f32[4,3,64,128]{3,2,1,0:T(8,128)S(1)}, f32[4,3,64,128]{3,2,1,0:T(8,128)S(1)}, u32[]{:S(2)}, u32[]{:S(2)}) %collective-permute-start.18) | collective-permute-done | bytes 393248 | tf_op jit(solution)/shard_map/ppermute | solution.py:23
  100.5 9.0 %collective-permute-done.19 = f32[4,3,64,128]{3,2,1,0:T(8,128)S(1)} collective-permute-done((f32[4,3,64,128]{3,2,1,0:T(8,128)S(1)}, f32[4,3,64,128]{3,2,1,0:T(8,128)S(1)}, u32[]{:S(2)}, u32[]{:S(2)}) %collective-permute-start.19) | collective-permute-done | bytes 393248 | tf_op jit(solution)/shard_map/ppermute | solution.py:25
  120.2 6.2 %collective-permute-done.20 = f32[4,3,64,128]{3,2,1,0:T(8,128)S(1)} collective-permute-done((f32[4,3,64,128]{3,2,1,0:T(8,128)S(1)}, f32[4,3,64,128]{3,2,1,0:T(8,128)S(1)}, u32[]{:S(2)}, u32[]{:S(2)}) %collective-permute-start.20) | collective-permute-done | bytes 393248 | tf_op jit(solution)/shard_map/ppermute | solution.py:23
  126.4 6.7 %collective-permute-done.21 = f32[4,3,64,128]{3,2,1,0:T(8,128)S(1)} collective-permute-done((f32[4,3,64,128]{3,2,1,0:T(8,128)S(1)}, f32[4,3,64,128]{3,2,1,0:T(8,128)S(1)}, u32[]{:S(2)}, u32[]{:S(2)}) %collective-permute-start.21) | collective-permute-done | bytes 393248 | tf_op jit(solution)/shard_map/ppermute | solution.py:25
  143.6 6.3 %collective-permute-done.22 = f32[4,3,64,128]{3,2,1,0:T(8,128)S(1)} collective-permute-done((f32[4,3,64,128]{3,2,1,0:T(8,128)S(1)}, f32[4,3,64,128]{3,2,1,0:T(8,128)S(1)}, u32[]{:S(2)}, u32[]{:S(2)}) %collective-permute-start.22) | collective-permute-done | bytes 393248 | tf_op jit(solution)/shard_map/ppermute | solution.py:23
  150.0 9.0 %collective-permute-done.23 = f32[4,3,64,128]{3,2,1,0:T(8,128)S(1)} collective-permute-done((f32[4,3,64,128]{3,2,1,0:T(8,128)S(1)}, f32[4,3,64,128]{3,2,1,0:T(8,128)S(1)}, u32[]{:S(2)}, u32[]{:S(2)}) %collective-permute-start.23) | collective-permute-done | bytes 393248 | tf_op jit(solution)/shard_map/ppermute | solution.py:25
  169.6 6.3 %collective-permute-done.24 = f32[4,3,64,128]{3,2,1,0:T(8,128)S(1)} collective-permute-done((f32[4,3,64,128]{3,2,1,0:T(8,128)S(1)}, f32[4,3,64,128]{3,2,1,0:T(8,128)S(1)}, u32[]{:S(2)}, u32[]{:S(2)}) %collective-permute-start.24) | collective-permute-done | bytes 393248 | tf_op jit(solution)/shard_map/ppermute | solution.py:23
  175.9 6.7 %collective-permute-done.25 = f32[4,3,64,128]{3,2,1,0:T(8,128)S(1)} collective-permute-done((f32[4,3,64,128]{3,2,1,0:T(8,128)S(1)}, f32[4,3,64,128]{3,2,1,0:T(8,128)S(1)}, u32[]{:S(2)}, u32[]{:S(2)}) %collective-permute-start.25) | collective-permute-done | bytes 393248 | tf_op jit(solution)/shard_map/ppermute | solution.py:25
  193.1 6.3 %collective-permute-done.26 = f32[4,3,64,128]{3,2,1,0:T(8,128)S(1)} collective-permute-done((f32[4,3,64,128]{3,2,1,0:T(8,128)S(1)}, f32[4,3,64,128]{3,2,1,0:T(8,128)S(1)}, u32[]{:S(2)}, u32[]{:S(2)}) %collective-permute-start.26) | collective-permute-done | bytes 393248 | tf_op jit(solution)/shard_map/ppermute | solution.py:23
  199.5 9.0 %collective-permute-done.27 = f32[4,3,64,128]{3,2,1,0:T(8,128)S(1)} collective-permute-done((f32[4,3,64,128]{3,2,1,0:T(8,128)S(1)}, f32[4,3,64,128]{3,2,1,0:T(8,128)S(1)}, u32[]{:S(2)}, u32[]{:S(2)}) %collective-permute-start.27) | collective-permute-done | bytes 393248 | tf_op jit(solution)/shard_map/ppermute | solution.py:25
  221.4 7.5 %collective-permute-done.29 = f32[4,3,64,128]{3,2,1,0:T(8,128)S(1)} collective-permute-done((f32[4,3,64,128]{3,2,1,0:T(8,128)S(1)}, f32[4,3,64,128]{3,2,1,0:T(8,128)S(1)}, u32[]{:S(2)}, u32[]{:S(2)}) %collective-permute-start.29) | collective-permute-done | bytes 393248 | tf_op jit(solution)/shard_map/ppermute | solution.py:23
  228.9 6.4 %collective-permute-done.30 = f32[4,3,64,128]{3,2,1,0:T(8,128)S(1)} collective-permute-done((f32[4,3,64,128]{3,2,1,0:T(8,128)S(1)}, f32[4,3,64,128]{3,2,1,0:T(8,128)S(1)}, u32[]{:S(2)}, u32[]{:S(2)}) %collective-permute-start.30) | collective-permute-done | bytes 393248 | tf_op jit(solution)/shard_map/ppermute | solution.py:25
  246.1 6.5 %collective-permute-done.31 = f32[4,3,64,128]{3,2,1,0:T(8,128)S(1)} collective-permute-done((f32[4,3,64,128]{3,2,1,0:T(8,128)S(1)}, f32[4,3,64,128]{3,2,1,0:T(8,128)S(1)}, u32[]{:S(2)}, u32[]{:S(2)}) %collective-permute-start.31) | collective-permute-done | bytes 393248 | tf_op jit(solution)/shard_map/ppermute | solution.py:23
  252.6 8.9 %collective-permute-done.32 = f32[4,3,64,128]{3,2,1,0:T(8,128)S(1)} collective-permute-done((f32[4,3,64,128]{3,2,1,0:T(8,128)S(1)}, f32[4,3,64,128]{3,2,1,0:T(8,128)S(1)}, u32[]{:S(2)}, u32[]{:S(2)}) %collective-permute-start.32) | collective-permute-done | bytes 393248 | tf_op jit(solution)/shard_map/ppermute | solution.py:25
  272.1 6.4 %collective-permute-done.33 = f32[4,3,64,128]{3,2,1,0:T(8,128)S(1)} collective-permute-done((f32[4,3,64,128]{3,2,1,0:T(8,128)S(1)}, f32[4,3,64,128]{3,2,1,0:T(8,128)S(1)}, u32[]{:S(2)}, u32[]{:S(2)}) %collective-permute-start.33) | collective-permute-done | bytes 393248 | tf_op jit(solution)/shard_map/ppermute | solution.py:23
  278.5 6.7 %collective-permute-done.34 = f32[4,3,64,128]{3,2,1,0:T(8,128)S(1)} collective-permute-done((f32[4,3,64,128]{3,2,1,0:T(8,128)S(1)}, f32[4,3,64,128]{3,2,1,0:T(8,128)S(1)}, u32[]{:S(2)}, u32[]{:S(2)}) %collective-permute-start.34) | collective-permute-done | bytes 393248 | tf_op jit(solution)/shard_map/ppermute | solution.py:25
  295.8 6.3 %collective-permute-done.35 = f32[4,3,64,128]{3,2,1,0:T(8,128)S(1)} collective-permute-done((f32[4,3,64,128]{3,2,1,0:T(8,128)S(1)}, f32[4,3,64,128]{3,2,1,0:T(8,128)S(1)}, u32[]{:S(2)}, u32[]{:S(2)}) %collective-permute-start.35) | collective-permute-done | bytes 393248 | tf_op jit(solution)/shard_map/ppermute | solution.py:23
  302.1 8.9 %collective-permute-done.36 = f32[4,3,64,128]{3,2,1,0:T(8,128)S(1)} collective-permute-done((f32[4,3,64,128]{3,2,1,0:T(8,128)S(1)}, f32[4,3,64,128]{3,2,1,0:T(8,128)S(1)}, u32[]{:S(2)}, u32[]{:S(2)}) %collective-permute-start.36) | collective-permute-done | bytes 393248 | tf_op jit(solution)/shard_map/ppermute | solution.py:25
  321.7 6.3 %collective-permute-done.37 = f32[4,3,64,128]{3,2,1,0:T(8,128)S(1)} collective-permute-done((f32[4,3,64,128]{3,2,1,0:T(8,128)S(1)}, f32[4,3,64,128]{3,2,1,0:T(8,128)S(1)}, u32[]{:S(2)}, u32[]{:S(2)}) %collective-permute-start.37) | collective-permute-done | bytes 393248 | tf_op jit(solution)/shard_map/ppermute | solution.py:23
  328.0 6.8 %collective-permute-done.38 = f32[4,3,64,128]{3,2,1,0:T(8,128)S(1)} collective-permute-done((f32[4,3,64,128]{3,2,1,0:T(8,128)S(1)}, f32[4,3,64,128]{3,2,1,0:T(8,128)S(1)}, u32[]{:S(2)}, u32[]{:S(2)}) %collective-permute-start.38) | collective-permute-done | bytes 393248 | tf_op jit(solution)/shard_map/ppermute | solution.py:25
  345.3 6.3 %collective-permute-done.39 = f32[4,3,64,128]{3,2,1,0:T(8,128)S(1)} collective-permute-done((f32[4,3,64,128]{3,2,1,0:T(8,128)S(1)}, f32[4,3,64,128]{3,2,1,0:T(8,128)S(1)}, u32[]{:S(2)}, u32[]{:S(2)}) %collective-permute-start.39) | collective-permute-done | bytes 393248 | tf_op jit(solution)/shard_map/ppermute | solution.py:23
  351.7 8.9 %collective-permute-done.40 = f32[4,3,64,128]{3,2,1,0:T(8,128)S(1)} collective-permute-done((f32[4,3,64,128]{3,2,1,0:T(8,128)S(1)}, f32[4,3,64,128]{3,2,1,0:T(8,128)S(1)}, u32[]{:S(2)}, u32[]{:S(2)}) %collective-permute-start.40) | collective-permute-done | bytes 393248 | tf_op jit(solution)/shard_map/ppermute | solution.py:25
  371.4 6.1 %collective-permute-done.41 = f32[4,3,64,128]{3,2,1,0:T(8,128)S(1)} collective-permute-done((f32[4,3,64,128]{3,2,1,0:T(8,128)S(1)}, f32[4,3,64,128]{3,2,1,0:T(8,128)S(1)}, u32[]{:S(2)}, u32[]{:S(2)}) %collective-permute-start.41) | collective-permute-done | bytes 393248 | tf_op jit(solution)/shard_map/ppermute | solution.py:23
  377.5 6.8 %collective-permute-done.42 = f32[4,3,64,128]{3,2,1,0:T(8,128)S(1)} collective-permute-done((f32[4,3,64,128]{3,2,1,0:T(8,128)S(1)}, f32[4,3,64,128]{3,2,1,0:T(8,128)S(1)}, u32[]{:S(2)}, u32[]{:S(2)}) %collective-permute-start.42) | collective-permute-done | bytes 393248 | tf_op jit(solution)/shard_map/ppermute | solution.py:25
  394.8 6.3 %collective-permute-done.43 = f32[4,3,64,128]{3,2,1,0:T(8,128)S(1)} collective-permute-done((f32[4,3,64,128]{3,2,1,0:T(8,128)S(1)}, f32[4,3,64,128]{3,2,1,0:T(8,128)S(1)}, u32[]{:S(2)}, u32[]{:S(2)}) %collective-permute-start.43) | collective-permute-done | bytes 393248 | tf_op jit(solution)/shard_map/ppermute | solution.py:23
  401.2 8.9 %collective-permute-done.44 = f32[4,3,64,128]{3,2,1,0:T(8,128)S(1)} collective-permute-done((f32[4,3,64,128]{3,2,1,0:T(8,128)S(1)}, f32[4,3,64,128]{3,2,1,0:T(8,128)S(1)}, u32[]{:S(2)}, u32[]{:S(2)}) %collective-permute-start.44) | collective-permute-done | bytes 393248 | tf_op jit(solution)/shard_map/ppermute | solution.py:25
  413.0 92.8 %while.12 = (s32[]{:T(128)}, f32[4,4,64,128]{3,2,1,0:T(8,128)S(1)}, f32[2,10,64,128]{3,2,1,0:T(8,128)S(1)}, f32[4,4,64,128]{3,2,1,0:T(8,128)S(1)}, s32[]{:T(128)}) while((s32[]{:T(128)}, f32[4,4,64,128]{3,2,1,0:T(8,128)S(1)}, f32[2,10,64,128]{3,2,1,0:T(8,128)S(1)}, f32[4,4,64,128]{3,2,1,0:T(8,128)S(1)}, s32[]{:T(128)}) %tuple.143), condition=%wide.region_1.2_spmd, body=%wide.region_0.1_spmd.sunk | while | flops 9306114 | bytes 32244132 | solution.py:119
  (297 shorter events, 283.2 us)
Async XLA Ops:
  4.5 17.0 %collective-permute-start.12 = (f32[2,3,64,128]{3,2,1,0:T(8,128)S(1)}, f32[2,3,64,128]{3,2,1,0:T(8,128)S(1)}, u32[]{:S(2)}, u32[]{:S(2)}) collective-permute-start(f32[2,3,64,128]{3,2,1,0:T(8,128)S(1)} %get-tuple-element.214), channel_id=1, source_target_pairs={{0,1},{1,2},{2,3},{3,4},{4,5},{5,6},{6,7},{7,8},{8,9},{9,10},{10,1... | collective-permute-start | bytes 589832 | tf_op jit(solution)/shard_map/ppermute | solution.py:23
  13.8 13.6 %collective-permute-start.10 = (f32[4,3,64,128]{3,2,1,0:T(8,128)S(1)}, f32[4,3,64,128]{3,2,1,0:T(8,128)S(1)}, u32[]{:S(2)}, u32[]{:S(2)}) collective-permute-start(f32[4,3,64,128]{3,2,1,0:T(8,128)S(1)} %get-tuple-element.212), channel_id=1, source_target_pairs={{0,1},{1,2},{2,3},{3,4},{4,5},{5,6},{6,7},{7,8},{8,9},{9,10},{10,1... | collective-permute-start | bytes 1179656 | tf_op jit(solution)/shard_map/ppermute | solution.py:23
  15.7 19.0 %collective-permute-start.11 = (f32[4,3,64,128]{3,2,1,0:T(8,128)S(1)}, f32[4,3,64,128]{3,2,1,0:T(8,128)S(1)}, u32[]{:S(2)}, u32[]{:S(2)}) collective-permute-start(f32[4,3,64,128]{3,2,1,0:T(8,128)S(1)} %get-tuple-element.213), channel_id=1, source_target_pairs={{1,0},{2,1},{3,2},{4,3},{5,4},{6,5},{7,6},{8,7},{9,8},{10,9},{11,1... | collective-permute-start | bytes 1179656 | tf_op jit(solution)/shard_map/ppermute | solution.py:25
  41.0 19.0 %collective-permute-start.15 = (f32[4,3,64,128]{3,2,1,0:T(8,128)S(1)}, f32[4,3,64,128]{3,2,1,0:T(8,128)S(1)}, u32[]{:S(2)}, u32[]{:S(2)}) collective-permute-start(f32[4,3,64,128]{3,2,1,0:T(8,128)S(1)} %get-tuple-element.211), channel_id=1, source_target_pairs={{1,0},{2,1},{3,2},{4,3},{5,4},{6,5},{7,6},{8,7},{9,8},{10,9},{11,1... | collective-permute-start | bytes 1179656 | tf_op jit(solution)/shard_map/ppermute | solution.py:25
  62.9 14.0 %collective-permute-start.16 = (f32[4,3,64,128]{3,2,1,0:T(8,128)S(1)}, f32[4,3,64,128]{3,2,1,0:T(8,128)S(1)}, u32[]{:S(2)}, u32[]{:S(2)}) collective-permute-start(f32[4,3,64,128]{3,2,1,0:T(8,128)S(1)} %get-tuple-element.208), channel_id=1, source_target_pairs={{0,1},{1,2},{2,3},{3,4},{4,5},{5,6},{6,7},{7,8},{8,9},{9,10},{10,1... | collective-permute-start | bytes 1179656 | tf_op jit(solution)/shard_map/ppermute | solution.py:23
  65.1 18.4 %collective-permute-start.17 = (f32[4,3,64,128]{3,2,1,0:T(8,128)S(1)}, f32[4,3,64,128]{3,2,1,0:T(8,128)S(1)}, u32[]{:S(2)}, u32[]{:S(2)}) collective-permute-start(f32[4,3,64,128]{3,2,1,0:T(8,128)S(1)} %get-tuple-element.209), channel_id=1, source_target_pairs={{1,0},{2,1},{3,2},{4,3},{5,4},{6,5},{7,6},{8,7},{9,8},{10,9},{11,1... | collective-permute-start | bytes 1179656 | tf_op jit(solution)/shard_map/ppermute | solution.py:25
  86.5 14.0 %collective-permute-start.18 = (f32[4,3,64,128]{3,2,1,0:T(8,128)S(1)}, f32[4,3,64,128]{3,2,1,0:T(8,128)S(1)}, u32[]{:S(2)}, u32[]{:S(2)}) collective-permute-start(f32[4,3,64,128]{3,2,1,0:T(8,128)S(1)} %get-tuple-element.206), channel_id=1, source_target_pairs={{0,1},{1,2},{2,3},{3,4},{4,5},{5,6},{6,7},{7,8},{8,9},{9,10},{10,1... | collective-permute-start | bytes 1179656 | tf_op jit(solution)/shard_map/ppermute | solution.py:23
  88.7 20.8 %collective-permute-start.19 = (f32[4,3,64,128]{3,2,1,0:T(8,128)S(1)}, f32[4,3,64,128]{3,2,1,0:T(8,128)S(1)}, u32[]{:S(2)}, u32[]{:S(2)}) collective-permute-start(f32[4,3,64,128]{3,2,1,0:T(8,128)S(1)} %get-tuple-element.207), channel_id=1, source_target_pairs={{1,0},{2,1},{3,2},{4,3},{5,4},{6,5},{7,6},{8,7},{9,8},{10,9},{11,1... | collective-permute-start | bytes 1179656 | tf_op jit(solution)/shard_map/ppermute | solution.py:25
  112.4 14.0 %collective-permute-start.20 = (f32[4,3,64,128]{3,2,1,0:T(8,128)S(1)}, f32[4,3,64,128]{3,2,1,0:T(8,128)S(1)}, u32[]{:S(2)}, u32[]{:S(2)}) collective-permute-start(f32[4,3,64,128]{3,2,1,0:T(8,128)S(1)} %get-tuple-element.204), channel_id=1, source_target_pairs={{0,1},{1,2},{2,3},{3,4},{4,5},{5,6},{6,7},{7,8},{8,9},{9,10},{10,1... | collective-permute-start | bytes 1179656 | tf_op jit(solution)/shard_map/ppermute | solution.py:23
  114.6 18.4 %collective-permute-start.21 = (f32[4,3,64,128]{3,2,1,0:T(8,128)S(1)}, f32[4,3,64,128]{3,2,1,0:T(8,128)S(1)}, u32[]{:S(2)}, u32[]{:S(2)}) collective-permute-start(f32[4,3,64,128]{3,2,1,0:T(8,128)S(1)} %get-tuple-element.205), channel_id=1, source_target_pairs={{1,0},{2,1},{3,2},{4,3},{5,4},{6,5},{7,6},{8,7},{9,8},{10,9},{11,1... | collective-permute-start | bytes 1179656 | tf_op jit(solution)/shard_map/ppermute | solution.py:25
  136.0 14.0 %collective-permute-start.22 = (f32[4,3,64,128]{3,2,1,0:T(8,128)S(1)}, f32[4,3,64,128]{3,2,1,0:T(8,128)S(1)}, u32[]{:S(2)}, u32[]{:S(2)}) collective-permute-start(f32[4,3,64,128]{3,2,1,0:T(8,128)S(1)} %get-tuple-element.202), channel_id=1, source_target_pairs={{0,1},{1,2},{2,3},{3,4},{4,5},{5,6},{6,7},{7,8},{8,9},{9,10},{10,1... | collective-permute-start | bytes 1179656 | tf_op jit(solution)/shard_map/ppermute | solution.py:23
  138.2 20.8 %collective-permute-start.23 = (f32[4,3,64,128]{3,2,1,0:T(8,128)S(1)}, f32[4,3,64,128]{3,2,1,0:T(8,128)S(1)}, u32[]{:S(2)}, u32[]{:S(2)}) collective-permute-start(f32[4,3,64,128]{3,2,1,0:T(8,128)S(1)} %get-tuple-element.203), channel_id=1, source_target_pairs={{1,0},{2,1},{3,2},{4,3},{5,4},{6,5},{7,6},{8,7},{9,8},{10,9},{11,1... | collective-permute-start | bytes 1179656 | tf_op jit(solution)/shard_map/ppermute | solution.py:25
  161.9 14.0 %collective-permute-start.24 = (f32[4,3,64,128]{3,2,1,0:T(8,128)S(1)}, f32[4,3,64,128]{3,2,1,0:T(8,128)S(1)}, u32[]{:S(2)}, u32[]{:S(2)}) collective-permute-start(f32[4,3,64,128]{3,2,1,0:T(8,128)S(1)} %get-tuple-element.200), channel_id=1, source_target_pairs={{0,1},{1,2},{2,3},{3,4},{4,5},{5,6},{6,7},{7,8},{8,9},{9,10},{10,1... | collective-permute-start | bytes 1179656 | tf_op jit(solution)/shard_map/ppermute | solution.py:23
  164.1 18.4 %collective-permute-start.25 = (f32[4,3,64,128]{3,2,1,0:T(8,128)S(1)}, f32[4,3,64,128]{3,2,1,0:T(8,128)S(1)}, u32[]{:S(2)}, u32[]{:S(2)}) collective-permute-start(f32[4,3,64,128]{3,2,1,0:T(8,128)S(1)} %get-tuple-element.201), channel_id=1, source_target_pairs={{1,0},{2,1},{3,2},{4,3},{5,4},{6,5},{7,6},{8,7},{9,8},{10,9},{11,1... | collective-permute-start | bytes 1179656 | tf_op jit(solution)/shard_map/ppermute | solution.py:25
  185.5 14.0 %collective-permute-start.26 = (f32[4,3,64,128]{3,2,1,0:T(8,128)S(1)}, f32[4,3,64,128]{3,2,1,0:T(8,128)S(1)}, u32[]{:S(2)}, u32[]{:S(2)}) collective-permute-start(f32[4,3,64,128]{3,2,1,0:T(8,128)S(1)} %get-tuple-element.198), channel_id=1, source_target_pairs={{0,1},{1,2},{2,3},{3,4},{4,5},{5,6},{6,7},{7,8},{8,9},{9,10},{10,1... | collective-permute-start | bytes 1179656 | tf_op jit(solution)/shard_map/ppermute | solution.py:23
  187.7 20.8 %collective-permute-start.27 = (f32[4,3,64,128]{3,2,1,0:T(8,128)S(1)}, f32[4,3,64,128]{3,2,1,0:T(8,128)S(1)}, u32[]{:S(2)}, u32[]{:S(2)}) collective-permute-start(f32[4,3,64,128]{3,2,1,0:T(8,128)S(1)} %get-tuple-element.199), channel_id=1, source_target_pairs={{1,0},{2,1},{3,2},{4,3},{5,4},{6,5},{7,6},{8,7},{9,8},{10,9},{11,1... | collective-permute-start | bytes 1179656 | tf_op jit(solution)/shard_map/ppermute | solution.py:25
  213.7 15.2 %collective-permute-start.29 = (f32[4,3,64,128]{3,2,1,0:T(8,128)S(1)}, f32[4,3,64,128]{3,2,1,0:T(8,128)S(1)}, u32[]{:S(2)}, u32[]{:S(2)}) collective-permute-start(f32[4,3,64,128]{3,2,1,0:T(8,128)S(1)} %get-tuple-element.196), channel_id=1, source_target_pairs={{0,1},{1,2},{2,3},{3,4},{4,5},{5,6},{6,7},{7,8},{8,9},{9,10},{10,1... | collective-permute-start | bytes 1179656 | tf_op jit(solution)/shard_map/ppermute | solution.py:23
  216.1 19.3 %collective-permute-start.30 = (f32[4,3,64,128]{3,2,1,0:T(8,128)S(1)}, f32[4,3,64,128]{3,2,1,0:T(8,128)S(1)}, u32[]{:S(2)}, u32[]{:S(2)}) collective-permute-start(f32[4,3,64,128]{3,2,1,0:T(8,128)S(1)} %get-tuple-element.197), channel_id=1, source_target_pairs={{1,0},{2,1},{3,2},{4,3},{5,4},{6,5},{7,6},{8,7},{9,8},{10,9},{11,1... | collective-permute-start | bytes 1179656 | tf_op jit(solution)/shard_map/ppermute | solution.py:25
  238.3 14.4 %collective-permute-start.31 = (f32[4,3,64,128]{3,2,1,0:T(8,128)S(1)}, f32[4,3,64,128]{3,2,1,0:T(8,128)S(1)}, u32[]{:S(2)}, u32[]{:S(2)}) collective-permute-start(f32[4,3,64,128]{3,2,1,0:T(8,128)S(1)} %get-tuple-element.194), channel_id=1, source_target_pairs={{0,1},{1,2},{2,3},{3,4},{4,5},{5,6},{6,7},{7,8},{8,9},{9,10},{10,1... | collective-permute-start | bytes 1179656 | tf_op jit(solution)/shard_map/ppermute | solution.py:23
  240.5 21.1 %collective-permute-start.32 = (f32[4,3,64,128]{3,2,1,0:T(8,128)S(1)}, f32[4,3,64,128]{3,2,1,0:T(8,128)S(1)}, u32[]{:S(2)}, u32[]{:S(2)}) collective-permute-start(f32[4,3,64,128]{3,2,1,0:T(8,128)S(1)} %get-tuple-element.195), channel_id=1, source_target_pairs={{1,0},{2,1},{3,2},{4,3},{5,4},{6,5},{7,6},{8,7},{9,8},{10,9},{11,1... | collective-permute-start | bytes 1179656 | tf_op jit(solution)/shard_map/ppermute | solution.py:25
  264.4 14.0 %collective-permute-start.33 = (f32[4,3,64,128]{3,2,1,0:T(8,128)S(1)}, f32[4,3,64,128]{3,2,1,0:T(8,128)S(1)}, u32[]{:S(2)}, u32[]{:S(2)}) collective-permute-start(f32[4,3,64,128]{3,2,1,0:T(8,128)S(1)} %get-tuple-element.192), channel_id=1, source_target_pairs={{0,1},{1,2},{2,3},{3,4},{4,5},{5,6},{6,7},{7,8},{8,9},{9,10},{10,1... | collective-permute-start | bytes 1179656 | tf_op jit(solution)/shard_map/ppermute | solution.py:23
  266.7 18.6 %collective-permute-start.34 = (f32[4,3,64,128]{3,2,1,0:T(8,128)S(1)}, f32[4,3,64,128]{3,2,1,0:T(8,128)S(1)}, u32[]{:S(2)}, u32[]{:S(2)}) collective-permute-start(f32[4,3,64,128]{3,2,1,0:T(8,128)S(1)} %get-tuple-element.193), channel_id=1, source_target_pairs={{1,0},{2,1},{3,2},{4,3},{5,4},{6,5},{7,6},{8,7},{9,8},{10,9},{11,1... | collective-permute-start | bytes 1179656 | tf_op jit(solution)/shard_map/ppermute | solution.py:25
  288.1 14.0 %collective-permute-start.35 = (f32[4,3,64,128]{3,2,1,0:T(8,128)S(1)}, f32[4,3,64,128]{3,2,1,0:T(8,128)S(1)}, u32[]{:S(2)}, u32[]{:S(2)}) collective-permute-start(f32[4,3,64,128]{3,2,1,0:T(8,128)S(1)} %get-tuple-element.190), channel_id=1, source_target_pairs={{0,1},{1,2},{2,3},{3,4},{4,5},{5,6},{6,7},{7,8},{8,9},{9,10},{10,1... | collective-permute-start | bytes 1179656 | tf_op jit(solution)/shard_map/ppermute | solution.py:23
  290.4 20.7 %collective-permute-start.36 = (f32[4,3,64,128]{3,2,1,0:T(8,128)S(1)}, f32[4,3,64,128]{3,2,1,0:T(8,128)S(1)}, u32[]{:S(2)}, u32[]{:S(2)}) collective-permute-start(f32[4,3,64,128]{3,2,1,0:T(8,128)S(1)} %get-tuple-element.191), channel_id=1, source_target_pairs={{1,0},{2,1},{3,2},{4,3},{5,4},{6,5},{7,6},{8,7},{9,8},{10,9},{11,1... | collective-permute-start | bytes 1179656 | tf_op jit(solution)/shard_map/ppermute | solution.py:25
  314.0 14.0 %collective-permute-start.37 = (f32[4,3,64,128]{3,2,1,0:T(8,128)S(1)}, f32[4,3,64,128]{3,2,1,0:T(8,128)S(1)}, u32[]{:S(2)}, u32[]{:S(2)}) collective-permute-start(f32[4,3,64,128]{3,2,1,0:T(8,128)S(1)} %get-tuple-element.188), channel_id=1, source_target_pairs={{0,1},{1,2},{2,3},{3,4},{4,5},{5,6},{6,7},{7,8},{8,9},{9,10},{10,1... | collective-permute-start | bytes 1179656 | tf_op jit(solution)/shard_map/ppermute | solution.py:23
  316.2 18.5 %collective-permute-start.38 = (f32[4,3,64,128]{3,2,1,0:T(8,128)S(1)}, f32[4,3,64,128]{3,2,1,0:T(8,128)S(1)}, u32[]{:S(2)}, u32[]{:S(2)}) collective-permute-start(f32[4,3,64,128]{3,2,1,0:T(8,128)S(1)} %get-tuple-element.189), channel_id=1, source_target_pairs={{1,0},{2,1},{3,2},{4,3},{5,4},{6,5},{7,6},{8,7},{9,8},{10,9},{11,1... | collective-permute-start | bytes 1179656 | tf_op jit(solution)/shard_map/ppermute | solution.py:25
  337.7 14.0 %collective-permute-start.39 = (f32[4,3,64,128]{3,2,1,0:T(8,128)S(1)}, f32[4,3,64,128]{3,2,1,0:T(8,128)S(1)}, u32[]{:S(2)}, u32[]{:S(2)}) collective-permute-start(f32[4,3,64,128]{3,2,1,0:T(8,128)S(1)} %get-tuple-element.186), channel_id=1, source_target_pairs={{0,1},{1,2},{2,3},{3,4},{4,5},{5,6},{6,7},{7,8},{8,9},{9,10},{10,1... | collective-permute-start | bytes 1179656 | tf_op jit(solution)/shard_map/ppermute | solution.py:23
  339.9 20.7 %collective-permute-start.40 = (f32[4,3,64,128]{3,2,1,0:T(8,128)S(1)}, f32[4,3,64,128]{3,2,1,0:T(8,128)S(1)}, u32[]{:S(2)}, u32[]{:S(2)}) collective-permute-start(f32[4,3,64,128]{3,2,1,0:T(8,128)S(1)} %get-tuple-element.187), channel_id=1, source_target_pairs={{1,0},{2,1},{3,2},{4,3},{5,4},{6,5},{7,6},{8,7},{9,8},{10,9},{11,1... | collective-permute-start | bytes 1179656 | tf_op jit(solution)/shard_map/ppermute | solution.py:25
  363.5 14.0 %collective-permute-start.41 = (f32[4,3,64,128]{3,2,1,0:T(8,128)S(1)}, f32[4,3,64,128]{3,2,1,0:T(8,128)S(1)}, u32[]{:S(2)}, u32[]{:S(2)}) collective-permute-start(f32[4,3,64,128]{3,2,1,0:T(8,128)S(1)} %get-tuple-element.184), channel_id=1, source_target_pairs={{0,1},{1,2},{2,3},{3,4},{4,5},{5,6},{6,7},{7,8},{8,9},{9,10},{10,1... | collective-permute-start | bytes 1179656 | tf_op jit(solution)/shard_map/ppermute | solution.py:23
  365.7 18.5 %collective-permute-start.42 = (f32[4,3,64,128]{3,2,1,0:T(8,128)S(1)}, f32[4,3,64,128]{3,2,1,0:T(8,128)S(1)}, u32[]{:S(2)}, u32[]{:S(2)}) collective-permute-start(f32[4,3,64,128]{3,2,1,0:T(8,128)S(1)} %get-tuple-element.185), channel_id=1, source_target_pairs={{1,0},{2,1},{3,2},{4,3},{5,4},{6,5},{7,6},{8,7},{9,8},{10,9},{11,1... | collective-permute-start | bytes 1179656 | tf_op jit(solution)/shard_map/ppermute | solution.py:25
  387.2 14.0 %collective-permute-start.43 = (f32[4,3,64,128]{3,2,1,0:T(8,128)S(1)}, f32[4,3,64,128]{3,2,1,0:T(8,128)S(1)}, u32[]{:S(2)}, u32[]{:S(2)}) collective-permute-start(f32[4,3,64,128]{3,2,1,0:T(8,128)S(1)} %get-tuple-element.182), channel_id=1, source_target_pairs={{0,1},{1,2},{2,3},{3,4},{4,5},{5,6},{6,7},{7,8},{8,9},{9,10},{10,1... | collective-permute-start | bytes 1179656 | tf_op jit(solution)/shard_map/ppermute | solution.py:23
  389.4 20.7 %collective-permute-start.44 = (f32[4,3,64,128]{3,2,1,0:T(8,128)S(1)}, f32[4,3,64,128]{3,2,1,0:T(8,128)S(1)}, u32[]{:S(2)}, u32[]{:S(2)}) collective-permute-start(f32[4,3,64,128]{3,2,1,0:T(8,128)S(1)} %get-tuple-element.183), channel_id=1, source_target_pairs={{1,0},{2,1},{3,2},{4,3},{5,4},{6,5},{7,6},{8,7},{9,8},{10,9},{11,1... | collective-permute-start | bytes 1179656 | tf_op jit(solution)/shard_map/ppermute | solution.py:25
  (59 other events, 264.3 us)
where the time goes:
time: 517 us; the launch traced here: 507 us
  waiting for transfers between devices  266 us (51%)
  starting transfers between devices  183 us (35%)
  other arithmetic  40.2 us (8%)
  local copies, waits for them, and re-layouts  15.3 us (3%)
    ppermute x25, waiting for transfers between devices, extended_2(): lax.ppermute(head, axis, [((i + 1) % count, i) for i in range(ends)])  134 us
    ppermute x25, waiting for transfers between devices, extended_2(): lax.ppermute(tail, axis, [(i, (i + 1) % count) for i in range(ends)])  129 us
    ppermute x25, starting transfers between devices, extended_2(): lax.ppermute(head, axis, [((i + 1) % count, i) for i in range(ends)])  107 us
    ppermute x25, starting transfers between devices, extended_2(): lax.ppermute(tail, axis, [(i, (i + 1) % count) for i in range(ends)])  70.9 us
    div x24, other arithmetic, advance_deep(): update = remain / middle  14.6 us
    add x24, other arithmetic, advance_deep(): ratio_next * ratio_now * update[:, 1:-1]  12 us
  transfers between devices with their start and end apart: 54, of which 51 were waited for; matrix products, arithmetic and copies ran while one was open for 1% of the time, Pallas kernels for 0%

commit v1 on v0

v1 whole, which is shorter than its diff:
```python
from functools import partial

import jax
import jax.numpy as jnp
import numpy as np
from jax import lax
from jax.experimental import pallas as pl
from jax.experimental.pallas import tpu as pltpu
from jax.sharding import PartitionSpec as P

COARSEN = 8
SWEEPS = 3
KAPPA_TOP = 3.0
SUB = 8
PLANES = 16
VMEM = pltpu.CompilerParams(vmem_limit_bytes=48 * 2**20)


def polynomials(scale, top):
    middle = (top + 1.0) / 2.0
    spread = (top - 1.0) / 2.0
    relative = middle / spread

    def run(start, source):
        def apply(poly):
            return scale * np.concatenate([[0.0], poly])[: SWEEPS + 1]

        ratio_now = 1.0 / relative
        remain = source - apply(start)
        update = remain / middle
        iterate = start + update
        for _ in range(SWEEPS - 1):
            remain = remain - (update + apply(update))
            ratio_next = 1.0 / (2.0 * relative - ratio_now)
            update = ratio_next * ratio_now * update + (2.0 * ratio_next / spread) * remain
            iterate = iterate + update
            ratio_now = ratio_next
        return iterate

    one = np.zeros(SWEEPS + 1)
    one[0] = 1.0
    return run(one, 0.0 * one), run(0.0 * one, one)


def linear_factors(poly):
    roots = np.roots(poly[::-1] / poly[-1])
    assert np.all(np.abs(roots.imag) < 1e-9)
    return sorted((float(1.0 / r) for r in roots.real), reverse=True)


FINE_P, FINE_Q = polynomials(1.0, 1.0 + 12.0 * KAPPA_TOP)
COARSE_P, _ = polynomials(float(COARSEN), 1.0 + 12.0 * KAPPA_TOP * COARSEN)
FINE = linear_factors(FINE_P)
COARSE = linear_factors(COARSE_P)


def rows(ref, z, j, J):
    return ref[z, pl.ds(j, SUB, stride=J), :]


def put_rows(ref, z, j, J, value):
    ref[z, pl.ds(j, SUB, stride=J), :] = value


def copy_planes(n, dst, src, d0=0, s0=0):
    J = dst.shape[1]

    def one(z, c):
        for j in range(J):
            dst[d0 + z, j] = src[s0 + z, j]
        return c

    lax.fori_loop(0, n, one, 0, unroll=4 if n % 4 == 0 else 3 if n % 3 == 0 else 1)


def masks(width):
    lane = lax.broadcasted_iota(jnp.int32, (SUB, width), 1)
    sub = lax.broadcasted_iota(jnp.int32, (SUB, width), 0)
    return lane == 0, lane == width - 1, sub == 0, sub == SUB - 1


def sweep(lo, hi, read, emit, J, width):
    first, last, top, bottom = masks(width)
    n = hi - lo
    steps = -(-n // PLANES)
    size = -(-n // steps)

    def chunk(i, c):
        z0 = jnp.minimum(lo + i * size, hi - size)
        for u in range(size):
            z = z0 + u
            w = [read(z, j) for j in range(J)]
            after = jnp.where(bottom, 0.0, pltpu.roll(w[0], SUB - 1, 0))
            before = jnp.where(top, 0.0, pltpu.roll(w[J - 1], 1, 0))
            for j in range(J):
                yp = w[j + 1] if j < J - 1 else after
                ym = w[j - 1] if j > 0 else before
                xm = jnp.where(first, 0.0, pltpu.roll(w[j], 1, 1))
                xp = jnp.where(last, 0.0, pltpu.roll(w[j], width - 1, 1))
                beside = (read(z - 1, j) + read(z + 1, j)) + (yp + ym) + (xm + xp)
                emit(z, j, w[j], beside)
        return c

    lax.fori_loop(0, steps, chunk, 0)


def factor(dst, src, cond, coef, lo, hi, s0=0, k0=0, extra=None):
    J, width = dst.shape[1], dst.shape[3]

    def emit(z, j, w, beside):
        out = w + (coef * cond[z + k0, j]) * (beside - 6.0 * w)
        if extra is not None:
            out = out + extra(z, j)
        dst[z, j] = out

    sweep(lo, hi, lambda z, j: src[z + s0, j], emit, J, width)


def fine_steps(a, b, cond, k0, total, levels, amounts=None, first_step=0, source=None):
    src, dst = a, b
    for level in range(levels):
        extra = None
        if source is not None and level % SWEEPS == SWEEPS - 1:
            amount = amounts[first_step + level // SWEEPS]
            extra = lambda z, j, amount=amount: amount * source[z + k0, j]
        factor(dst, src, cond, FINE[level % SWEEPS], level + 1, total - level - 1, k0=k0, extra=extra)
        src, dst = dst, src
    return src


def place_kernel(where, own, r1, r2, r3, field, coef, field_up, field_dn, *, each, halo, wide):
    q = where[0]
    J = field.shape[1]
    for j, ref in enumerate((own, r1, r2, r3)):
        base = lax.bitwise_xor(q, j) * each
        for z in range(each):
            for row in range(J):
                field[base + z, row] = rows(ref, z, row, J)
                coef[base + z, row] = rows(ref, each + z, row, J)
    slab = field.shape[0]
    copy_planes(halo, field_up, field, 0, slab - halo)
    copy_planes(wide, field_up, coef, halo, slab - wide)
    copy_planes(halo, field_dn, field, 0, 0)
    copy_planes(wide, field_dn, coef, halo, 0)


def first_kernel(
    where, amounts, field, mine, other, got_lo, got_hi, other_lo, other_hi,
    out, up, dn, cond, force, a, b, raw, *, halo, wide,
):
    core = where[1]
    J, width = a.shape[1], a.shape[3]
    slab = field.shape[0]
    total = slab + 2 * halo
    span = slab + 2 * wide
    copy_planes(halo, a, got_lo, 0, 0)
    copy_planes(slab, a, field, halo, 0)
    copy_planes(halo, a, got_hi, halo + slab, 0)

    def fill(slot, lo, mid, hi, off):
        def one(n, src, d0, s0):
            def body(z, c):
                for j in range(J):
                    raw[slot, d0 + z, j] = src[s0 + z, j]
                return c

            lax.fori_loop(0, n, body, 0)

        one(wide, lo, 0, off)
        one(slab, mid, wide, 0)
        one(wide, hi, wide + slab, off)

    fill(core, got_lo, mine, got_hi, halo)
    fill(1 - core, other_lo, other, other_hi, 0)
    copy_planes(span, cond, raw.at[0])

    def inner(z, j, w, beside):
        raw[0, z, j] = FINE_Q[1] * w + FINE_Q[2] * cond[z, j] * (6.0 * w - beside)

    def outer(z, j, w, beside):
        force[z, j] = FINE_Q[0] * raw[1, z, j] + cond[z, j] * (6.0 * w - beside)

    margin = wide - (halo - SWEEPS)
    sweep(margin - 1, span - margin + 1, lambda z, j: raw[1, z, j], inner, J, width)
    sweep(margin, span - margin, lambda z, j: raw[0, z, j], outer, J, width)

    state = fine_steps(a, b, cond, wide - halo, total, halo, amounts, 0, force)
    copy_planes(slab, out, state, 0, halo)
    copy_planes(halo, up, state, 0, halo + slab - halo)
    copy_planes(halo, dn, state, 0, halo)


def load_state(a, lo, mid, hi):
    halo, slab = lo.shape[0], mid.shape[0]
    copy_planes(halo, a, lo, 0, 0)
    copy_planes(slab, a, mid, halo, 0)
    copy_planes(halo, a, hi, halo + slab, 0)


def second_kernel(
    where, amounts, field, lo, hi, cond, force, n0, n1, n2, n3,
    p0, p1, p2, p3, out, up, dn, a, b, *, wide, each, step,
):
    q = where[0]
    halo, slab, J = lo.shape[0], field.shape[0], a.shape[1]
    load_state(a, lo, field, hi)
    state = fine_steps(a, b, cond, wide - halo, slab + 2 * halo, halo, amounts, step, force)
    for i, (piece, after) in enumerate(((p0, n0), (p1, n1), (p2, n2), (p3, n3))):
        base = lax.bitwise_xor(q, i) * each
        for z in range(each):
            for j in range(J):
                value = state[halo + base + z, j]
                put_rows(piece, z, j, J, value)
                out[base + z, j] = value - rows(after, z, j, J)
    copy_planes(halo, up, out, 0, slab - halo)
    copy_planes(halo, dn, out, 0, 0)


def third_kernel(field, lo, hi, cond, out, up, dn, a, b, *, wide):
    halo, slab = lo.shape[0], field.shape[0]
    load_state(a, lo, field, hi)
    state = fine_steps(a, b, cond, wide - halo, slab + 2 * halo, halo)
    copy_planes(slab, out, state, 0, halo)
    copy_planes(up.shape[0], up, state, 0, halo + slab - up.shape[0])
    copy_planes(dn.shape[0], dn, state, 0, halo)


def fourth_kernel(where, field, lo, hi, cond, out, p0, p1, p2, p3, a, b, *, levels, each):
    q = where[0]
    halo, slab, J = lo.shape[0], field.shape[0], a.shape[1]
    load_state(a, lo, field, hi)
    state = fine_steps(a, b, cond, 0, slab + 2 * halo, levels)
    copy_planes(out.shape[0], out, state, 0, levels)
    for i, piece in enumerate((p0, p1, p2, p3)):
        base = lax.bitwise_xor(q, i) * each
        for z in range(each):
            for j in range(J):
                put_rows(piece, z, j, J, state[halo + base + z, j])


def pair_kernel(where, mine, other, cond, out, both, a, b, *, wide):
    core = where[1]
    J = a.shape[1]
    total = mine.shape[0]
    slab = out.shape[0]

    def body(z, c):
        for j in range(J):
            both[core, z, j] = mine[z, j]
            both[1 - core, z, j] = other[z, j]
        return c

    lax.fori_loop(0, total, body, 0)
    k0 = wide - SWEEPS
    factor(a, both.at[0], cond, COARSE[0], 1, total - 1, k0=k0)
    factor(b, a, cond, COARSE[1], 2, total - 2, k0=k0)
    factor(a, b, cond, COARSE[2], 3, total - 3, k0=k0, extra=lambda z, j: both[1, z, j])
    copy_planes(slab, out, a, 0, SWEEPS)


def chain_kernel(where, sums, got_lo, got_hi, cond, *refs, wide, each, reach):
    pieces, refs = refs[:16], refs[16:]
    corrected, residual, ends, a, b, c, d, relaxed, remain, error = refs
    q, core = where[0], where[1]
    J = a.shape[1]
    count = len(reach) + 1
    slab = sums.shape[0] // count
    mine_rel, other_rel, mine_res, other_res = (pieces[4 * i : 4 * i + 4] for i in range(4))
    for i in range(4):
        place = lax.bitwise_xor(q, i)
        for z in range(each):
            for j in range(J):
                relaxed[2 * place + core, z, j] = rows(mine_rel[i], z, j, J)
                relaxed[2 * place + 1 - core, z, j] = rows(other_rel[i], z, j, J)
                remain[2 * place + 1 + core, z, j] = rows(mine_res[i], z, j, J)
                remain[2 * place + 2 - core, z, j] = rows(other_res[i], z, j, J)
    zero = jnp.zeros(a.shape[2:], jnp.float32)
    for z in range(each):
        for j in range(J):
            remain[0, z, j] = zero
            error[0, z, j] = zero
    offset = 0
    for i, h in enumerate(reach):
        copy_planes(h, ends.at[i], got_lo, 0, offset)
        copy_planes(slab, ends.at[i], sums, h, i * slab)
        copy_planes(h, ends.at[i], got_hi, h + slab, offset)
        offset += h
    top = reach[0]
    window = each + 2 * top
    base = each * q

    def keep(k, ref, s0):
        for z in range(each):
            for j in range(J):
                error[k, z, j] = ref[top + z + s0, j]

    keep(2, ends.at[0], base)
    for z in range(each):
        for j in range(J):
            error[1, z, j] = remain[1, z, j]
    src, s0, lo, hi = ends.at[0], base, 0, window
    for i in range(len(reach)):
        k = 2 * i + 3
        inner = dict(k0=base)
        m0, m1 = top, top + each
        factor(c, src, cond, COARSE[0], m0 - 2, m1 + 2, s0=s0, **inner)
        factor(d, c, cond, COARSE[1], m0 - 1, m1 + 1, **inner)
        factor(c, d, cond, COARSE[2], m0, m1, extra=lambda z, j, k=k: remain[k, z - top, j], **inner)
        keep(k, c, 0)
        if i + 1 < len(reach):
            nxt = ends.at[i + 1]
            shift = base - top + reach[i + 1]
            bufs = (a, b)
            for level in range(2 * SWEEPS):
                lo, hi = lo + 1, hi - 1
                dst = bufs[level % 2]
                extra = None
                if level == 2 * SWEEPS - 1:
                    extra = lambda z, j, nxt=nxt, shift=shift: nxt[z + shift, j]
                factor(dst, src, cond, COARSE[level % SWEEPS], lo, hi, s0=s0, extra=extra, **inner)
                src, s0 = dst, 0
            keep(2 * i + 4, src, 0)
    slots = corrected.shape[0]
    for i in range(slots):
        k = core * slots + i
        for z in range(each):
            for j in range(J):
                corrected[i, z, pl.ds(j, SUB, stride=J), :] = relaxed[k, z, j] + error[k, z, j]
                residual[i, z, pl.ds(j, SUB, stride=J), :] = remain[k, z, j]


def body(initial, guess, conduct, source, profile):
    slots, each, nx, ny = guess.shape
    J = nx // SUB
    cores = lax.axis_size("tm")
    count = lax.axis_size("space")
    assert cores == 2 and slots == 4 and count % slots == 0 and nx % SUB == 0
    core = lax.axis_index("tm")
    place = lax.axis_index("space")
    q = place % slots
    slab = slots * each
    halo = COARSEN * SWEEPS // 2
    wide = halo + SWEEPS
    where = jnp.stack([q, core]).astype(jnp.int32)
    f32 = jnp.float32

    def blocked(n):
        return jax.ShapeDtypeStruct((n, J, SUB, ny), f32)

    def natural(n):
        return jax.ShapeDtypeStruct((n, nx, ny), f32)

    def scratch(*lead):
        return pltpu.VMEM((*lead, J, SUB, ny), f32)

    smem = pl.BlockSpec(memory_space=pltpu.SMEM)
    vmem = pl.BlockSpec(memory_space=pltpu.VMEM)

    def call(kernel, scalars, arrays, outs, scratches, name):
        return pl.pallas_call(
            kernel,
            out_shape=outs,
            in_specs=[smem] * len(scalars) + [vmem] * len(arrays),
            out_specs=jax.tree.map(lambda _: vmem, outs),
            scratch_shapes=scratches,
            compiler_params=VMEM,
            name=name,
        )(*scalars, *arrays)

    def swap(value):
        return lax.ppermute(value, "tm", [(0, 1), (1, 0)])

    def across(value, j):
        return lax.ppermute(value, "space", [(s, s - s % slots + ((s % slots) ^ j)) for s in range(count)])

    def up(value):
        return lax.ppermute(value, "space", [(s, s + slots) for s in range(count - slots)])

    def down(value):
        return lax.ppermute(value, "space", [(s + slots, s) for s in range(count - slots)])

    first = core == 0
    theirs = swap(guess)
    low, high = jnp.where(first, guess, theirs), jnp.where(first, theirs, guess)
    guesses = jnp.concatenate([low, high], axis=0)
    amounts_other = swap(profile)
    profiles = jnp.concatenate([jnp.where(first, profile, amounts_other), jnp.where(first, amounts_other, profile)])
    task = 2 * q + core
    amounts = lax.dynamic_slice_in_dim(profiles, task * COARSEN, COARSEN)

    entries = jnp.concatenate([initial[None], guesses[:-1]], axis=0)
    coef = jnp.where(first, conduct, source)

    def entry_for(j):
        t = 2 * (q ^ j) + core
        return jnp.concatenate([lax.dynamic_index_in_dim(entries, t, 0, False), coef], axis=0)

    def after_for(j):
        t = 2 * (q ^ j) + core
        return lax.dynamic_index_in_dim(guesses, t, 0, False)

    got = [entry_for(0)] + [across(entry_for(j), j) for j in range(1, slots)]
    after = [after_for(0)] + [across(after_for(j), j) for j in range(1, slots)]

    field, mine, send_up, send_dn = call(
        partial(place_kernel, each=each, halo=halo, wide=wide),
        [where], got, [blocked(slab), blocked(slab), blocked(halo + wide), blocked(halo + wide)], [], "place",
    )
    other = swap(mine)
    got_lo, got_hi = up(send_up), down(send_dn)
    other_lo, other_hi = swap(got_lo[halo:]), swap(got_hi[halo:])
    span, total = slab + 2 * wide, slab + 2 * halo
    state, send_up, send_dn, cond, force = call(
        partial(first_kernel, halo=halo, wide=wide),
        [where, amounts], [field, mine, other, got_lo, got_hi, other_lo, other_hi],
        [blocked(slab), blocked(halo), blocked(halo), blocked(span), blocked(span)],
        [scratch(total), scratch(total), scratch(2, span)], "relax_first",
    )
    *rel, state, send_up, send_dn = call(
        partial(second_kernel, wide=wide, each=each, step=halo // SWEEPS),
        [where, amounts], [state, up(send_up), down(send_dn), cond, force, *after],
        [natural(each)] * 4 + [blocked(slab), blocked(halo), blocked(halo)],
        [scratch(total), scratch(total)], "relax_second",
    )
    rel = [rel[0]] + [across(rel[j], j) for j in range(1, slots)]
    state, send_up, send_dn = call(
        partial(third_kernel, wide=wide),
        [], [state, up(send_up), down(send_dn), cond],
        [blocked(slab), blocked(wide), blocked(wide)],
        [scratch(total), scratch(total)], "again_first",
    )
    remain, *res = call(
        partial(fourth_kernel, levels=halo, each=each),
        [where], [state, up(send_up), down(send_dn), cond],
        [blocked(slab + 2 * SWEEPS)] + [natural(each)] * 4,
        [scratch(span), scratch(span)], "again_second",
    )
    res = [res[0]] + [across(res[j], j) for j in range(1, slots)]
    rel_other = [swap(r) for r in rel]
    res_other = [swap(r) for r in res]

    pair = call(
        partial(pair_kernel, wide=wide),
        [where], [remain, swap(remain), cond],
        blocked(slab), [scratch(2, slab + 2 * SWEEPS), scratch(slab + 2 * SWEEPS), scratch(slab + 2 * SWEEPS)], "pairs",
    )
    groups = [[g * slots + i for i in range(slots)] for g in range(count // slots)]
    sums = lax.all_gather(pair, "space", axis=0, tiled=True, axis_index_groups=groups)
    reach = [2 * SWEEPS * (slots - 2 - i) + SWEEPS for i in range(slots - 1)]
    send_up = jnp.concatenate([sums[(i + 1) * slab - h : (i + 1) * slab] for i, h in enumerate(reach)], axis=0)
    send_dn = jnp.concatenate([sums[i * slab : i * slab + h] for i, h in enumerate(reach)], axis=0)
    window = each + 2 * reach[0]
    corrected, residual = call(
        partial(chain_kernel, wide=wide, each=each, reach=reach),
        [where], [sums, up(send_up), down(send_dn), cond, *rel, *rel_other, *res, *res_other],
        [jax.ShapeDtypeStruct(guess.shape, f32)] * 2,
        [scratch(len(reach), slab + 2 * reach[0])]
        + [scratch(window)] * 4
        + [scratch(2 * slots, each), scratch(2 * slots + 1, each), scratch(2 * slots, each)],
        "chain",
    )
    return corrected, residual


def solution(mesh):
    return jax.shard_map(
        body,
        mesh=mesh,
        in_specs=(
            P("space", None, None),
            P("tm", "space", None, None),
            P("space", None, None),
            P("space", None, None),
            P("tm"),
        ),
        out_specs=(P("tm", "space", None, None), P("tm", "space", None, None)),
        check_vma=False,
    )
```

time: 517 us -> 232 us (0.45)
  the two profiles are of different devices: /device:TPU:24 before, /device:TPU:0 now
where the time goes in v1:
time: 232 us; the launch traced here: 231 us
  waiting for transfers between devices  114 us (49%)
  Pallas kernels  53.4 us (23%)
  starting transfers between devices  40.8 us (18%)
  between operations  14.3 us (6%)
  local copies, waits for them, and re-layouts  5.66 us (2%)
  other arithmetic  2.89 us (1%)
    pallas_call x7, Pallas kernels, call(): pl.pallas_call(kernel, out_shape=outs, in_specs=[smem] * len(scalars) + [...  53.4 us
    all_gather x1, waiting for transfers between devices, body(): lax.all_gather(pair, 'space', axis=0, tiled=True, axis_index_groups=groups)  34.3 us
    ppermute x5, waiting for transfers between devices, up(): lax.ppermute(value, 'space', [(s, s + slots) for s in range(count - slots)])  30.9 us
    ppermute x12, waiting for transfers between devices, across(): lax.ppermute(value, 'space', [(s, s - s % slots + (s % slots ^ j)) for s...  28.3 us
    ppermute x5, starting transfers between devices, up(): lax.ppermute(value, 'space', [(s, s + slots) for s in range(count - slots)])  16.6 us
    ppermute x12, starting transfers between devices, across(): lax.ppermute(value, 'space', [(s, s - s % slots + (s % slots ^ j)) for s...  15 us
    ppermute x5, waiting for transfers between devices, down(): lax.ppermute(value, 'space', [(s + slots, s) for s in range(count - slots)])  14.1 us
    ppermute x5, starting transfers between devices, down(): lax.ppermute(value, 'space', [(s + slots, s) for s in range(count - slots)])  6.86 us
  transfers between devices with their start and end apart: 37, of which 25 were waited for; matrix products, arithmetic and copies ran while one was open for 1% of the time, Pallas kernels for 0%

profile of v1, /device:TPU:0, one launch (start us, length us, event | category | flops | bytes accessed | tf_op | source)
XLA Modules:
  0.0 231.4 jit_solution(2596489992134109027)
XLA Ops:
  11.7 3.8 %collective-permute-start.4 = (f32[8,64,128]{2,1,0:T(8,128)S(1)}, f32[8,64,128]{2,1,0:T(8,128)S(1)}, u32[]{:S(2)}, u32[]{:S(2)}) collective-permute-start(f32[8,64,128]{2,1,0:T(8,128)S(1)} %get-tuple-element.66), channel_id=1, source_target_pairs={{0,3},{1,2},{2,1},{3,0},{4,7},{5,6},{6,5},{7,4},{8,11},{9,10},{10,... | collective-permute-start | bytes 786440 | tf_op jit(solution)/shard_map/ppermute | solution.py:374
  16.1 6.5 %collective-permute-done.4.r3 = f32[8,64,128]{2,1,0:T(8,128)S(1)} collective-permute-done((f32[8,64,128]{2,1,0:T(8,128)S(1)}, f32[8,64,128]{2,1,0:T(8,128)S(1)}, u32[]{:S(2)}, u32[]{:S(2)}) %collective-permute-start.4) | collective-permute-done | bytes 262176 | tf_op jit(solution)/shard_map/ppermute | solution.py:374
  22.6 5.4 %collective-permute-done.2.r1 = f32[8,64,128]{2,1,0:T(8,128)S(1)} collective-permute-done((f32[8,64,128]{2,1,0:T(8,128)S(1)}, f32[8,64,128]{2,1,0:T(8,128)S(1)}, u32[]{:S(2)}, u32[]{:S(2)}) %collective-permute-start.2) | collective-permute-done | bytes 262176 | tf_op jit(solution)/shard_map/ppermute | solution.py:374
  28.9 3.5 %collective-permute-start.6 = (f32[27,8,8,128]{3,2,1,0:T(8,128)S(1)}, f32[27,8,8,128]{3,2,1,0:T(8,128)S(1)}, u32[]{:S(2)}, u32[]{:S(2)}) collective-permute-start(f32[27,8,8,128]{3,2,1,0:T(8,128)S(1)} %get-tuple-element.28), channel_id=1, source_target_pairs={{0,4},{1,5},{2,6},{3,7},{4,8},{5,9},{6,10},{7,11},{8,12},{9,13},{1... | collective-permute-start | bytes 2654216 | tf_op jit(solution)/shard_map/ppermute | solution.py:377
  33.8 17.5 %collective-permute-done.6.got_lo = f32[27,8,8,128]{3,2,1,0:T(8,128)S(1)} collective-permute-done((f32[27,8,8,128]{3,2,1,0:T(8,128)S(1)}, f32[27,8,8,128]{3,2,1,0:T(8,128)S(1)}, u32[]{:S(2)}, u32[]{:S(2)}) %collective-permute-start.6) | collective-permute-done | bytes 884768 | tf_op jit(solution)/shard_map/ppermute | solution.py:377
  52.2 3.3 %collective-permute-done.7.got_hi = f32[27,8,8,128]{3,2,1,0:T(8,128)S(1)} collective-permute-done((f32[27,8,8,128]{3,2,1,0:T(8,128)S(1)}, f32[27,8,8,128]{3,2,1,0:T(8,128)S(1)}, u32[]{:S(2)}, u32[]{:S(2)}) %collective-permute-start.7) | collective-permute-done | bytes 884768 | tf_op jit(solution)/shard_map/ppermute | solution.py:380
  58.5 13.0 %relax_first.1 = (f32[16,8,8,128]{3,2,1,0:T(8,128)S(1)}, f32[12,8,8,128]{3,2,1,0:T(8,128)S(1)}, f32[12,8,8,128]{3,2,1,0:T(8,128)S(1)}, f32[46,8,8,128]{3,2,1,0:T(8,128)}, f32[46,8,8,128]{3,2,1,0:T(8,128)}) custom-call(s32[2]{0:T(128)S(1)} %pad_add_fusion.where, f32[8]{0:T(128)S(1)} %dynamic_slice.28.amounts, f32[16,8,8,128]{3,2,1,0:T(8,128)S(1)} %get-tuple-element.26.field, ...), custom_call_target="tpu_custom_call" | custom-call | tf_op jit(solution)/shard_map/relax_first/pallas_call | solution.py:360
  71.5 3.6 %collective-permute-start.10 = (f32[12,8,8,128]{3,2,1,0:T(8,128)S(1)}, f32[12,8,8,128]{3,2,1,0:T(8,128)S(1)}, u32[]{:S(2)}, u32[]{:S(2)}) collective-permute-start(f32[12,8,8,128]{3,2,1,0:T(8,128)S(1)} %get-tuple-element.31), channel_id=1, source_target_pairs={{0,4},{1,5},{2,6},{3,7},{4,8},{5,9},{6,10},{7,11},{8,12},{9,13},{1... | collective-permute-start | bytes 1179656 | tf_op jit(solution)/shard_map/ppermute | solution.py:377
  76.6 2.5 %collective-permute-start.14 = (f32[4,64,128]{2,1,0:T(8,128)S(1)}, f32[4,64,128]{2,1,0:T(8,128)S(1)}, u32[]{:S(2)}, u32[]{:S(2)}) collective-permute-start(f32[4,64,128]{2,1,0:T(8,128)S(1)} %get-tuple-element.56), channel_id=1, source_target_pairs={{0,3},{1,2},{2,1},{3,0},{4,7},{5,6},{6,5},{7,4},{8,11},{9,10},{10,... | collective-permute-start | bytes 393224 | tf_op jit(solution)/shard_map/ppermute | solution.py:374
  80.1 3.8 %collective-permute-done.14.n3 = f32[4,64,128]{2,1,0:T(8,128)S(1)} collective-permute-done((f32[4,64,128]{2,1,0:T(8,128)S(1)}, f32[4,64,128]{2,1,0:T(8,128)S(1)}, u32[]{:S(2)}, u32[]{:S(2)}) %collective-permute-start.14) | collective-permute-done | bytes 131104 | tf_op jit(solution)/shard_map/ppermute | solution.py:374
  83.9 1.7 collective-permute-done.12.n1
  85.7 2.2 collective-permute-done.11.hi
  87.9 9.2 %relax_second.1 = (f32[4,64,128]{2,1,0:T(8,128)S(1)}, f32[4,64,128]{2,1,0:T(8,128)S(1)}, f32[4,64,128]{2,1,0:T(8,128)S(1)}, f32[4,64,128]{2,1,0:T(8,128)S(1)}, f...) custom-call(s32[2]{0:T(128)S(1)} %pad_add_fusion.where, ...), custom_call_target="tpu_custom_call" | custom-call | tf_op jit(solution)/shard_map/relax_second/pallas_call | solution.py:360
  97.1 3.5 %collective-permute-start.15 = (f32[12,8,8,128]{3,2,1,0:T(8,128)S(1)}, f32[12,8,8,128]{3,2,1,0:T(8,128)S(1)}, u32[]{:S(2)}, u32[]{:S(2)}) collective-permute-start(f32[12,8,8,128]{3,2,1,0:T(8,128)S(1)} %get-tuple-element.36), channel_id=1, source_target_pairs={{0,4},{1,5},{2,6},{3,7},{4,8},{5,9},{6,10},{7,11},{8,12},{9,13},{1... | collective-permute-start | bytes 1179656 | tf_op jit(solution)/shard_map/ppermute | solution.py:377
  102.1 6.0 %collective-permute-done.15.lo = f32[12,8,8,128]{3,2,1,0:T(8,128)S(1)} collective-permute-done((f32[12,8,8,128]{3,2,1,0:T(8,128)S(1)}, f32[12,8,8,128]{3,2,1,0:T(8,128)S(1)}, u32[]{:S(2)}, u32[]{:S(2)}) %collective-permute-start.15) | collective-permute-done | bytes 393248 | tf_op jit(solution)/shard_map/ppermute | solution.py:377
  108.1 4.1 %collective-permute-done.16.hi = f32[12,8,8,128]{3,2,1,0:T(8,128)S(1)} collective-permute-done((f32[12,8,8,128]{3,2,1,0:T(8,128)S(1)}, f32[12,8,8,128]{3,2,1,0:T(8,128)S(1)}, u32[]{:S(2)}, u32[]{:S(2)}) %collective-permute-start.16) | collective-permute-done | bytes 393248 | tf_op jit(solution)/shard_map/ppermute | solution.py:380
  112.2 7.6 %again_first.1 = (f32[16,8,8,128]{3,2,1,0:T(8,128)S(1)}, f32[15,8,8,128]{3,2,1,0:T(8,128)S(1)}, f32[15,8,8,128]{3,2,1,0:T(8,128)S(1)}) custom-call(f32[16,8,8,128]{3,2,1,0:T(8,128)S(1)} %get-tuple-element.35.field, f32[12,8,8,128]{3,2,1,0:T(8,128)S(1)} %collective-permute-done.15.lo, f32[12,8,8,128]{3,2,1,0:T(8,128)S(1)} %collective-permute-done.16.hi, ...), custom_call_target="tpu_custom_call" | custom-call | tf_op jit(solution)/shard_map/again_first/pallas_call | solution.py:360
  119.8 2.5 %collective-permute-start.17 = (f32[15,8,8,128]{3,2,1,0:T(8,128)S(1)}, f32[15,8,8,128]{3,2,1,0:T(8,128)S(1)}, u32[]{:S(2)}, u32[]{:S(2)}) collective-permute-start(f32[15,8,8,128]{3,2,1,0:T(8,128)S(1)} %get-tuple-element.39), channel_id=1, source_target_pairs={{0,4},{1,5},{2,6},{3,7},{4,8},{5,9},{6,10},{7,11},{8,12},{9,13},{1... | collective-permute-start | bytes 1474568 | tf_op jit(solution)/shard_map/ppermute | solution.py:377
  123.7 7.4 %collective-permute-done.17.lo = f32[15,8,8,128]{3,2,1,0:T(8,128)S(1)} collective-permute-done((f32[15,8,8,128]{3,2,1,0:T(8,128)S(1)}, f32[15,8,8,128]{3,2,1,0:T(8,128)S(1)}, u32[]{:S(2)}, u32[]{:S(2)}) %collective-permute-start.17) | collective-permute-done | bytes 491552 | tf_op jit(solution)/shard_map/ppermute | solution.py:377
  131.1 4.1 %collective-permute-done.18.hi = f32[15,8,8,128]{3,2,1,0:T(8,128)S(1)} collective-permute-done((f32[15,8,8,128]{3,2,1,0:T(8,128)S(1)}, f32[15,8,8,128]{3,2,1,0:T(8,128)S(1)}, u32[]{:S(2)}, u32[]{:S(2)}) %collective-permute-start.18) | collective-permute-done | bytes 491552 | tf_op jit(solution)/shard_map/ppermute | solution.py:380
  135.2 9.8 %again_second.1 = (f32[22,8,8,128]{3,2,1,0:T(8,128)S(1)}, f32[4,64,128]{2,1,0:T(8,128)S(1)}, f32[4,64,128]{2,1,0:T(8,128)S(1)}, f32[4,64,128]{2,1,0:T(8,128)S(1)}, f32[4,64,128]{2,1,0:T(8,128)S(1)}) custom-call(s32[2]{0:T(128)S(1)} %pad_add_fusion.where, f32[16,8,8,128]{3,2,1,0:T(8,128)S(1)} %get-tuple-element.38.field, ...), custom_call_target="tpu_custom_call" | custom-call | tf_op jit(solution)/shard_map/again_second/pallas_call | solution.py:360
  145.1 2.2 collective-permute-done.19.other
  147.3 3.0 %pairs.1 = f32[16,8,8,128]{3,2,1,0:T(8,128)} custom-call(s32[2]{0:T(128)S(1)} %pad_add_fusion.where, f32[22,8,8,128]{3,2,1,0:T(8,128)S(1)} %get-tuple-element.41.mine, f32[22,8,8,128]{3,2,1,0:T(8,128)S(1)} %collective-permute-done.19.other, f32[46,8,8,128]{3,2,1,0:T(8,128)S(1)} %copy-done), custom_call_target="tpu_custom_call" | custom-call | tf_op jit(solution)/shard_map/pairs/pallas_call | solution.py:360
  150.3 34.3 %all-gather.2.cloned.1.call-done.sums = f32[64,8,8,128]{3,2,1,0:T(8,128)} async-done(((f32[16,8,8,128]{3,2,1,0:T(8,128)}), f32[64,8,8,128]{3,2,1,0:T(8,128)}) %all-gather.2.cloned.1.call-update) | async-done | bytes 2097168 | tf_op jit(solution)/shard_map/all_gather | solution.py:448
  188.1 3.4 %collective-permute-start.20 = (f32[27,8,8,128]{3,2,1,0:T(8,128)S(1)}, f32[27,8,8,128]{3,2,1,0:T(8,128)S(1)}, u32[]{:S(2)}, u32[]{:S(2)}) collective-permute-start(f32[27,8,8,128]{3,2,1,0:T(8,128)S(1)} %pad_maximum_fusion), channel_id=1, source_target_pairs={{0,4},{1,5},{2,6},{3,7},{4,8},{5,9},{6,10},{7,11},{8,12},{9,13},{1... | collective-permute-start | bytes 2654216 | tf_op jit(solution)/shard_map/ppermute | solution.py:377
  191.6 1.5 collective-permute-start.21
  193.1 1.5 collective-permute-start.22
  196.7 1.9 collective-permute-done.22.refs_1_
  198.6 3.6 %collective-permute-done.23.refs_2_ = f32[4,64,128]{2,1,0:T(8,128)S(1)} collective-permute-done((f32[4,64,128]{2,1,0:T(8,128)S(1)}, f32[4,64,128]{2,1,0:T(8,128)S(1)}, u32[]{:S(2)}, u32[]{:S(2)}) %collective-permute-start.23) | collective-permute-done | bytes 131104 | tf_op jit(solution)/shard_map/ppermute | solution.py:374
  207.0 2.8 %collective-permute-done.29.refs_9_ = f32[4,64,128]{2,1,0:T(8,128)S(1)} collective-permute-done((f32[4,64,128]{2,1,0:T(8,128)S(1)}, f32[4,64,128]{2,1,0:T(8,128)S(1)}, u32[]{:S(2)}, u32[]{:S(2)}) %collective-permute-start.29) | collective-permute-done | bytes 131104 | tf_op jit(solution)/shard_map/ppermute | solution.py:374
  209.9 2.6 %collective-permute-done.30.refs_10_ = f32[4,64,128]{2,1,0:T(8,128)S(1)} collective-permute-done((f32[4,64,128]{2,1,0:T(8,128)S(1)}, f32[4,64,128]{2,1,0:T(8,128)S(1)}, u32[]{:S(2)}, u32[]{:S(2)}) %collective-permute-start.30) | collective-permute-done | bytes 131104 | tf_op jit(solution)/shard_map/ppermute | solution.py:374
  214.6 9.9 %chain.1 = (f32[4,4,64,128]{3,2,1,0:T(8,128)}, f32[4,4,64,128]{3,2,1,0:T(8,128)}) custom-call(s32[2]{0:T(128)S(1)} %pad_add_fusion.where, f32[64,8,8,128]{3,2,1,0:T(8,128)} %all-gather.2.cloned.1.call-done.sums, f32[27,8,8,128]{3,2,1,0:T(8,128)S(1)} %collective-permute-done.20.got_lo, f32[27,8,8,128]{3,2,1,0:T(8,128)S(1)} %collective-permute-done.21.got_hi, ...), custom_call_target="tpu_custom_call" | custom-call | tf_op jit(solution)/shard_map/chain/pallas_call | solution.py:360
  (81 shorter events, 29.0 us)
Async XLA Ops:
  7.2 177.5 %all-gather.2.cloned.1.call-start = ((), (), s32[]{:S(2)}) async-start(), calls=%async_computation | async-start | bytes 2621440 | tf_op jit(solution)/shard_map/all_gather | solution.py:448
  7.2 2.3 collective-permute-start.1
  11.7 10.9 %collective-permute-start.4 = (f32[8,64,128]{2,1,0:T(8,128)S(1)}, f32[8,64,128]{2,1,0:T(8,128)S(1)}, u32[]{:S(2)}, u32[]{:S(2)}) collective-permute-start(f32[8,64,128]{2,1,0:T(8,128)S(1)} %get-tuple-element.66), channel_id=1, source_target_pairs={{0,3},{1,2},{2,1},{3,0},{4,7},{5,6},{6,5},{7,4},{8,11},{9,10},{10,... | collective-permute-start | bytes 786440 | tf_op jit(solution)/shard_map/ppermute | solution.py:374
  15.5 12.5 %collective-permute-start.2 = (f32[8,64,128]{2,1,0:T(8,128)S(1)}, f32[8,64,128]{2,1,0:T(8,128)S(1)}, u32[]{:S(2)}, u32[]{:S(2)}) collective-permute-start(f32[8,64,128]{2,1,0:T(8,128)S(1)} %get-tuple-element.67), channel_id=1, source_target_pairs={{0,1},{1,0},{2,3},{3,2},{4,5},{5,4},{6,7},{7,6},{8,9},{9,8},{10,11... | collective-permute-start | bytes 786440 | tf_op jit(solution)/shard_map/ppermute | solution.py:374
  16.0 12.0 %collective-permute-start.3 = (f32[8,64,128]{2,1,0:T(8,128)S(1)}, f32[8,64,128]{2,1,0:T(8,128)S(1)}, u32[]{:S(2)}, u32[]{:S(2)}) collective-permute-start(f32[8,64,128]{2,1,0:T(8,128)S(1)} %get-tuple-element.68), channel_id=1, source_target_pairs={{0,2},{1,3},{2,0},{3,1},{4,6},{5,7},{6,4},{7,5},{8,10},{9,11},{10,... | collective-permute-start | bytes 786440 | tf_op jit(solution)/shard_map/ppermute | solution.py:374
  28.9 22.5 %collective-permute-start.6 = (f32[27,8,8,128]{3,2,1,0:T(8,128)S(1)}, f32[27,8,8,128]{3,2,1,0:T(8,128)S(1)}, u32[]{:S(2)}, u32[]{:S(2)}) collective-permute-start(f32[27,8,8,128]{3,2,1,0:T(8,128)S(1)} %get-tuple-element.28), channel_id=1, source_target_pairs={{0,4},{1,5},{2,6},{3,7},{4,8},{5,9},{6,10},{7,11},{8,12},{9,13},{1... | collective-permute-start | bytes 2654216 | tf_op jit(solution)/shard_map/ppermute | solution.py:377
  32.4 23.1 %collective-permute-start.7 = (f32[27,8,8,128]{3,2,1,0:T(8,128)S(1)}, f32[27,8,8,128]{3,2,1,0:T(8,128)S(1)}, u32[]{:S(2)}, u32[]{:S(2)}) collective-permute-start(f32[27,8,8,128]{3,2,1,0:T(8,128)S(1)} %get-tuple-element.29), channel_id=1, source_target_pairs={{4,0},{5,1},{6,2},{7,3},{8,4},{9,5},{10,6},{11,7},{12,8},{13,9},{1... | collective-permute-start | bytes 2654216 | tf_op jit(solution)/shard_map/ppermute | solution.py:380
  33.7 24.3 %collective-permute-start.5 = (f32[16,8,8,128]{3,2,1,0:T(8,128)S(1)}, f32[16,8,8,128]{3,2,1,0:T(8,128)S(1)}, u32[]{:S(2)}, u32[]{:S(2)}) collective-permute-start(f32[16,8,8,128]{3,2,1,0:T(8,128)S(1)} %get-tuple-element.27.mine), channel_id=1, source_target_pairs={{0,16},{16,0},{1,17},{17,1},{2,18},{18,2},{3,19},{19,3},{4,20},{20... | collective-permute-start | bytes 1572872 | tf_op jit(solution)/shard_map/ppermute | solution.py:371
  52.2 5.8 %collective-permute-start.8 = (f32[15,8,8,128]{3,2,1,0:T(8,128)}, f32[15,8,8,128]{3,2,1,0:T(8,128)}, u32[]{:S(2)}, u32[]{:S(2)}) collective-permute-start(f32[15,8,8,128]{3,2,1,0:T(8,128)} %slice.38), channel_id=1, source_target_pairs={{0,16},{16,0},{1,17},{17,1},{2,18},{18,2},{3,19},{19,3},{4,20},{20... | collective-permute-start | bytes 1474568 | tf_op jit(solution)/shard_map/ppermute | solution.py:371
  56.3 2.2 collective-permute-start.9
  71.5 14.1 %collective-permute-start.10 = (f32[12,8,8,128]{3,2,1,0:T(8,128)S(1)}, f32[12,8,8,128]{3,2,1,0:T(8,128)S(1)}, u32[]{:S(2)}, u32[]{:S(2)}) collective-permute-start(f32[12,8,8,128]{3,2,1,0:T(8,128)S(1)} %get-tuple-element.31), channel_id=1, source_target_pairs={{0,4},{1,5},{2,6},{3,7},{4,8},{5,9},{6,10},{7,11},{8,12},{9,13},{1... | collective-permute-start | bytes 1179656 | tf_op jit(solution)/shard_map/ppermute | solution.py:377
  75.1 12.8 %collective-permute-start.11 = (f32[12,8,8,128]{3,2,1,0:T(8,128)S(1)}, f32[12,8,8,128]{3,2,1,0:T(8,128)S(1)}, u32[]{:S(2)}, u32[]{:S(2)}) collective-permute-start(f32[12,8,8,128]{3,2,1,0:T(8,128)S(1)} %get-tuple-element.32), channel_id=1, source_target_pairs={{4,0},{5,1},{6,2},{7,3},{8,4},{9,5},{10,6},{11,7},{12,8},{13,9},{1... | collective-permute-start | bytes 1179656 | tf_op jit(solution)/shard_map/ppermute | solution.py:380
  76.6 7.3 %collective-permute-start.14 = (f32[4,64,128]{2,1,0:T(8,128)S(1)}, f32[4,64,128]{2,1,0:T(8,128)S(1)}, u32[]{:S(2)}, u32[]{:S(2)}) collective-permute-start(f32[4,64,128]{2,1,0:T(8,128)S(1)} %get-tuple-element.56), channel_id=1, source_target_pairs={{0,3},{1,2},{2,1},{3,0},{4,7},{5,6},{6,5},{7,4},{8,11},{9,10},{10,... | collective-permute-start | bytes 393224 | tf_op jit(solution)/shard_map/ppermute | solution.py:374
  79.1 6.6 %collective-permute-start.12 = (f32[4,64,128]{2,1,0:T(8,128)S(1)}, f32[4,64,128]{2,1,0:T(8,128)S(1)}, u32[]{:S(2)}, u32[]{:S(2)}) collective-permute-start(f32[4,64,128]{2,1,0:T(8,128)S(1)} %get-tuple-element.58), channel_id=1, source_target_pairs={{0,1},{1,0},{2,3},{3,2},{4,5},{5,4},{6,7},{7,6},{8,9},{9,8},{10,11... | collective-permute-start | bytes 393224 | tf_op jit(solution)/shard_map/ppermute | solution.py:374
  79.6 6.0 %collective-permute-start.13 = (f32[4,64,128]{2,1,0:T(8,128)S(1)}, f32[4,64,128]{2,1,0:T(8,128)S(1)}, u32[]{:S(2)}, u32[]{:S(2)}) collective-permute-start(f32[4,64,128]{2,1,0:T(8,128)S(1)} %get-tuple-element.59), channel_id=1, source_target_pairs={{0,2},{1,3},{2,0},{3,1},{4,6},{5,7},{6,4},{7,5},{8,10},{9,11},{10,... | collective-permute-start | bytes 393224 | tf_op jit(solution)/shard_map/ppermute | solution.py:374
  97.1 11.0 %collective-permute-start.15 = (f32[12,8,8,128]{3,2,1,0:T(8,128)S(1)}, f32[12,8,8,128]{3,2,1,0:T(8,128)S(1)}, u32[]{:S(2)}, u32[]{:S(2)}) collective-permute-start(f32[12,8,8,128]{3,2,1,0:T(8,128)S(1)} %get-tuple-element.36), channel_id=1, source_target_pairs={{0,4},{1,5},{2,6},{3,7},{4,8},{5,9},{6,10},{7,11},{8,12},{9,13},{1... | collective-permute-start | bytes 1179656 | tf_op jit(solution)/shard_map/ppermute | solution.py:377
  100.6 11.6 %collective-permute-start.16 = (f32[12,8,8,128]{3,2,1,0:T(8,128)S(1)}, f32[12,8,8,128]{3,2,1,0:T(8,128)S(1)}, u32[]{:S(2)}, u32[]{:S(2)}) collective-permute-start(f32[12,8,8,128]{3,2,1,0:T(8,128)S(1)} %get-tuple-element.37), channel_id=1, source_target_pairs={{4,0},{5,1},{6,2},{7,3},{8,4},{9,5},{10,6},{11,7},{12,8},{13,9},{1... | collective-permute-start | bytes 1179656 | tf_op jit(solution)/shard_map/ppermute | solution.py:380
  119.8 11.2 %collective-permute-start.17 = (f32[15,8,8,128]{3,2,1,0:T(8,128)S(1)}, f32[15,8,8,128]{3,2,1,0:T(8,128)S(1)}, u32[]{:S(2)}, u32[]{:S(2)}) collective-permute-start(f32[15,8,8,128]{3,2,1,0:T(8,128)S(1)} %get-tuple-element.39), channel_id=1, source_target_pairs={{0,4},{1,5},{2,6},{3,7},{4,8},{5,9},{6,10},{7,11},{8,12},{9,13},{1... | collective-permute-start | bytes 1474568 | tf_op jit(solution)/shard_map/ppermute | solution.py:377
  122.4 12.8 %collective-permute-start.18 = (f32[15,8,8,128]{3,2,1,0:T(8,128)S(1)}, f32[15,8,8,128]{3,2,1,0:T(8,128)S(1)}, u32[]{:S(2)}, u32[]{:S(2)}) collective-permute-start(f32[15,8,8,128]{3,2,1,0:T(8,128)S(1)} %get-tuple-element.40), channel_id=1, source_target_pairs={{4,0},{5,1},{6,2},{7,3},{8,4},{9,5},{10,6},{11,7},{12,8},{13,9},{1... | collective-permute-start | bytes 1474568 | tf_op jit(solution)/shard_map/ppermute | solution.py:380
  145.1 2.3 collective-permute-start.19
  188.1 26.2 %collective-permute-start.20 = (f32[27,8,8,128]{3,2,1,0:T(8,128)S(1)}, f32[27,8,8,128]{3,2,1,0:T(8,128)S(1)}, u32[]{:S(2)}, u32[]{:S(2)}) collective-permute-start(f32[27,8,8,128]{3,2,1,0:T(8,128)S(1)} %pad_maximum_fusion), channel_id=1, source_target_pairs={{0,4},{1,5},{2,6},{3,7},{4,8},{5,9},{6,10},{7,11},{8,12},{9,13},{1... | collective-permute-start | bytes 2654216 | tf_op jit(solution)/shard_map/ppermute | solution.py:377
  191.6 23.0 %collective-permute-start.21 = (f32[27,8,8,128]{3,2,1,0:T(8,128)S(1)}, f32[27,8,8,128]{3,2,1,0:T(8,128)S(1)}, u32[]{:S(2)}, u32[]{:S(2)}) collective-permute-start(f32[27,8,8,128]{3,2,1,0:T(8,128)S(1)} %pad_maximum_fusion.1), channel_id=1, source_target_pairs={{4,0},{5,1},{6,2},{7,3},{8,4},{9,5},{10,6},{11,7},{12,8},{13,9},{1... | collective-permute-start | bytes 2654216 | tf_op jit(solution)/shard_map/ppermute | solution.py:380
  193.1 5.5 %collective-permute-start.22 = (f32[4,64,128]{2,1,0:T(8,128)S(1)}, f32[4,64,128]{2,1,0:T(8,128)S(1)}, u32[]{:S(2)}, u32[]{:S(2)}) collective-permute-start(f32[4,64,128]{2,1,0:T(8,128)S(1)} %get-tuple-element.43), channel_id=1, source_target_pairs={{0,1},{1,0},{2,3},{3,2},{4,5},{5,4},{6,7},{7,6},{8,9},{9,8},{10,11... | collective-permute-start | bytes 393224 | tf_op jit(solution)/shard_map/ppermute | solution.py:374
  194.7 7.5 %collective-permute-start.23 = (f32[4,64,128]{2,1,0:T(8,128)S(1)}, f32[4,64,128]{2,1,0:T(8,128)S(1)}, u32[]{:S(2)}, u32[]{:S(2)}) collective-permute-start(f32[4,64,128]{2,1,0:T(8,128)S(1)} %get-tuple-element.44), channel_id=1, source_target_pairs={{0,2},{1,3},{2,0},{3,1},{4,6},{5,7},{6,4},{7,5},{8,10},{9,11},{10,... | collective-permute-start | bytes 393224 | tf_op jit(solution)/shard_map/ppermute | solution.py:374
  195.2 7.0 %collective-permute-start.24 = (f32[4,64,128]{2,1,0:T(8,128)S(1)}, f32[4,64,128]{2,1,0:T(8,128)S(1)}, u32[]{:S(2)}, u32[]{:S(2)}) collective-permute-start(f32[4,64,128]{2,1,0:T(8,128)S(1)} %get-tuple-element.45), channel_id=1, source_target_pairs={{0,3},{1,2},{2,1},{3,0},{4,7},{5,6},{6,5},{7,4},{8,11},{9,10},{10,... | collective-permute-start | bytes 393224 | tf_op jit(solution)/shard_map/ppermute | solution.py:374
  198.6 4.1 %collective-permute-start.25 = (f32[4,64,128]{2,1,0:T(8,128)S(1)}, f32[4,64,128]{2,1,0:T(8,128)S(1)}, u32[]{:S(2)}, u32[]{:S(2)}) collective-permute-start(f32[4,64,128]{2,1,0:T(8,128)S(1)} %get-tuple-element.42.refs_0_), channel_id=1, source_target_pairs={{0,16},{16,0},{1,17},{17,1},{2,18},{18,2},{3,19},{19,3},{4,20},{20... | collective-permute-start | bytes 393224 | tf_op jit(solution)/shard_map/ppermute | solution.py:371
  202.2 2.2 collective-permute-start.27
  202.7 2.9 %collective-permute-start.28 = (f32[4,64,128]{2,1,0:T(8,128)S(1)}, f32[4,64,128]{2,1,0:T(8,128)S(1)}, u32[]{:S(2)}, u32[]{:S(2)}) collective-permute-start(f32[4,64,128]{2,1,0:T(8,128)S(1)} %collective-permute-done.24.refs_3_), channel_id=1, source_target_pairs={{0,16},{16,0},{1,17},{17,1},{2,18},{18,2},{3,19},{19,3},{4,20},{20... | collective-permute-start | bytes 393224 | tf_op jit(solution)/shard_map/ppermute | solution.py:371
  203.5 6.3 %collective-permute-start.29 = (f32[4,64,128]{2,1,0:T(8,128)S(1)}, f32[4,64,128]{2,1,0:T(8,128)S(1)}, u32[]{:S(2)}, u32[]{:S(2)}) collective-permute-start(f32[4,64,128]{2,1,0:T(8,128)S(1)} %get-tuple-element.47), channel_id=1, source_target_pairs={{0,1},{1,0},{2,3},{3,2},{4,5},{5,4},{6,7},{7,6},{8,9},{9,8},{10,11... | collective-permute-start | bytes 393224 | tf_op jit(solution)/shard_map/ppermute | solution.py:374
  204.4 8.1 %collective-permute-start.30 = (f32[4,64,128]{2,1,0:T(8,128)S(1)}, f32[4,64,128]{2,1,0:T(8,128)S(1)}, u32[]{:S(2)}, u32[]{:S(2)}) collective-permute-start(f32[4,64,128]{2,1,0:T(8,128)S(1)} %get-tuple-element.48), channel_id=1, source_target_pairs={{0,2},{1,3},{2,0},{3,1},{4,6},{5,7},{6,4},{7,5},{8,10},{9,11},{10,... | collective-permute-start | bytes 393224 | tf_op jit(solution)/shard_map/ppermute | solution.py:374
  205.6 6.9 %collective-permute-start.31 = (f32[4,64,128]{2,1,0:T(8,128)S(1)}, f32[4,64,128]{2,1,0:T(8,128)S(1)}, u32[]{:S(2)}, u32[]{:S(2)}) collective-permute-start(f32[4,64,128]{2,1,0:T(8,128)S(1)} %get-tuple-element.49), channel_id=1, source_target_pairs={{0,3},{1,2},{2,1},{3,0},{4,7},{5,6},{6,5},{7,4},{8,11},{9,10},{10,... | collective-permute-start | bytes 393224 | tf_op jit(solution)/shard_map/ppermute | solution.py:374
  209.9 3.1 %collective-permute-start.32 = (f32[4,64,128]{2,1,0:T(8,128)S(1)}, f32[4,64,128]{2,1,0:T(8,128)S(1)}, u32[]{:S(2)}, u32[]{:S(2)}) collective-permute-start(f32[4,64,128]{2,1,0:T(8,128)S(1)} %get-tuple-element.46.refs_8_), channel_id=1, source_target_pairs={{0,16},{16,0},{1,17},{17,1},{2,18},{18,2},{3,19},{19,3},{4,20},{20... | collective-permute-start | bytes 393224 | tf_op jit(solution)/shard_map/ppermute | solution.py:371
  (12 other events, 108.5 us)
Sparse Core Ops, SparseCore 0:
  150.4 34.1 all-gather.1

commit v2 on v1

--- a/solution.py
+++ b/solution.py
@@ -128,7 +128,7 @@
     return src
 
 
-def place_kernel(where, own, r1, r2, r3, field, coef, field_up, field_dn, *, each, halo, wide):
+def place_kernel(where, own, r1, r2, r3, field, field_up, field_dn, *, each):
     q = where[0]
     J = field.shape[1]
     for j, ref in enumerate((own, r1, r2, r3)):
@@ -136,53 +136,40 @@
         for z in range(each):
             for row in range(J):
                 field[base + z, row] = rows(ref, z, row, J)
-                coef[base + z, row] = rows(ref, each + z, row, J)
-    slab = field.shape[0]
-    copy_planes(halo, field_up, field, 0, slab - halo)
-    copy_planes(wide, field_up, coef, halo, slab - wide)
+    halo = field_up.shape[0]
+    copy_planes(halo, field_up, field, 0, field.shape[0] - halo)
     copy_planes(halo, field_dn, field, 0, 0)
-    copy_planes(wide, field_dn, coef, halo, 0)
 
 
 def first_kernel(
-    where, amounts, field, mine, other, got_lo, got_hi, other_lo, other_hi,
-    out, up, dn, cond, force, a, b, raw, *, halo, wide,
+    where, amounts, field, lo, hi, m0, m1, m2, m3, o0, o1, o2, o3,
+    out, up, dn, cond, force, a, b, raw, *, wide, each,
 ):
-    core = where[1]
+    q, core = where[0], where[1]
     J, width = a.shape[1], a.shape[3]
-    slab = field.shape[0]
+    slab, halo = field.shape[0], lo.shape[0]
     total = slab + 2 * halo
     span = slab + 2 * wide
-    copy_planes(halo, a, got_lo, 0, 0)
-    copy_planes(slab, a, field, halo, 0)
-    copy_planes(halo, a, got_hi, halo + slab, 0)
-
-    def fill(slot, lo, mid, hi, off):
-        def one(n, src, d0, s0):
-            def body(z, c):
-                for j in range(J):
-                    raw[slot, d0 + z, j] = src[s0 + z, j]
-                return c
-
-            lax.fori_loop(0, n, body, 0)
-
-        one(wide, lo, 0, off)
-        one(slab, mid, wide, 0)
-        one(wide, hi, wide + slab, off)
-
-    fill(core, got_lo, mine, got_hi, halo)
-    fill(1 - core, other_lo, other, other_hi, 0)
-    copy_planes(span, cond, raw.at[0])
+    load_state(a, lo, field, hi)
+    skip = slab - wide
+    for i, pieces in enumerate(zip((m0, m1, m2, m3), (o0, o1, o2, o3))):
+        base = lax.bitwise_xor(q, i) * each
+        for slot, ref in zip((core, 1 - core), pieces):
+            for part in range(3):
+                for z in range(each):
+                    for j in range(J):
+                        raw[slot, part * slab + base + z, j] = rows(ref, part * each + z, j, J)
+    copy_planes(span, cond, raw.at[0], 0, skip)
 
     def inner(z, j, w, beside):
-        raw[0, z, j] = FINE_Q[1] * w + FINE_Q[2] * cond[z, j] * (6.0 * w - beside)
+        raw[0, z + skip, j] = FINE_Q[1] * w + FINE_Q[2] * cond[z, j] * (6.0 * w - beside)
 
     def outer(z, j, w, beside):
-        force[z, j] = FINE_Q[0] * raw[1, z, j] + cond[z, j] * (6.0 * w - beside)
+        force[z, j] = FINE_Q[0] * raw[1, z + skip, j] + cond[z, j] * (6.0 * w - beside)
 
     margin = wide - (halo - SWEEPS)
-    sweep(margin - 1, span - margin + 1, lambda z, j: raw[1, z, j], inner, J, width)
-    sweep(margin, span - margin, lambda z, j: raw[0, z, j], outer, J, width)
+    sweep(margin - 1, span - margin + 1, lambda z, j: raw[1, z + skip, j], inner, J, width)
+    sweep(margin, span - margin, lambda z, j: raw[0, z + skip, j], outer, J, width)
 
     state = fine_steps(a, b, cond, wide - halo, total, halo, amounts, 0, force)
     copy_planes(slab, out, state, 0, halo)
@@ -255,25 +242,47 @@
     factor(a, both.at[0], cond, COARSE[0], 1, total - 1, k0=k0)
     factor(b, a, cond, COARSE[1], 2, total - 2, k0=k0)
     factor(a, b, cond, COARSE[2], 3, total - 3, k0=k0, extra=lambda z, j: both[1, z, j])
-    copy_planes(slab, out, a, 0, SWEEPS)
-
-
-def chain_kernel(where, sums, got_lo, got_hi, cond, *refs, wide, each, reach):
-    pieces, refs = refs[:16], refs[16:]
+    half = out.shape[1]
+
+    def give(z, c):
+        for j in range(half):
+            out[z, j] = a[SWEEPS + z, core * half + j]
+        return c
+
+    lax.fori_loop(0, slab, give, 0)
+
+
+def order_kernel(where, own, r1, r2, r3, sums, send_up, send_dn, all_sums, *, reach):
+    q = where[0]
+    slab = own.shape[0]
+    for i, ref in enumerate((own, r1, r2, r3)):
+        copy_planes(slab, all_sums, ref, lax.bitwise_xor(q, i) * slab, 0)
+    offset = 0
+    for i, h in enumerate(reach):
+        copy_planes(slab, sums, all_sums, i * slab, i * slab)
+        copy_planes(h, send_up, all_sums, offset, (i + 1) * slab - h)
+        copy_planes(h, send_dn, all_sums, offset, i * slab)
+        offset += h
+
+
+def chain_kernel(
+    where, sums, got_lo, got_hi, other_sums, other_lo, other_hi, cond, *refs, wide, each, reach
+):
+    pieces, refs = refs[:10], refs[10:]
     corrected, residual, ends, a, b, c, d, relaxed, remain, error = refs
     q, core = where[0], where[1]
     J = a.shape[1]
-    count = len(reach) + 1
-    slab = sums.shape[0] // count
-    mine_rel, other_rel, mine_res, other_res = (pieces[4 * i : 4 * i + 4] for i in range(4))
+    slab = sums.shape[0] // len(reach)
+    half = J // 2
+    mine_rel, other_rel, mine_res, other_res = pieces[:4], pieces[4], pieces[5:9], pieces[9]
     for i in range(4):
         place = lax.bitwise_xor(q, i)
         for z in range(each):
             for j in range(J):
                 relaxed[2 * place + core, z, j] = rows(mine_rel[i], z, j, J)
-                relaxed[2 * place + 1 - core, z, j] = rows(other_rel[i], z, j, J)
+                relaxed[2 * place + 1 - core, z, j] = rows(other_rel, i * each + z, j, J)
                 remain[2 * place + 1 + core, z, j] = rows(mine_res[i], z, j, J)
-                remain[2 * place + 2 - core, z, j] = rows(other_res[i], z, j, J)
+                remain[2 * place + 2 - core, z, j] = rows(other_res, i * each + z, j, J)
     zero = jnp.zeros(a.shape[2:], jnp.float32)
     for z in range(each):
         for j in range(J):
@@ -281,9 +290,19 @@
             error[0, z, j] = zero
     offset = 0
     for i, h in enumerate(reach):
-        copy_planes(h, ends.at[i], got_lo, 0, offset)
-        copy_planes(slab, ends.at[i], sums, h, i * slab)
-        copy_planes(h, ends.at[i], got_hi, h + slab, offset)
+
+        def fill(n, mine, other, d0, s0, i=i):
+            def one(z, carry):
+                for j in range(half):
+                    ends[i, d0 + z, core * half + j] = mine[s0 + z, j]
+                    ends[i, d0 + z, (1 - core) * half + j] = other[s0 + z, j]
+                return carry
+
+            lax.fori_loop(0, n, one, 0)
+
+        fill(h, got_lo, other_lo, 0, offset)
+        fill(slab, sums, other_sums, h, i * slab)
+        fill(h, got_hi, other_hi, h + slab, offset)
         offset += h
     top = reach[0]
     window = each + 2 * top
@@ -356,7 +375,7 @@
     smem = pl.BlockSpec(memory_space=pltpu.SMEM)
     vmem = pl.BlockSpec(memory_space=pltpu.VMEM)
 
-    def call(kernel, scalars, arrays, outs, scratches, name):
+    def call(kernel, scalars, arrays, outs, scratches, name, micros):
         return pl.pallas_call(
             kernel,
             out_shape=outs,
@@ -364,6 +383,9 @@
             out_specs=jax.tree.map(lambda _: vmem, outs),
             scratch_shapes=scratches,
             compiler_params=VMEM,
+            cost_estimate=pl.CostEstimate(
+                flops=micros * 10**9, bytes_accessed=micros * 3 * 10**6, transcendentals=0
+            ),
             name=name,
         )(*scalars, *arrays)
 
@@ -390,74 +412,88 @@
 
     entries = jnp.concatenate([initial[None], guesses[:-1]], axis=0)
     coef = jnp.where(first, conduct, source)
+    coef = jnp.concatenate([up(coef), coef, down(coef)], axis=0)
 
     def entry_for(j):
-        t = 2 * (q ^ j) + core
-        return jnp.concatenate([lax.dynamic_index_in_dim(entries, t, 0, False), coef], axis=0)
+        return lax.dynamic_index_in_dim(entries, 2 * (q ^ j) + core, 0, False)
 
     def after_for(j):
-        t = 2 * (q ^ j) + core
-        return lax.dynamic_index_in_dim(guesses, t, 0, False)
-
-    got = [entry_for(0)] + [across(entry_for(j), j) for j in range(1, slots)]
-    after = [after_for(0)] + [across(after_for(j), j) for j in range(1, slots)]
-
-    field, mine, send_up, send_dn = call(
-        partial(place_kernel, each=each, halo=halo, wide=wide),
-        [where], got, [blocked(slab), blocked(slab), blocked(halo + wide), blocked(halo + wide)], [], "place",
-    )
-    other = swap(mine)
-    got_lo, got_hi = up(send_up), down(send_dn)
-    other_lo, other_hi = swap(got_lo[halo:]), swap(got_hi[halo:])
+        return lax.dynamic_index_in_dim(guesses, 2 * (q ^ j) + core, 0, False)
+
+    def gathered(pieces):
+        return [pieces[0]] + [across(pieces[j], j) for j in range(1, slots)]
+
+    field, send_up, send_dn = call(
+        partial(place_kernel, each=each),
+        [where], gathered([entry_for(j) for j in range(slots)]),
+        [blocked(slab), blocked(halo), blocked(halo)], [], "place", 1,
+    )
+    mine = gathered([coef] * slots)
+    lo, hi = up(send_up), down(send_dn)
     span, total = slab + 2 * wide, slab + 2 * halo
+    others = [swap(m) for m in mine]
+    after = [after_for(j) for j in range(slots)]
+    *after, lo = lax.optimization_barrier((*after, lo))
+    after = gathered(after)
     state, send_up, send_dn, cond, force = call(
-        partial(first_kernel, halo=halo, wide=wide),
-        [where, amounts], [field, mine, other, got_lo, got_hi, other_lo, other_hi],
+        partial(first_kernel, wide=wide, each=each),
+        [where, amounts], [field, lo, hi, *mine, *others],
         [blocked(slab), blocked(halo), blocked(halo), blocked(span), blocked(span)],
-        [scratch(total), scratch(total), scratch(2, span)], "relax_first",
-    )
+        [scratch(total), scratch(total), scratch(2, 3 * slab)], "relax_first", 12,
+    )
+    *after, send_up, send_dn = lax.optimization_barrier((*after, send_up, send_dn))
     *rel, state, send_up, send_dn = call(
         partial(second_kernel, wide=wide, each=each, step=halo // SWEEPS),
         [where, amounts], [state, up(send_up), down(send_dn), cond, force, *after],
         [natural(each)] * 4 + [blocked(slab), blocked(halo), blocked(halo)],
-        [scratch(total), scratch(total)], "relax_second",
-    )
-    rel = [rel[0]] + [across(rel[j], j) for j in range(1, slots)]
+        [scratch(total), scratch(total)], "relax_second", 9,
+    )
+    lo, hi = up(send_up), down(send_dn)
+    *rel, lo = lax.optimization_barrier((*rel, lo))
+    rel = gathered(rel)
     state, send_up, send_dn = call(
         partial(third_kernel, wide=wide),
-        [], [state, up(send_up), down(send_dn), cond],
+        [], [state, lo, hi, cond],
         [blocked(slab), blocked(wide), blocked(wide)],
-        [scratch(total), scratch(total)], "again_first",
-    )
+        [scratch(total), scratch(total)], "again_first", 8,
+    )
+    *rel, send_up, send_dn = lax.optimization_barrier((*rel, send_up, send_dn))
+    rel_other = swap(jnp.concatenate(rel, axis=0))
+    lo, hi = up(send_up), down(send_dn)
+    rel_other, lo = lax.optimization_barrier((rel_other, lo))
     remain, *res = call(
         partial(fourth_kernel, levels=halo, each=each),
-        [where], [state, up(send_up), down(send_dn), cond],
+        [where], [state, lo, hi, cond],
         [blocked(slab + 2 * SWEEPS)] + [natural(each)] * 4,
-        [scratch(span), scratch(span)], "again_second",
-    )
-    res = [res[0]] + [across(res[j], j) for j in range(1, slots)]
-    rel_other = [swap(r) for r in rel]
-    res_other = [swap(r) for r in res]
-
+        [scratch(span), scratch(span)], "again_second", 9,
+    )
     pair = call(
         partial(pair_kernel, wide=wide),
         [where], [remain, swap(remain), cond],
-        blocked(slab), [scratch(2, slab + 2 * SWEEPS), scratch(slab + 2 * SWEEPS), scratch(slab + 2 * SWEEPS)], "pairs",
-    )
-    groups = [[g * slots + i for i in range(slots)] for g in range(count // slots)]
-    sums = lax.all_gather(pair, "space", axis=0, tiled=True, axis_index_groups=groups)
+        jax.ShapeDtypeStruct((slab, J // 2, SUB, ny), f32),
+        [scratch(2, slab + 2 * SWEEPS), scratch(slab + 2 * SWEEPS), scratch(slab + 2 * SWEEPS)], "pairs", 3,
+    )
     reach = [2 * SWEEPS * (slots - 2 - i) + SWEEPS for i in range(slots - 1)]
-    send_up = jnp.concatenate([sums[(i + 1) * slab - h : (i + 1) * slab] for i, h in enumerate(reach)], axis=0)
-    send_dn = jnp.concatenate([sums[i * slab : i * slab + h] for i, h in enumerate(reach)], axis=0)
+    halves = lambda n: jax.ShapeDtypeStruct((n, J // 2, SUB, ny), f32)
+    sums, send_up, send_dn = call(
+        partial(order_kernel, reach=reach),
+        [where], gathered([pair] * slots),
+        [halves(len(reach) * slab), halves(sum(reach)), halves(sum(reach))],
+        [pltpu.VMEM((slots * slab, J // 2, SUB, ny), f32)], "order", 1,
+    )
+    *res, sums = lax.optimization_barrier((*res, sums))
+    res = gathered(res)
+    res_other = swap(jnp.concatenate(res, axis=0))
+    lo, hi = up(send_up), down(send_dn)
     window = each + 2 * reach[0]
     corrected, residual = call(
         partial(chain_kernel, wide=wide, each=each, reach=reach),
-        [where], [sums, up(send_up), down(send_dn), cond, *rel, *rel_other, *res, *res_other],
+        [where], [sums, lo, hi, swap(sums), swap(lo), swap(hi), cond, *rel, rel_other, *res, res_other],
         [jax.ShapeDtypeStruct(guess.shape, f32)] * 2,
         [scratch(len(reach), slab + 2 * reach[0])]
         + [scratch(window)] * 4
         + [scratch(2 * slots, each), scratch(2 * slots + 1, each), scratch(2 * slots, each)],
-        "chain",
+        "chain", 9,
     )
     return corrected, residual
 

time: 232 us -> 188 us (0.81)
  waiting for transfers between devices: 114 us -> 70.3 us
  starting transfers between devices: 40.8 us -> 57 us
  between operations: 14.3 us -> 1.06 us
  local copies, waits for them, and re-layouts: 5.66 us -> 2.45 us
    all_gather x1 -> x0, waiting for transfers between devices: 34.3 us -> none  [body(): lax.all_gather(pair, 'space', axis=0, tiled=True, axis_index_groups=groups)]
    ppermute x5 -> x6, waiting for transfers between devices: 30.9 us -> 19.2 us  [up(): lax.ppermute(value, 'space', [(s, s + slots) for s in range(count - slots)])]
    ppermute x12 -> x18, starting transfers between devices: 15 us -> 24.2 us  [across(): lax.ppermute(value, 'space', [(s, s - s % slots + (s % slots ^ j)) for s...]
    ppermute x5 -> x6, starting transfers between devices: 16.6 us -> 22.5 us  [up(): lax.ppermute(value, 'space', [(s, s + slots) for s in range(count - slots)])]
    slice x5 -> x0, local copies, waits for them, and re-layouts: 4.97 us -> none  [the longest x3 3.32 us: body(): sums[i * slab:i * slab + h]]
    ppermute x5 -> x6, waiting for transfers between devices: 14.1 us -> 16 us  [down(): lax.ppermute(value, 'space', [(s + slots, s) for s in range(count - slots)])]
    ppermute x12 -> x18, waiting for transfers between devices: 28.3 us -> 30 us  [across(): lax.ppermute(value, 'space', [(s, s - s % slots + (s % slots ^ j)) for s...]
    ppermute x14 -> x12, waiting for transfers between devices: 6.57 us -> 5.08 us  [swap(): return lax.ppermute(value, 'tm', [(0, 1), (1, 0)])]
  transfers between devices with their start and end apart: 37 -> 42, of which waited for: 25 -> 21; matrix products, arithmetic and copies ran while one was open for 1% -> 2% of each run, Pallas kernels for 0% -> 11%
where the time goes in v2:
time: 188 us
  waiting for transfers between devices  70.3 us (37%)
  starting transfers between devices  57 us (30%)
  Pallas kernels  53.2 us (28%)
  other arithmetic  3.75 us (2%)
  local copies, waits for them, and re-layouts  2.45 us (1%)
    pallas_call x8, Pallas kernels, call(): pl.pallas_call(kernel, out_shape=outs, in_specs=[smem] * len(scalars) + [...  53.2 us
    ppermute x18, waiting for transfers between devices, across(): lax.ppermute(value, 'space', [(s, s - s % slots + (s % slots ^ j)) for s...  30 us
    ppermute x18, starting transfers between devices, across(): lax.ppermute(value, 'space', [(s, s - s % slots + (s % slots ^ j)) for s...  24.2 us
    ppermute x6, starting transfers between devices, up(): lax.ppermute(value, 'space', [(s, s + slots) for s in range(count - slots)])  22.5 us
    ppermute x6, waiting for transfers between devices, up(): lax.ppermute(value, 'space', [(s, s + slots) for s in range(count - slots)])  19.2 us
    ppermute x6, waiting for transfers between devices, down(): lax.ppermute(value, 'space', [(s + slots, s) for s in range(count - slots)])  16 us
    ppermute x6, starting transfers between devices, down(): lax.ppermute(value, 'space', [(s + slots, s) for s in range(count - slots)])  8.14 us
    ppermute x12, waiting for transfers between devices, swap(): return lax.ppermute(value, 'tm', [(0, 1), (1, 0)])  5.08 us
  transfers between devices with their start and end apart: 42, of which 21 were waited for; matrix products, arithmetic and copies ran while one was open for 2% of the time, Pallas kernels for 11%

profile of v2, /device:TPU:0, one launch (start us, length us, event | category | flops | bytes accessed | tf_op | source)
XLA Modules:
  0.0 187.7 jit_solution(17168450711170355425)
XLA Ops:
  3.4 5.1 %collective-permute-start.7 = (f32[4,64,128]{2,1,0:T(8,128)S(1)}, f32[4,64,128]{2,1,0:T(8,128)S(1)}, u32[]{:S(2)}, u32[]{:S(2)}) collective-permute-start(f32[4,64,128]{2,1,0:T(8,128)S(1)} %broadcast_select_fusion.2), channel_id=1, source_target_pairs={{0,4},{1,5},{2,6},{3,7},{4,8},{5,9},{6,10},{7,11},{8,12},{9,13},{1... | collective-permute-start | bytes 393224 | tf_op jit(solution)/shard_map/ppermute | solution.py:399
  11.0 2.9 %collective-permute-start.4 = (f32[4,64,128]{2,1,0:T(8,128)S(1)}, f32[4,64,128]{2,1,0:T(8,128)S(1)}, u32[]{:S(2)}, u32[]{:S(2)}) collective-permute-start(f32[4,64,128]{2,1,0:T(8,128)S(1)} %get-tuple-element.116), channel_id=1, source_target_pairs={{0,3},{1,2},{2,1},{3,0},{4,7},{5,6},{6,5},{7,4},{8,11},{9,10},{10,... | collective-permute-start | bytes 393224 | tf_op jit(solution)/shard_map/ppermute | solution.py:396
  14.7 2.9 %collective-permute-start.11 = (f32[12,64,128]{2,1,0:T(8,128)S(1)}, f32[12,64,128]{2,1,0:T(8,128)S(1)}, u32[]{:S(2)}, u32[]{:S(2)}) collective-permute-start(f32[12,64,128]{2,1,0:T(8,128)S(1)} %pad_maximum_fusion.2.m0), channel_id=1, source_target_pairs={{0,3},{1,2},{2,1},{3,0},{4,7},{5,6},{6,5},{7,4},{8,11},{9,10},{10,... | collective-permute-start | bytes 1179656 | tf_op jit(solution)/shard_map/ppermute | solution.py:396
  18.3 2.0 %collective-permute-start.9 = (f32[12,64,128]{2,1,0:T(8,128)S(1)}, f32[12,64,128]{2,1,0:T(8,128)S(1)}, u32[]{:S(2)}, u32[]{:S(2)}) collective-permute-start(f32[12,64,128]{2,1,0:T(8,128)S(1)} %pad_maximum_fusion.2.m0), channel_id=1, source_target_pairs={{0,1},{1,0},{2,3},{3,2},{4,5},{5,4},{6,7},{7,6},{8,9},{9,8},{10,11... | collective-permute-start | bytes 1179656 | tf_op jit(solution)/shard_map/ppermute | solution.py:396
  21.7 7.7 %collective-permute-done.3.r2 = f32[4,64,128]{2,1,0:T(8,128)S(1)} collective-permute-done((f32[4,64,128]{2,1,0:T(8,128)S(1)}, f32[4,64,128]{2,1,0:T(8,128)S(1)}, u32[]{:S(2)}, u32[]{:S(2)}) %collective-permute-start.3) | collective-permute-done | bytes 131104 | tf_op jit(solution)/shard_map/ppermute | solution.py:396
  30.1 3.5 %collective-permute-start.5 = (f32[12,8,8,128]{3,2,1,0:T(8,128)S(1)}, f32[12,8,8,128]{3,2,1,0:T(8,128)S(1)}, u32[]{:S(2)}, u32[]{:S(2)}) collective-permute-start(f32[12,8,8,128]{3,2,1,0:T(8,128)S(1)} %get-tuple-element.58), channel_id=1, source_target_pairs={{0,4},{1,5},{2,6},{3,7},{4,8},{5,9},{6,10},{7,11},{8,12},{9,13},{1... | collective-permute-start | bytes 1179656 | tf_op jit(solution)/shard_map/ppermute | solution.py:399
  35.3 1.9 %collective-permute-done.10.m2 = f32[12,64,128]{2,1,0:T(8,128)S(1)} collective-permute-done((f32[12,64,128]{2,1,0:T(8,128)S(1)}, f32[12,64,128]{2,1,0:T(8,128)S(1)}, u32[]{:S(2)}, u32[]{:S(2)}) %collective-permute-start.10) | collective-permute-done | bytes 393248 | tf_op jit(solution)/shard_map/ppermute | solution.py:396
  45.1 5.9 %collective-permute-done.6.hi = f32[12,8,8,128]{3,2,1,0:T(8,128)S(1)} collective-permute-done((f32[12,8,8,128]{3,2,1,0:T(8,128)S(1)}, f32[12,8,8,128]{3,2,1,0:T(8,128)S(1)}, u32[]{:S(2)}, u32[]{:S(2)}) %collective-permute-start.6) | collective-permute-done | bytes 393248 | tf_op jit(solution)/shard_map/ppermute | solution.py:402
  50.9 12.3 %relax_first.1 = (f32[16,8,8,128]{3,2,1,0:T(8,128)S(1)}, f32[12,8,8,128]{3,2,1,0:T(8,128)S(1)}, f32[12,8,8,128]{3,2,1,0:T(8,128)S(1)}, f32[46,8,8,128]{3,2,1,0:T(8,128)}, f32[46,8,8,128]{3,2,1,0:T(8,128)}) custom-call(s32[2]{0:T(128)S(1)} %pad_add_fusion.where, f32[8]{0:T(128)S(1)} %dynamic_slice.28.amounts, f32[16,8,8,128]{3,2,1,0:T(8,128)S(1)} %get-tuple-element.57.field, ...), custom_call_target="tpu_custom_call" | custom-call | flops 12000000000 | bytes 36000000 | tf_op jit(solution)/shard_map/relax_first/pallas_call | solution.py:379
  63.2 3.5 %collective-permute-start.19 = (f32[12,8,8,128]{3,2,1,0:T(8,128)S(1)}, f32[12,8,8,128]{3,2,1,0:T(8,128)S(1)}, u32[]{:S(2)}, u32[]{:S(2)}) collective-permute-start(f32[12,8,8,128]{3,2,1,0:T(8,128)S(1)} %get-tuple-element.68), channel_id=1, source_target_pairs={{0,4},{1,5},{2,6},{3,7},{4,8},{5,9},{6,10},{7,11},{8,12},{9,13},{1... | collective-permute-start | bytes 1179656 | tf_op jit(solution)/shard_map/ppermute | solution.py:399
  68.0 4.5 %collective-permute-done.19.lo = f32[12,8,8,128]{3,2,1,0:T(8,128)S(1)} collective-permute-done((f32[12,8,8,128]{3,2,1,0:T(8,128)S(1)}, f32[12,8,8,128]{3,2,1,0:T(8,128)S(1)}, u32[]{:S(2)}, u32[]{:S(2)}) %collective-permute-start.19) | collective-permute-done | bytes 393248 | tf_op jit(solution)/shard_map/ppermute | solution.py:399
  72.5 4.1 %collective-permute-done.20.hi = f32[12,8,8,128]{3,2,1,0:T(8,128)S(1)} collective-permute-done((f32[12,8,8,128]{3,2,1,0:T(8,128)S(1)}, f32[12,8,8,128]{3,2,1,0:T(8,128)S(1)}, u32[]{:S(2)}, u32[]{:S(2)}) %collective-permute-start.20) | collective-permute-done | bytes 393248 | tf_op jit(solution)/shard_map/ppermute | solution.py:402
  78.1 9.3 %relax_second.1 = (f32[4,64,128]{2,1,0:T(8,128)S(1)}, f32[4,64,128]{2,1,0:T(8,128)S(1)}, f32[4,64,128]{2,1,0:T(8,128)S(1)}, f32[4,64,128]{2,1,0:T(8,128)S(1)}, f...) custom-call(s32[2]{0:T(128)S(1)} %pad_add_fusion.where, ...), custom_call_target="tpu_custom_call" | custom-call | flops 8999999488 | bytes 27000000 | tf_op jit(solution)/shard_map/relax_second/pallas_call | solution.py:379
  87.4 3.5 %collective-permute-start.21 = (f32[12,8,8,128]{3,2,1,0:T(8,128)S(1)}, f32[12,8,8,128]{3,2,1,0:T(8,128)S(1)}, u32[]{:S(2)}, u32[]{:S(2)}) collective-permute-start(f32[12,8,8,128]{3,2,1,0:T(8,128)S(1)} %get-tuple-element.81), channel_id=1, source_target_pairs={{0,4},{1,5},{2,6},{3,7},{4,8},{5,9},{6,10},{7,11},{8,12},{9,13},{1... | collective-permute-start | bytes 1179656 | tf_op jit(solution)/shard_map/ppermute | solution.py:399
  92.4 3.8 %collective-permute-done.21.lo = f32[12,8,8,128]{3,2,1,0:T(8,128)S(1)} collective-permute-done((f32[12,8,8,128]{3,2,1,0:T(8,128)S(1)}, f32[12,8,8,128]{3,2,1,0:T(8,128)S(1)}, u32[]{:S(2)}, u32[]{:S(2)}) %collective-permute-start.21) | collective-permute-done | bytes 393248 | tf_op jit(solution)/shard_map/ppermute | solution.py:399
  97.6 2.9 %collective-permute-start.24 = (f32[4,64,128]{2,1,0:T(8,128)S(1)}, f32[4,64,128]{2,1,0:T(8,128)S(1)}, u32[]{:S(2)}, u32[]{:S(2)}) collective-permute-start(f32[4,64,128]{2,1,0:T(8,128)S(1)} %get-tuple-element.87), channel_id=1, source_target_pairs={{0,2},{1,3},{2,0},{3,1},{4,6},{5,7},{6,4},{7,5},{8,10},{9,11},{10,... | collective-permute-start | bytes 393224 | tf_op jit(solution)/shard_map/ppermute | solution.py:396
  100.6 7.6 %again_first.1 = (f32[16,8,8,128]{3,2,1,0:T(8,128)S(1)}, f32[15,8,8,128]{3,2,1,0:T(8,128)S(1)}, f32[15,8,8,128]{3,2,1,0:T(8,128)S(1)}) custom-call(f32[16,8,8,128]{3,2,1,0:T(8,128)S(1)} %get-tuple-element.76.field, f32[12,8,8,128]{3,2,1,0:T(8,128)S(1)} %collective-permute-done.21.lo, f32[12,8,8,128]{3,2,1,0:T(8,128)S(1)} %collective-permute-done.22.hi, ...), custom_call_target="tpu_custom_call" | custom-call | flops 8000000000 | bytes 24000000 | tf_op jit(solution)/shard_map/again_first/pallas_call | solution.py:379
  108.4 4.4 %collective-permute-start.27 = (f32[15,8,8,128]{3,2,1,0:T(8,128)S(1)}, f32[15,8,8,128]{3,2,1,0:T(8,128)S(1)}, u32[]{:S(2)}, u32[]{:S(2)}) collective-permute-start(f32[15,8,8,128]{3,2,1,0:T(8,128)S(1)} %get-tuple-element.95), channel_id=1, source_target_pairs={{0,4},{1,5},{2,6},{3,7},{4,8},{5,9},{6,10},{7,11},{8,12},{9,13},{1... | collective-permute-start | bytes 1474568 | tf_op jit(solution)/shard_map/ppermute | solution.py:399
  114.1 9.8 %collective-permute-done.27.lo = f32[15,8,8,128]{3,2,1,0:T(8,128)S(1)} collective-permute-done((f32[15,8,8,128]{3,2,1,0:T(8,128)S(1)}, f32[15,8,8,128]{3,2,1,0:T(8,128)S(1)}, u32[]{:S(2)}, u32[]{:S(2)}) %collective-permute-start.27) | collective-permute-done | bytes 491552 | tf_op jit(solution)/shard_map/ppermute | solution.py:399
  123.9 4.1 %collective-permute-done.28.hi = f32[15,8,8,128]{3,2,1,0:T(8,128)S(1)} collective-permute-done((f32[15,8,8,128]{3,2,1,0:T(8,128)S(1)}, f32[15,8,8,128]{3,2,1,0:T(8,128)S(1)}, u32[]{:S(2)}, u32[]{:S(2)}) %collective-permute-start.28) | collective-permute-done | bytes 491552 | tf_op jit(solution)/shard_map/ppermute | solution.py:402
  128.0 9.8 %again_second.1 = (f32[22,8,8,128]{3,2,1,0:T(8,128)S(1)}, f32[4,64,128]{2,1,0:T(8,128)S(1)}, f32[4,64,128]{2,1,0:T(8,128)S(1)}, f32[4,64,128]{2,1,0:T(8,128)S(1)}, f32[4,64,128]{2,1,0:T(8,128)S(1)}) custom-call(s32[2]{0:T(128)S(1)} %pad_add_fusion.where, f32[16,8,8,128]{3,2,1,0:T(8,128)S(1)} %get-tuple-element.84.field, ...), custom_call_target="tpu_custom_call" | custom-call | flops 8999999488 | bytes 27000000 | tf_op jit(solution)/shard_map/again_second/pallas_call | solution.py:379
  137.9 2.2 %collective-permute-done.29.other = f32[22,8,8,128]{3,2,1,0:T(8,128)S(1)} collective-permute-done((f32[22,8,8,128]{3,2,1,0:T(8,128)S(1)}, f32[22,8,8,128]{3,2,1,0:T(8,128)S(1)}, u32[]{:S(2)}, u32[]{:S(2)}) %collective-permute-start.29) | collective-permute-done | bytes 720928 | tf_op jit(solution)/shard_map/ppermute | solution.py:393
  140.1 2.2 %pairs.1.own = f32[16,4,8,128]{3,2,1,0:T(8,128)S(1)} custom-call(s32[2]{0:T(128)S(1)} %pad_add_fusion.where, f32[22,8,8,128]{3,2,1,0:T(8,128)S(1)} %get-tuple-element.102.mine, f32[22,8,8,128]{3,2,1,0:T(8,128)S(1)} %collective-permute-done.29.other, f32[46,8,8,128]{3,2,1,0:T(8,128)S(1)} %copy-done.1), custom_call_target="tpu_custom_call" | custom-call | flops 3000000000 | bytes 9000000 | tf_op jit(solution)/shard_map/pairs/pallas_call | solution.py:379
  142.3 3.0 %collective-permute-start.32 = (f32[16,4,8,128]{3,2,1,0:T(8,128)S(1)}, f32[16,4,8,128]{3,2,1,0:T(8,128)S(1)}, u32[]{:S(2)}, u32[]{:S(2)}) collective-permute-start(f32[16,4,8,128]{3,2,1,0:T(8,128)S(1)} %pairs.1.own), channel_id=1, source_target_pairs={{0,3},{1,2},{2,1},{3,0},{4,7},{5,6},{6,5},{7,4},{8,11},{9,10},{10,... | collective-permute-start | bytes 786440 | tf_op jit(solution)/shard_map/ppermute | solution.py:396
  146.0 6.5 %collective-permute-done.32.r3 = f32[16,4,8,128]{3,2,1,0:T(8,128)S(1)} collective-permute-done((f32[16,4,8,128]{3,2,1,0:T(8,128)S(1)}, f32[16,4,8,128]{3,2,1,0:T(8,128)S(1)}, u32[]{:S(2)}, u32[]{:S(2)}) %collective-permute-start.32) | collective-permute-done | bytes 262176 | tf_op jit(solution)/shard_map/ppermute | solution.py:396
  152.5 5.1 %collective-permute-done.31.r2 = f32[16,4,8,128]{3,2,1,0:T(8,128)S(1)} collective-permute-done((f32[16,4,8,128]{3,2,1,0:T(8,128)S(1)}, f32[16,4,8,128]{3,2,1,0:T(8,128)S(1)}, u32[]{:S(2)}, u32[]{:S(2)}) %collective-permute-start.31) | collective-permute-done | bytes 262176 | tf_op jit(solution)/shard_map/ppermute | solution.py:396
  158.7 1.6 collective-permute-start.38
  160.2 2.5 %collective-permute-start.33 = (f32[27,4,8,128]{3,2,1,0:T(8,128)S(1)}, f32[27,4,8,128]{3,2,1,0:T(8,128)S(1)}, u32[]{:S(2)}, u32[]{:S(2)}) collective-permute-start(f32[27,4,8,128]{3,2,1,0:T(8,128)S(1)} %get-tuple-element.105), channel_id=1, source_target_pairs={{0,4},{1,5},{2,6},{3,7},{4,8},{5,9},{6,10},{7,11},{8,12},{9,13},{1... | collective-permute-start | bytes 1327112 | tf_op jit(solution)/shard_map/ppermute | solution.py:399
  166.4 6.7 %collective-permute-done.39.refs_7_ = f32[4,64,128]{2,1,0:T(8,128)S(1)} collective-permute-done((f32[4,64,128]{2,1,0:T(8,128)S(1)}, f32[4,64,128]{2,1,0:T(8,128)S(1)}, u32[]{:S(2)}, u32[]{:S(2)}) %collective-permute-start.39) | collective-permute-done | bytes 131104 | tf_op jit(solution)/shard_map/ppermute | solution.py:396
  173.6 1.9 collective-permute-done.34.got_hi
  175.7 1.6 collective-permute-done.37.other_hi
  177.3 10.4 %chain.1 = (f32[4,4,64,128]{3,2,1,0:T(8,128)}, f32[4,4,64,128]{3,2,1,0:T(8,128)}) custom-call(s32[2]{0:T(128)S(1)} %pad_add_fusion.where, f32[48,4,8,128]{3,2,1,0:T(8,128)S(1)} %get-tuple-element.104.sums, f32[27,4,8,128]{3,2,1,0:T(8,128)S(1)} %collective-permute-done.33.got_lo, f32[27,4,8,128]{3,2,1,0:T(8,128)S(1)} %collective-permute-done.34.got_hi, ...), custom_call_target="tpu_custom_call" | custom-call | flops 8999999488 | bytes 27000000 | tf_op jit(solution)/shard_map/chain/pallas_call | solution.py:379
  (84 shorter events, 31.4 us)
Async XLA Ops:
  0.6 7.9 %collective-permute-start.1 = (f32[4,4,64,128]{3,2,1,0:T(8,128)}, f32[4,4,64,128]{3,2,1,0:T(8,128)S(1)}, u32[]{:S(2)}, u32[]{:S(2)}) collective-permute-start(f32[4,4,64,128]{3,2,1,0:T(8,128)} %param.6), channel_id=1, source_target_pairs={{0,16},{16,0},{1,17},{17,1},{2,18},{18,2},{3,19},{19,3},{4,20},{20... | collective-permute-start | bytes 1572872 | tf_op jit(solution)/shard_map/ppermute | solution.py:393
  2.1 12.6 %collective-permute-start.8 = (f32[4,64,128]{2,1,0:T(8,128)S(1)}, f32[4,64,128]{2,1,0:T(8,128)S(1)}, u32[]{:S(2)}, u32[]{:S(2)}) collective-permute-start(f32[4,64,128]{2,1,0:T(8,128)S(1)} %broadcast_select_fusion.2), channel_id=1, source_target_pairs={{4,0},{5,1},{6,2},{7,3},{8,4},{9,5},{10,6},{11,7},{12,8},{13,9},{1... | collective-permute-start | bytes 393224 | tf_op jit(solution)/shard_map/ppermute | solution.py:402
  3.4 11.3 %collective-permute-start.7 = (f32[4,64,128]{2,1,0:T(8,128)S(1)}, f32[4,64,128]{2,1,0:T(8,128)S(1)}, u32[]{:S(2)}, u32[]{:S(2)}) collective-permute-start(f32[4,64,128]{2,1,0:T(8,128)S(1)} %broadcast_select_fusion.2), channel_id=1, source_target_pairs={{0,4},{1,5},{2,6},{3,7},{4,8},{5,9},{6,10},{7,11},{8,12},{9,13},{1... | collective-permute-start | bytes 393224 | tf_op jit(solution)/shard_map/ppermute | solution.py:399
  14.0 7.7 %collective-permute-start.2 = (f32[4,64,128]{2,1,0:T(8,128)S(1)}, f32[4,64,128]{2,1,0:T(8,128)S(1)}, u32[]{:S(2)}, u32[]{:S(2)}) collective-permute-start(f32[4,64,128]{2,1,0:T(8,128)S(1)} %get-tuple-element.118), channel_id=1, source_target_pairs={{0,1},{1,0},{2,3},{3,2},{4,5},{5,4},{6,7},{7,6},{8,9},{9,8},{10,11... | collective-permute-start | bytes 393224 | tf_op jit(solution)/shard_map/ppermute | solution.py:396
  14.5 14.9 %collective-permute-start.3 = (f32[4,64,128]{2,1,0:T(8,128)S(1)}, f32[4,64,128]{2,1,0:T(8,128)S(1)}, u32[]{:S(2)}, u32[]{:S(2)}) collective-permute-start(f32[4,64,128]{2,1,0:T(8,128)S(1)} %get-tuple-element.119), channel_id=1, source_target_pairs={{0,2},{1,3},{2,0},{3,1},{4,6},{5,7},{6,4},{7,5},{8,10},{9,11},{10,... | collective-permute-start | bytes 393224 | tf_op jit(solution)/shard_map/ppermute | solution.py:396
  14.7 20.3 %collective-permute-start.11 = (f32[12,64,128]{2,1,0:T(8,128)S(1)}, f32[12,64,128]{2,1,0:T(8,128)S(1)}, u32[]{:S(2)}, u32[]{:S(2)}) collective-permute-start(f32[12,64,128]{2,1,0:T(8,128)S(1)} %pad_maximum_fusion.2.m0), channel_id=1, source_target_pairs={{0,3},{1,2},{2,1},{3,0},{4,7},{5,6},{6,5},{7,4},{8,11},{9,10},{10,... | collective-permute-start | bytes 1179656 | tf_op jit(solution)/shard_map/ppermute | solution.py:396
  17.6 19.6 %collective-permute-start.10 = (f32[12,64,128]{2,1,0:T(8,128)S(1)}, f32[12,64,128]{2,1,0:T(8,128)S(1)}, u32[]{:S(2)}, u32[]{:S(2)}) collective-permute-start(f32[12,64,128]{2,1,0:T(8,128)S(1)} %pad_maximum_fusion.2.m0), channel_id=1, source_target_pairs={{0,2},{1,3},{2,0},{3,1},{4,6},{5,7},{6,4},{7,5},{8,10},{9,11},{10,... | collective-permute-start | bytes 1179656 | tf_op jit(solution)/shard_map/ppermute | solution.py:396
  18.3 19.2 %collective-permute-start.9 = (f32[12,64,128]{2,1,0:T(8,128)S(1)}, f32[12,64,128]{2,1,0:T(8,128)S(1)}, u32[]{:S(2)}, u32[]{:S(2)}) collective-permute-start(f32[12,64,128]{2,1,0:T(8,128)S(1)} %pad_maximum_fusion.2.m0), channel_id=1, source_target_pairs={{0,1},{1,0},{2,3},{3,2},{4,5},{5,4},{6,7},{7,6},{8,9},{9,8},{10,11... | collective-permute-start | bytes 1179656 | tf_op jit(solution)/shard_map/ppermute | solution.py:396
  30.1 8.8 %collective-permute-start.5 = (f32[12,8,8,128]{3,2,1,0:T(8,128)S(1)}, f32[12,8,8,128]{3,2,1,0:T(8,128)S(1)}, u32[]{:S(2)}, u32[]{:S(2)}) collective-permute-start(f32[12,8,8,128]{3,2,1,0:T(8,128)S(1)} %get-tuple-element.58), channel_id=1, source_target_pairs={{0,4},{1,5},{2,6},{3,7},{4,8},{5,9},{6,10},{7,11},{8,12},{9,13},{1... | collective-permute-start | bytes 1179656 | tf_op jit(solution)/shard_map/ppermute | solution.py:399
  35.0 8.1 %collective-permute-start.15 = (f32[12,64,128]{2,1,0:T(8,128)S(1)}, f32[12,64,128]{2,1,0:T(8,128)S(1)}, u32[]{:S(2)}, u32[]{:S(2)}) collective-permute-start(f32[12,64,128]{2,1,0:T(8,128)S(1)} %collective-permute-done.11.m3), channel_id=1, source_target_pairs={{0,16},{16,0},{1,17},{17,1},{2,18},{18,2},{3,19},{19,3},{4,20},{20... | collective-permute-start | bytes 1179656 | tf_op jit(solution)/shard_map/ppermute | solution.py:393
  38.8 12.1 %collective-permute-start.6 = (f32[12,8,8,128]{3,2,1,0:T(8,128)S(1)}, f32[12,8,8,128]{3,2,1,0:T(8,128)S(1)}, u32[]{:S(2)}, u32[]{:S(2)}) collective-permute-start(f32[12,8,8,128]{3,2,1,0:T(8,128)S(1)} %get-tuple-element.60), channel_id=1, source_target_pairs={{4,0},{5,1},{6,2},{7,3},{8,4},{9,5},{10,6},{11,7},{12,8},{13,9},{1... | collective-permute-start | bytes 1179656 | tf_op jit(solution)/shard_map/ppermute | solution.py:402
  41.5 21.7 %collective-permute-start.16 = (f32[4,64,128]{2,1,0:T(8,128)S(1)}, f32[4,64,128]{2,1,0:T(8,128)S(1)}, u32[]{:S(2)}, u32[]{:S(2)}) collective-permute-start(f32[4,64,128]{2,1,0:T(8,128)S(1)} %get-tuple-element.63), channel_id=1, source_target_pairs={{0,1},{1,0},{2,3},{3,2},{4,5},{5,4},{6,7},{7,6},{8,9},{9,8},{10,11... | collective-permute-start | bytes 393224 | tf_op jit(solution)/shard_map/ppermute | solution.py:396
  43.1 20.1 %collective-permute-start.17 = (f32[4,64,128]{2,1,0:T(8,128)S(1)}, f32[4,64,128]{2,1,0:T(8,128)S(1)}, u32[]{:S(2)}, u32[]{:S(2)}) collective-permute-start(f32[4,64,128]{2,1,0:T(8,128)S(1)} %get-tuple-element.64), channel_id=1, source_target_pairs={{0,2},{1,3},{2,0},{3,1},{4,6},{5,7},{6,4},{7,5},{8,10},{9,11},{10,... | collective-permute-start | bytes 393224 | tf_op jit(solution)/shard_map/ppermute | solution.py:396
  43.6 19.5 %collective-permute-start.18 = (f32[4,64,128]{2,1,0:T(8,128)S(1)}, f32[4,64,128]{2,1,0:T(8,128)S(1)}, u32[]{:S(2)}, u32[]{:S(2)}) collective-permute-start(f32[4,64,128]{2,1,0:T(8,128)S(1)} %get-tuple-element.65), channel_id=1, source_target_pairs={{0,3},{1,2},{2,1},{3,0},{4,7},{5,6},{6,5},{7,4},{8,11},{9,10},{10,... | collective-permute-start | bytes 393224 | tf_op jit(solution)/shard_map/ppermute | solution.py:396
  63.2 9.3 %collective-permute-start.19 = (f32[12,8,8,128]{3,2,1,0:T(8,128)S(1)}, f32[12,8,8,128]{3,2,1,0:T(8,128)S(1)}, u32[]{:S(2)}, u32[]{:S(2)}) collective-permute-start(f32[12,8,8,128]{3,2,1,0:T(8,128)S(1)} %get-tuple-element.68), channel_id=1, source_target_pairs={{0,4},{1,5},{2,6},{3,7},{4,8},{5,9},{6,10},{7,11},{8,12},{9,13},{1... | collective-permute-start | bytes 1179656 | tf_op jit(solution)/shard_map/ppermute | solution.py:399
  66.7 10.0 %collective-permute-start.20 = (f32[12,8,8,128]{3,2,1,0:T(8,128)S(1)}, f32[12,8,8,128]{3,2,1,0:T(8,128)S(1)}, u32[]{:S(2)}, u32[]{:S(2)}) collective-permute-start(f32[12,8,8,128]{3,2,1,0:T(8,128)S(1)} %get-tuple-element.69), channel_id=1, source_target_pairs={{4,0},{5,1},{6,2},{7,3},{8,4},{9,5},{10,6},{11,7},{12,8},{13,9},{1... | collective-permute-start | bytes 1179656 | tf_op jit(solution)/shard_map/ppermute | solution.py:402
  87.4 8.7 %collective-permute-start.21 = (f32[12,8,8,128]{3,2,1,0:T(8,128)S(1)}, f32[12,8,8,128]{3,2,1,0:T(8,128)S(1)}, u32[]{:S(2)}, u32[]{:S(2)}) collective-permute-start(f32[12,8,8,128]{3,2,1,0:T(8,128)S(1)} %get-tuple-element.81), channel_id=1, source_target_pairs={{0,4},{1,5},{2,6},{3,7},{4,8},{5,9},{6,10},{7,11},{8,12},{9,13},{1... | collective-permute-start | bytes 1179656 | tf_op jit(solution)/shard_map/ppermute | solution.py:399
  90.9 9.7 %collective-permute-start.22 = (f32[12,8,8,128]{3,2,1,0:T(8,128)S(1)}, f32[12,8,8,128]{3,2,1,0:T(8,128)S(1)}, u32[]{:S(2)}, u32[]{:S(2)}) collective-permute-start(f32[12,8,8,128]{3,2,1,0:T(8,128)S(1)} %get-tuple-element.83), channel_id=1, source_target_pairs={{4,0},{5,1},{6,2},{7,3},{8,4},{9,5},{10,6},{11,7},{12,8},{13,9},{1... | collective-permute-start | bytes 1179656 | tf_op jit(solution)/shard_map/ppermute | solution.py:402
  96.1 12.1 %collective-permute-start.23 = (f32[4,64,128]{2,1,0:T(8,128)S(1)}, f32[4,64,128]{2,1,0:T(8,128)S(1)}, u32[]{:S(2)}, u32[]{:S(2)}) collective-permute-start(f32[4,64,128]{2,1,0:T(8,128)S(1)} %get-tuple-element.86), channel_id=1, source_target_pairs={{0,1},{1,0},{2,3},{3,2},{4,5},{5,4},{6,7},{7,6},{8,9},{9,8},{10,11... | collective-permute-start | bytes 393224 | tf_op jit(solution)/shard_map/ppermute | solution.py:396
  97.6 10.6 %collective-permute-start.24 = (f32[4,64,128]{2,1,0:T(8,128)S(1)}, f32[4,64,128]{2,1,0:T(8,128)S(1)}, u32[]{:S(2)}, u32[]{:S(2)}) collective-permute-start(f32[4,64,128]{2,1,0:T(8,128)S(1)} %get-tuple-element.87), channel_id=1, source_target_pairs={{0,2},{1,3},{2,0},{3,1},{4,6},{5,7},{6,4},{7,5},{8,10},{9,11},{10,... | collective-permute-start | bytes 393224 | tf_op jit(solution)/shard_map/ppermute | solution.py:396
  100.6 7.7 %collective-permute-start.25 = (f32[4,64,128]{2,1,0:T(8,128)S(1)}, f32[4,64,128]{2,1,0:T(8,128)S(1)}, u32[]{:S(2)}, u32[]{:S(2)}) collective-permute-start(f32[4,64,128]{2,1,0:T(8,128)S(1)} %get-tuple-element.88), channel_id=1, source_target_pairs={{0,3},{1,2},{2,1},{3,0},{4,7},{5,6},{6,5},{7,4},{8,11},{9,10},{10,... | collective-permute-start | bytes 393224 | tf_op jit(solution)/shard_map/ppermute | solution.py:396
  108.3 15.6 %collective-permute-start.26 = (f32[16,64,128]{2,1,0:T(8,128)S(1)}, f32[16,64,128]{2,1,0:T(8,128)S(1)}, u32[]{:S(2)}, u32[]{:S(2)}) collective-permute-start(f32[16,64,128]{2,1,0:T(8,128)S(1)} %pad_maximum_fusion), channel_id=1, source_target_pairs={{0,16},{16,0},{1,17},{17,1},{2,18},{18,2},{3,19},{19,3},{4,20},{20... | collective-permute-start | bytes 1572872 | tf_op jit(solution)/shard_map/ppermute | solution.py:393
  108.4 15.5 %collective-permute-start.27 = (f32[15,8,8,128]{3,2,1,0:T(8,128)S(1)}, f32[15,8,8,128]{3,2,1,0:T(8,128)S(1)}, u32[]{:S(2)}, u32[]{:S(2)}) collective-permute-start(f32[15,8,8,128]{3,2,1,0:T(8,128)S(1)} %get-tuple-element.95), channel_id=1, source_target_pairs={{0,4},{1,5},{2,6},{3,7},{4,8},{5,9},{6,10},{7,11},{8,12},{9,13},{1... | collective-permute-start | bytes 1474568 | tf_op jit(solution)/shard_map/ppermute | solution.py:399
  112.8 15.2 %collective-permute-start.28 = (f32[15,8,8,128]{3,2,1,0:T(8,128)S(1)}, f32[15,8,8,128]{3,2,1,0:T(8,128)S(1)}, u32[]{:S(2)}, u32[]{:S(2)}) collective-permute-start(f32[15,8,8,128]{3,2,1,0:T(8,128)S(1)} %get-tuple-element.97), channel_id=1, source_target_pairs={{4,0},{5,1},{6,2},{7,3},{8,4},{9,5},{10,6},{11,7},{12,8},{13,9},{1... | collective-permute-start | bytes 1474568 | tf_op jit(solution)/shard_map/ppermute | solution.py:402
  142.3 10.1 %collective-permute-start.32 = (f32[16,4,8,128]{3,2,1,0:T(8,128)S(1)}, f32[16,4,8,128]{3,2,1,0:T(8,128)S(1)}, u32[]{:S(2)}, u32[]{:S(2)}) collective-permute-start(f32[16,4,8,128]{3,2,1,0:T(8,128)S(1)} %pairs.1.own), channel_id=1, source_target_pairs={{0,3},{1,2},{2,1},{3,0},{4,7},{5,6},{6,5},{7,4},{8,11},{9,10},{10,... | collective-permute-start | bytes 786440 | tf_op jit(solution)/shard_map/ppermute | solution.py:396
  145.3 12.2 %collective-permute-start.31 = (f32[16,4,8,128]{3,2,1,0:T(8,128)S(1)}, f32[16,4,8,128]{3,2,1,0:T(8,128)S(1)}, u32[]{:S(2)}, u32[]{:S(2)}) collective-permute-start(f32[16,4,8,128]{3,2,1,0:T(8,128)S(1)} %pairs.1.own), channel_id=1, source_target_pairs={{0,2},{1,3},{2,0},{3,1},{4,6},{5,7},{6,4},{7,5},{8,10},{9,11},{10,... | collective-permute-start | bytes 786440 | tf_op jit(solution)/shard_map/ppermute | solution.py:396
  145.3 12.5 %collective-permute-start.30 = (f32[16,4,8,128]{3,2,1,0:T(8,128)S(1)}, f32[16,4,8,128]{3,2,1,0:T(8,128)S(1)}, u32[]{:S(2)}, u32[]{:S(2)}) collective-permute-start(f32[16,4,8,128]{3,2,1,0:T(8,128)S(1)} %pairs.1.own), channel_id=1, source_target_pairs={{0,1},{1,0},{2,3},{3,2},{4,5},{5,4},{6,7},{7,6},{8,9},{9,8},{10,11... | collective-permute-start | bytes 786440 | tf_op jit(solution)/shard_map/ppermute | solution.py:396
  160.2 12.9 %collective-permute-start.33 = (f32[27,4,8,128]{3,2,1,0:T(8,128)S(1)}, f32[27,4,8,128]{3,2,1,0:T(8,128)S(1)}, u32[]{:S(2)}, u32[]{:S(2)}) collective-permute-start(f32[27,4,8,128]{3,2,1,0:T(8,128)S(1)} %get-tuple-element.105), channel_id=1, source_target_pairs={{0,4},{1,5},{2,6},{3,7},{4,8},{5,9},{6,10},{7,11},{8,12},{9,13},{1... | collective-permute-start | bytes 1327112 | tf_op jit(solution)/shard_map/ppermute | solution.py:399
  162.7 12.8 %collective-permute-start.34 = (f32[27,4,8,128]{3,2,1,0:T(8,128)S(1)}, f32[27,4,8,128]{3,2,1,0:T(8,128)S(1)}, u32[]{:S(2)}, u32[]{:S(2)}) collective-permute-start(f32[27,4,8,128]{3,2,1,0:T(8,128)S(1)} %get-tuple-element.106), channel_id=1, source_target_pairs={{4,0},{5,1},{6,2},{7,3},{8,4},{9,5},{10,6},{11,7},{12,8},{13,9},{1... | collective-permute-start | bytes 1327112 | tf_op jit(solution)/shard_map/ppermute | solution.py:402
  164.2 11.3 %collective-permute-start.35 = (f32[48,4,8,128]{3,2,1,0:T(8,128)S(1)}, f32[48,4,8,128]{3,2,1,0:T(8,128)S(1)}, u32[]{:S(2)}, u32[]{:S(2)}) collective-permute-start(f32[48,4,8,128]{3,2,1,0:T(8,128)S(1)} %get-tuple-element.104.sums), channel_id=1, source_target_pairs={{0,16},{16,0},{1,17},{17,1},{2,18},{18,2},{3,19},{19,3},{4,20},{20... | collective-permute-start | bytes 2359304 | tf_op jit(solution)/shard_map/ppermute | solution.py:393
  164.3 8.7 %collective-permute-start.39 = (f32[4,64,128]{2,1,0:T(8,128)S(1)}, f32[4,64,128]{2,1,0:T(8,128)S(1)}, u32[]{:S(2)}, u32[]{:S(2)}) collective-permute-start(f32[4,64,128]{2,1,0:T(8,128)S(1)} %get-tuple-element.110), channel_id=1, source_target_pairs={{0,2},{1,3},{2,0},{3,1},{4,6},{5,7},{6,4},{7,5},{8,10},{9,11},{10,... | collective-permute-start | bytes 393224 | tf_op jit(solution)/shard_map/ppermute | solution.py:396
  165.0 8.1 %collective-permute-start.40 = (f32[4,64,128]{2,1,0:T(8,128)S(1)}, f32[4,64,128]{2,1,0:T(8,128)S(1)}, u32[]{:S(2)}, u32[]{:S(2)}) collective-permute-start(f32[4,64,128]{2,1,0:T(8,128)S(1)} %get-tuple-element.111), channel_id=1, source_target_pairs={{0,3},{1,2},{2,1},{3,0},{4,7},{5,6},{6,5},{7,4},{8,11},{9,10},{10,... | collective-permute-start | bytes 393224 | tf_op jit(solution)/shard_map/ppermute | solution.py:396
  (16 other events, 76.1 us)

commit v3 on v2

--- a/solution.py
+++ b/solution.py
@@ -12,7 +12,8 @@
 SWEEPS = 3
 KAPPA_TOP = 3.0
 SUB = 8
-PLANES = 16
+PLANES = 40
+MATRIX = 3
 VMEM = pltpu.CompilerParams(vmem_limit_bytes=48 * 2**20)
 
 
@@ -79,6 +80,20 @@
     return lane == 0, lane == width - 1, sub == 0, sub == SUB - 1
 
 
+def lane_sums(parts, width):
+    far = lax.broadcasted_iota(jnp.int32, (width, width), 0) - lax.broadcasted_iota(jnp.int32, (width, width), 1)
+    ones = jnp.where(jnp.abs(far) == 1, 1.0, 0.0).astype(jnp.bfloat16)
+    whole = jnp.concatenate(parts, axis=0)
+    high = whole.astype(jnp.bfloat16)
+    rest = whole - high.astype(jnp.float32)
+    mid = rest.astype(jnp.bfloat16)
+    low = (rest - mid.astype(jnp.float32)).astype(jnp.bfloat16)
+    total = jnp.dot(
+        jnp.concatenate([high, mid], axis=1), jnp.concatenate([ones, ones], axis=0), preferred_element_type=jnp.float32
+    ) + jnp.dot(low, ones, preferred_element_type=jnp.float32)
+    return [total[i * SUB : (i + 1) * SUB] for i in range(len(parts))]
+
+
 def sweep(lo, hi, read, emit, J, width):
     first, last, top, bottom = masks(width)
     n = hi - lo
@@ -87,21 +102,29 @@
 
     def chunk(i, c):
         z0 = jnp.minimum(lo + i * size, hi - size)
-        for u in range(size):
+        planes = [[read(z0 + u, j) for j in range(J)] for u in range(size)]
+        by_matrix = MATRIX if size >= 8 else 0
+        if by_matrix:
+            sums = lane_sums([w[j] for w in planes for j in range(J - by_matrix, J)], width)
+        for u, w in enumerate(planes):
             z = z0 + u
-            w = [read(z, j) for j in range(J)]
             after = jnp.where(bottom, 0.0, pltpu.roll(w[0], SUB - 1, 0))
             before = jnp.where(top, 0.0, pltpu.roll(w[J - 1], 1, 0))
             for j in range(J):
                 yp = w[j + 1] if j < J - 1 else after
                 ym = w[j - 1] if j > 0 else before
-                xm = jnp.where(first, 0.0, pltpu.roll(w[j], 1, 1))
-                xp = jnp.where(last, 0.0, pltpu.roll(w[j], width - 1, 1))
-                beside = (read(z - 1, j) + read(z + 1, j)) + (yp + ym) + (xm + xp)
+                if j >= J - by_matrix:
+                    xs = sums[u * by_matrix + j - (J - by_matrix)]
+                else:
+                    xs = jnp.where(first, 0.0, pltpu.roll(w[j], 1, 1)) + jnp.where(last, 0.0, pltpu.roll(w[j], width - 1, 1))
+                beside = (read(z - 1, j) + read(z + 1, j)) + (yp + ym) + xs
                 emit(z, j, w[j], beside)
         return c
 
-    lax.fori_loop(0, steps, chunk, 0)
+    if steps == 1:
+        chunk(0, 0)
+    else:
+        lax.fori_loop(0, steps, chunk, 0)
 
 
 def factor(dst, src, cond, coef, lo, hi, s0=0, k0=0, extra=None):
@@ -141,16 +164,10 @@
     copy_planes(halo, field_dn, field, 0, 0)
 
 
-def first_kernel(
-    where, amounts, field, lo, hi, m0, m1, m2, m3, o0, o1, o2, o3,
-    out, up, dn, cond, force, a, b, raw, *, wide, each,
-):
+def coefficient_kernel(where, m0, m1, m2, m3, o0, o1, o2, o3, cond, force, raw, *, wide, halo, each):
     q, core = where[0], where[1]
-    J, width = a.shape[1], a.shape[3]
-    slab, halo = field.shape[0], lo.shape[0]
-    total = slab + 2 * halo
-    span = slab + 2 * wide
-    load_state(a, lo, field, hi)
+    span, J, width = cond.shape[0], cond.shape[1], cond.shape[3]
+    slab = span - 2 * wide
     skip = slab - wide
     for i, pieces in enumerate(zip((m0, m1, m2, m3), (o0, o1, o2, o3))):
         base = lax.bitwise_xor(q, i) * each
@@ -171,7 +188,11 @@
     sweep(margin - 1, span - margin + 1, lambda z, j: raw[1, z + skip, j], inner, J, width)
     sweep(margin, span - margin, lambda z, j: raw[0, z + skip, j], outer, J, width)
 
-    state = fine_steps(a, b, cond, wide - halo, total, halo, amounts, 0, force)
+
+def first_kernel(amounts, field, lo, hi, cond, force, out, up, dn, a, b, *, wide):
+    slab, halo = field.shape[0], lo.shape[0]
+    load_state(a, lo, field, hi)
+    state = fine_steps(a, b, cond, wide - halo, slab + 2 * halo, halo, amounts, 0, force)
     copy_planes(slab, out, state, 0, halo)
     copy_planes(halo, up, state, 0, halo + slab - halo)
     copy_planes(halo, dn, state, 0, halo)
@@ -185,20 +206,20 @@
 
 
 def second_kernel(
-    where, amounts, field, lo, hi, cond, force, n0, n1, n2, n3,
+    where, amounts, field, lo, hi, cond, force, after,
     p0, p1, p2, p3, out, up, dn, a, b, *, wide, each, step,
 ):
     q = where[0]
     halo, slab, J = lo.shape[0], field.shape[0], a.shape[1]
     load_state(a, lo, field, hi)
     state = fine_steps(a, b, cond, wide - halo, slab + 2 * halo, halo, amounts, step, force)
-    for i, (piece, after) in enumerate(((p0, n0), (p1, n1), (p2, n2), (p3, n3))):
+    for i, piece in enumerate((p0, p1, p2, p3)):
         base = lax.bitwise_xor(q, i) * each
         for z in range(each):
             for j in range(J):
                 value = state[halo + base + z, j]
                 put_rows(piece, z, j, J, value)
-                out[base + z, j] = value - rows(after, z, j, J)
+                out[base + z, j] = value - after[base + z, j]
     copy_planes(halo, up, out, 0, slab - halo)
     copy_planes(halo, dn, out, 0, 0)
 
@@ -417,34 +438,36 @@
     def entry_for(j):
         return lax.dynamic_index_in_dim(entries, 2 * (q ^ j) + core, 0, False)
 
-    def after_for(j):
-        return lax.dynamic_index_in_dim(guesses, 2 * (q ^ j) + core, 0, False)
-
     def gathered(pieces):
         return [pieces[0]] + [across(pieces[j], j) for j in range(1, slots)]
 
+    *entry, coef = lax.optimization_barrier((*gathered([entry_for(j) for j in range(slots)]), coef))
     field, send_up, send_dn = call(
         partial(place_kernel, each=each),
-        [where], gathered([entry_for(j) for j in range(slots)]),
+        [where], entry,
         [blocked(slab), blocked(halo), blocked(halo)], [], "place", 1,
     )
     mine = gathered([coef] * slots)
     lo, hi = up(send_up), down(send_dn)
     span, total = slab + 2 * wide, slab + 2 * halo
     others = [swap(m) for m in mine]
-    after = [after_for(j) for j in range(slots)]
-    *after, lo = lax.optimization_barrier((*after, lo))
-    after = gathered(after)
-    state, send_up, send_dn, cond, force = call(
-        partial(first_kernel, wide=wide, each=each),
-        [where, amounts], [field, lo, hi, *mine, *others],
-        [blocked(slab), blocked(halo), blocked(halo), blocked(span), blocked(span)],
-        [scratch(total), scratch(total), scratch(2, 3 * slab)], "relax_first", 12,
-    )
-    *after, send_up, send_dn = lax.optimization_barrier((*after, send_up, send_dn))
+    cond, force = call(
+        partial(coefficient_kernel, wide=wide, halo=halo, each=each),
+        [where], [*mine, *others], [blocked(span), blocked(span)], [scratch(2, 3 * slab)], "coefficients", 4,
+    )
+    field_sent, lo = lax.optimization_barrier((field, lo))
+    pairs = [(count + s, s) for s in range(count)] + [(s, count + s - 1) for s in range(count) if s % slots]
+    after = lax.ppermute(field_sent, ("tm", "space"), pairs)
+    state, send_up, send_dn = call(
+        partial(first_kernel, wide=wide),
+        [amounts], [field, lo, hi, cond, force],
+        [blocked(slab), blocked(halo), blocked(halo)],
+        [scratch(total), scratch(total)], "relax_first", 8,
+    )
+    after, send_up, send_dn = lax.optimization_barrier((after, send_up, send_dn))
     *rel, state, send_up, send_dn = call(
         partial(second_kernel, wide=wide, each=each, step=halo // SWEEPS),
-        [where, amounts], [state, up(send_up), down(send_dn), cond, force, *after],
+        [where, amounts], [state, up(send_up), down(send_dn), cond, force, after],
         [natural(each)] * 4 + [blocked(slab), blocked(halo), blocked(halo)],
         [scratch(total), scratch(total)], "relax_second", 9,
     )

time: 188 us -> 178 us (0.947)
  Pallas kernels: 53.2 us -> 43.5 us
  waiting for transfers between devices: 70.3 us -> 78.8 us
  starting transfers between devices: 57 us -> 51.1 us
  local copies, waits for them, and re-layouts: 2.45 us -> 0.14 us
    pallas_call x8 -> x9, Pallas kernels: 53.2 us -> 43.5 us  [call(): pl.pallas_call(kernel, out_shape=outs, in_specs=[smem] * len(scalars) + [...]
    ppermute x18 -> x15, starting transfers between devices: 24.2 us -> 17.7 us  [across(): lax.ppermute(value, 'space', [(s, s - s % slots + (s % slots ^ j)) for s...]
    ppermute x18 -> x15, waiting for transfers between devices: 30 us -> 34.5 us  [across(): lax.ppermute(value, 'space', [(s, s - s % slots + (s % slots ^ j)) for s...]
    unnamed x12 -> x8, local copies, waits for them, and re-layouts: 2.38 us -> 0.02 us
    ppermute x6, waiting for transfers between devices: 16 us -> 18.1 us  [down(): lax.ppermute(value, 'space', [(s + slots, s) for s in range(count - slots)])]
    ppermute x6, waiting for transfers between devices: 19.2 us -> 21.1 us  [up(): lax.ppermute(value, 'space', [(s, s + slots) for s in range(count - slots)])]
  transfers between devices with their start and end apart: 42 -> 40, of which waited for: 21 -> 20; matrix products, arithmetic and copies ran while one was open for 2% -> 1% of each run, Pallas kernels for 11% -> 10%
where the time goes in v3:
time: 178 us; the launch traced here: 177 us
  waiting for transfers between devices  78.8 us (44%)
  starting transfers between devices  51.1 us (29%)
  Pallas kernels  43.5 us (24%)
  other arithmetic  2.42 us (1%)
    pallas_call x9, Pallas kernels, call(): pl.pallas_call(kernel, out_shape=outs, in_specs=[smem] * len(scalars) + [...  43.5 us
    ppermute x15, waiting for transfers between devices, across(): lax.ppermute(value, 'space', [(s, s - s % slots + (s % slots ^ j)) for s...  34.5 us
    ppermute x6, starting transfers between devices, up(): lax.ppermute(value, 'space', [(s, s + slots) for s in range(count - slots)])  21.9 us
    ppermute x6, waiting for transfers between devices, up(): lax.ppermute(value, 'space', [(s, s + slots) for s in range(count - slots)])  21.1 us
    ppermute x6, waiting for transfers between devices, down(): lax.ppermute(value, 'space', [(s + slots, s) for s in range(count - slots)])  18.1 us
    ppermute x15, starting transfers between devices, across(): lax.ppermute(value, 'space', [(s, s - s % slots + (s % slots ^ j)) for s...  17.7 us
    ppermute x6, starting transfers between devices, down(): lax.ppermute(value, 'space', [(s + slots, s) for s in range(count - slots)])  8.4 us
    ppermute x12, waiting for transfers between devices, swap(): return lax.ppermute(value, 'tm', [(0, 1), (1, 0)])  5.08 us
  transfers between devices with their start and end apart: 40, of which 20 were waited for; matrix products, arithmetic and copies ran while one was open for 1% of the time, Pallas kernels for 10%

profile of v3, /device:TPU:0, one launch (start us, length us, event | category | flops | bytes accessed | tf_op | source)
XLA Modules:
  0.0 177.1 jit_solution(13676954685220570992)
XLA Ops:
  3.4 5.1 %collective-permute-start.5 = (f32[4,64,128]{2,1,0:T(8,128)S(1)}, f32[4,64,128]{2,1,0:T(8,128)S(1)}, u32[]{:S(2)}, u32[]{:S(2)}) collective-permute-start(f32[4,64,128]{2,1,0:T(8,128)S(1)} %broadcast_select_fusion.2), channel_id=1, source_target_pairs={{0,4},{1,5},{2,6},{3,7},{4,8},{5,9},{6,10},{7,11},{8,12},{9,13},{1... | collective-permute-start | bytes 393224 | tf_op jit(solution)/shard_map/ppermute | solution.py:420
  9.9 2.9 %collective-permute-start.4 = (f32[4,64,128]{2,1,0:T(8,128)S(1)}, f32[4,64,128]{2,1,0:T(8,128)S(1)}, u32[]{:S(2)}, u32[]{:S(2)}) collective-permute-start(f32[4,64,128]{2,1,0:T(8,128)S(1)} %get-tuple-element.110), channel_id=1, source_target_pairs={{0,3},{1,2},{2,1},{3,0},{4,7},{5,6},{6,5},{7,4},{8,11},{9,10},{10,... | collective-permute-start | bytes 393224 | tf_op jit(solution)/shard_map/ppermute | solution.py:417
  13.5 3.2 %collective-permute-done.4.r3 = f32[4,64,128]{2,1,0:T(8,128)S(1)} collective-permute-done((f32[4,64,128]{2,1,0:T(8,128)S(1)}, f32[4,64,128]{2,1,0:T(8,128)S(1)}, u32[]{:S(2)}, u32[]{:S(2)}) %collective-permute-start.4) | collective-permute-done | bytes 131104 | tf_op jit(solution)/shard_map/ppermute | solution.py:417
  16.7 2.5 %collective-permute-done.3.r2 = f32[4,64,128]{2,1,0:T(8,128)S(1)} collective-permute-done((f32[4,64,128]{2,1,0:T(8,128)S(1)}, f32[4,64,128]{2,1,0:T(8,128)S(1)}, u32[]{:S(2)}, u32[]{:S(2)}) %collective-permute-start.3) | collective-permute-done | bytes 131104 | tf_op jit(solution)/shard_map/ppermute | solution.py:417
  24.5 3.5 %collective-permute-start.7 = (f32[12,8,8,128]{3,2,1,0:T(8,128)}, f32[12,8,8,128]{3,2,1,0:T(8,128)S(1)}, u32[]{:S(2)}, u32[]{:S(2)}) collective-permute-start(f32[12,8,8,128]{3,2,1,0:T(8,128)} %get-tuple-element.61), channel_id=1, source_target_pairs={{0,4},{1,5},{2,6},{3,7},{4,8},{5,9},{6,10},{7,11},{8,12},{9,13},{1... | collective-permute-start | bytes 1179656 | tf_op jit(solution)/shard_map/ppermute | solution.py:420
  29.4 3.0 %collective-permute-done.11.m3 = f32[12,64,128]{2,1,0:T(8,128)S(1)} collective-permute-done((f32[12,64,128]{2,1,0:T(8,128)S(1)}, f32[12,64,128]{2,1,0:T(8,128)S(1)}, u32[]{:S(2)}, u32[]{:S(2)}) %collective-permute-start.11) | collective-permute-done | bytes 393248 | tf_op jit(solution)/shard_map/ppermute | solution.py:417
  32.4 7.2 %collective-permute-done.10.m2 = f32[12,64,128]{2,1,0:T(8,128)S(1)} collective-permute-done((f32[12,64,128]{2,1,0:T(8,128)S(1)}, f32[12,64,128]{2,1,0:T(8,128)S(1)}, u32[]{:S(2)}, u32[]{:S(2)}) %collective-permute-start.10) | collective-permute-done | bytes 393248 | tf_op jit(solution)/shard_map/ppermute | solution.py:417
  42.9 3.3 %coefficients.1 = (f32[46,8,8,128]{3,2,1,0:T(8,128)S(1)}, f32[46,8,8,128]{3,2,1,0:T(8,128)S(1)}) custom-call(s32[2]{0:T(128)S(1)} %pad_add_fusion.where, f32[12,64,128]{2,1,0:T(8,128)S(1)} %pad_maximum_fusion.3.m0, f32[12,64,128]{2,1,0:T(8,128)S(1)} %collective-permute-done.9.m1, f32[12,64,128]{2,1,0:T(8,128)S(1)} %collective-permute-done.10.m2, ...), custom_call_target="tpu_custom_call" | custom-call | flops 4000000000 | bytes 12000000 | tf_op jit(solution)/shard_map/coefficients/pallas_call | solution.py:400
  46.3 7.0 %collective-permute-done.8.hi = f32[12,8,8,128]{3,2,1,0:T(8,128)S(1)} collective-permute-done((f32[12,8,8,128]{3,2,1,0:T(8,128)S(1)}, f32[12,8,8,128]{3,2,1,0:T(8,128)S(1)}, u32[]{:S(2)}, u32[]{:S(2)}) %collective-permute-start.8) | collective-permute-done | bytes 393248 | tf_op jit(solution)/shard_map/ppermute | solution.py:423
  53.3 6.5 %relax_first.1 = (f32[16,8,8,128]{3,2,1,0:T(8,128)S(1)}, f32[12,8,8,128]{3,2,1,0:T(8,128)S(1)}, f32[12,8,8,128]{3,2,1,0:T(8,128)S(1)}) custom-call(f32[8]{0:T(128)S(1)} %dynamic_slice.16.amounts, f32[16,8,8,128]{3,2,1,0:T(8,128)S(1)} %get-tuple-element.68.field, f32[12,8,8,128]{3,2,1,0:T(8,128)S(1)} %collective-permute-done.7.lo, ...), custom_call_target="tpu_custom_call" | custom-call | flops 8000000000 | bytes 24000000 | tf_op jit(solution)/shard_map/relax_first/pallas_call | solution.py:400
  59.9 3.5 %collective-permute-start.17 = (f32[12,8,8,128]{3,2,1,0:T(8,128)S(1)}, f32[12,8,8,128]{3,2,1,0:T(8,128)S(1)}, u32[]{:S(2)}, u32[]{:S(2)}) collective-permute-start(f32[12,8,8,128]{3,2,1,0:T(8,128)S(1)} %get-tuple-element.71), channel_id=1, source_target_pairs={{0,4},{1,5},{2,6},{3,7},{4,8},{5,9},{6,10},{7,11},{8,12},{9,13},{1... | collective-permute-start | bytes 1179656 | tf_op jit(solution)/shard_map/ppermute | solution.py:420
  64.9 6.3 %collective-permute-done.17.lo = f32[12,8,8,128]{3,2,1,0:T(8,128)S(1)} collective-permute-done((f32[12,8,8,128]{3,2,1,0:T(8,128)S(1)}, f32[12,8,8,128]{3,2,1,0:T(8,128)S(1)}, u32[]{:S(2)}, u32[]{:S(2)}) %collective-permute-start.17) | collective-permute-done | bytes 393248 | tf_op jit(solution)/shard_map/ppermute | solution.py:420
  71.2 4.1 %collective-permute-done.18.hi = f32[12,8,8,128]{3,2,1,0:T(8,128)S(1)} collective-permute-done((f32[12,8,8,128]{3,2,1,0:T(8,128)S(1)}, f32[12,8,8,128]{3,2,1,0:T(8,128)S(1)}, u32[]{:S(2)}, u32[]{:S(2)}) %collective-permute-start.18) | collective-permute-done | bytes 393248 | tf_op jit(solution)/shard_map/ppermute | solution.py:423
  75.3 7.3 %relax_second.1 = (f32[4,64,128]{2,1,0:T(8,128)S(1)}, f32[4,64,128]{2,1,0:T(8,128)S(1)}, f32[4,64,128]{2,1,0:T(8,128)S(1)}, f32[4,64,128]{2,1,0:T(8,128)S(1)}, f...) custom-call(s32[2]{0:T(128)S(1)} %pad_add_fusion.where, ...), custom_call_target="tpu_custom_call" | custom-call | flops 8999999488 | bytes 27000000 | tf_op jit(solution)/shard_map/relax_second/pallas_call | solution.py:400
  82.6 3.5 %collective-permute-start.19 = (f32[12,8,8,128]{3,2,1,0:T(8,128)S(1)}, f32[12,8,8,128]{3,2,1,0:T(8,128)S(1)}, u32[]{:S(2)}, u32[]{:S(2)}) collective-permute-start(f32[12,8,8,128]{3,2,1,0:T(8,128)S(1)} %get-tuple-element.79), channel_id=1, source_target_pairs={{0,4},{1,5},{2,6},{3,7},{4,8},{5,9},{6,10},{7,11},{8,12},{9,13},{1... | collective-permute-start | bytes 1179656 | tf_op jit(solution)/shard_map/ppermute | solution.py:420
  87.4 5.3 %collective-permute-done.19.lo = f32[12,8,8,128]{3,2,1,0:T(8,128)S(1)} collective-permute-done((f32[12,8,8,128]{3,2,1,0:T(8,128)S(1)}, f32[12,8,8,128]{3,2,1,0:T(8,128)S(1)}, u32[]{:S(2)}, u32[]{:S(2)}) %collective-permute-start.19) | collective-permute-done | bytes 393248 | tf_op jit(solution)/shard_map/ppermute | solution.py:420
  93.9 1.7 collective-permute-start.22
  96.8 5.7 %again_first.1 = (f32[16,8,8,128]{3,2,1,0:T(8,128)S(1)}, f32[15,8,8,128]{3,2,1,0:T(8,128)S(1)}, f32[15,8,8,128]{3,2,1,0:T(8,128)S(1)}) custom-call(f32[16,8,8,128]{3,2,1,0:T(8,128)S(1)} %get-tuple-element.74.field, f32[12,8,8,128]{3,2,1,0:T(8,128)S(1)} %collective-permute-done.19.lo, f32[12,8,8,128]{3,2,1,0:T(8,128)S(1)} %collective-permute-done.20.hi, ...), custom_call_target="tpu_custom_call" | custom-call | flops 8000000000 | bytes 24000000 | tf_op jit(solution)/shard_map/again_first/pallas_call | solution.py:400
  102.7 3.8 %collective-permute-start.25 = (f32[15,8,8,128]{3,2,1,0:T(8,128)S(1)}, f32[15,8,8,128]{3,2,1,0:T(8,128)S(1)}, u32[]{:S(2)}, u32[]{:S(2)}) collective-permute-start(f32[15,8,8,128]{3,2,1,0:T(8,128)S(1)} %get-tuple-element.93), channel_id=1, source_target_pairs={{0,4},{1,5},{2,6},{3,7},{4,8},{5,9},{6,10},{7,11},{8,12},{9,13},{1... | collective-permute-start | bytes 1474568 | tf_op jit(solution)/shard_map/ppermute | solution.py:420
  108.0 9.6 %collective-permute-done.25.lo = f32[15,8,8,128]{3,2,1,0:T(8,128)S(1)} collective-permute-done((f32[15,8,8,128]{3,2,1,0:T(8,128)S(1)}, f32[15,8,8,128]{3,2,1,0:T(8,128)S(1)}, u32[]{:S(2)}, u32[]{:S(2)}) %collective-permute-start.25) | collective-permute-done | bytes 491552 | tf_op jit(solution)/shard_map/ppermute | solution.py:420
  117.6 4.1 %collective-permute-done.26.hi = f32[15,8,8,128]{3,2,1,0:T(8,128)S(1)} collective-permute-done((f32[15,8,8,128]{3,2,1,0:T(8,128)S(1)}, f32[15,8,8,128]{3,2,1,0:T(8,128)S(1)}, u32[]{:S(2)}, u32[]{:S(2)}) %collective-permute-start.26) | collective-permute-done | bytes 491552 | tf_op jit(solution)/shard_map/ppermute | solution.py:423
  121.7 7.9 %again_second.1 = (f32[22,8,8,128]{3,2,1,0:T(8,128)S(1)}, f32[4,64,128]{2,1,0:T(8,128)S(1)}, f32[4,64,128]{2,1,0:T(8,128)S(1)}, f32[4,64,128]{2,1,0:T(8,128)S(1)}, f32[4,64,128]{2,1,0:T(8,128)S(1)}) custom-call(s32[2]{0:T(128)S(1)} %pad_add_fusion.where, f32[16,8,8,128]{3,2,1,0:T(8,128)S(1)} %get-tuple-element.82.field, ...), custom_call_target="tpu_custom_call" | custom-call | flops 8999999488 | bytes 27000000 | tf_op jit(solution)/shard_map/again_second/pallas_call | solution.py:400
  129.6 2.2 %collective-permute-done.27.other = f32[22,8,8,128]{3,2,1,0:T(8,128)S(1)} collective-permute-done((f32[22,8,8,128]{3,2,1,0:T(8,128)S(1)}, f32[22,8,8,128]{3,2,1,0:T(8,128)S(1)}, u32[]{:S(2)}, u32[]{:S(2)}) %collective-permute-start.27) | collective-permute-done | bytes 720928 | tf_op jit(solution)/shard_map/ppermute | solution.py:414
  131.8 1.9 %pairs.1.own = f32[16,4,8,128]{3,2,1,0:T(8,128)S(1)} custom-call(s32[2]{0:T(128)S(1)} %pad_add_fusion.where, f32[22,8,8,128]{3,2,1,0:T(8,128)S(1)} %get-tuple-element.100.mine, f32[22,8,8,128]{3,2,1,0:T(8,128)S(1)} %collective-permute-done.27.other, f32[46,8,8,128]{3,2,1,0:T(8,128)S(1)} %get-tuple-element.65.cond), custom_call_target="tpu_custom_call" | custom-call | flops 3000000000 | bytes 9000000 | tf_op jit(solution)/shard_map/pairs/pallas_call | solution.py:400
  133.8 2.4 %collective-permute-start.30 = (f32[16,4,8,128]{3,2,1,0:T(8,128)S(1)}, f32[16,4,8,128]{3,2,1,0:T(8,128)S(1)}, u32[]{:S(2)}, u32[]{:S(2)}) collective-permute-start(f32[16,4,8,128]{3,2,1,0:T(8,128)S(1)} %pairs.1.own), channel_id=1, source_target_pairs={{0,3},{1,2},{2,1},{3,0},{4,7},{5,6},{6,5},{7,4},{8,11},{9,10},{10,... | collective-permute-start | bytes 786440 | tf_op jit(solution)/shard_map/ppermute | solution.py:417
  137.3 6.6 %collective-permute-done.30.r3 = f32[16,4,8,128]{3,2,1,0:T(8,128)S(1)} collective-permute-done((f32[16,4,8,128]{3,2,1,0:T(8,128)S(1)}, f32[16,4,8,128]{3,2,1,0:T(8,128)S(1)}, u32[]{:S(2)}, u32[]{:S(2)}) %collective-permute-start.30) | collective-permute-done | bytes 262176 | tf_op jit(solution)/shard_map/ppermute | solution.py:417
  143.9 4.8 %collective-permute-done.29.r2 = f32[16,4,8,128]{3,2,1,0:T(8,128)S(1)} collective-permute-done((f32[16,4,8,128]{3,2,1,0:T(8,128)S(1)}, f32[16,4,8,128]{3,2,1,0:T(8,128)S(1)}, u32[]{:S(2)}, u32[]{:S(2)}) %collective-permute-start.29) | collective-permute-done | bytes 262176 | tf_op jit(solution)/shard_map/ppermute | solution.py:417
  151.1 2.5 %collective-permute-start.31 = (f32[27,4,8,128]{3,2,1,0:T(8,128)S(1)}, f32[27,4,8,128]{3,2,1,0:T(8,128)S(1)}, u32[]{:S(2)}, u32[]{:S(2)}) collective-permute-start(f32[27,4,8,128]{3,2,1,0:T(8,128)S(1)} %get-tuple-element.103), channel_id=1, source_target_pairs={{0,4},{1,5},{2,6},{3,7},{4,8},{5,9},{6,10},{7,11},{8,12},{9,13},{1... | collective-permute-start | bytes 1327112 | tf_op jit(solution)/shard_map/ppermute | solution.py:420
  157.3 6.7 %collective-permute-done.37.refs_7_ = f32[4,64,128]{2,1,0:T(8,128)S(1)} collective-permute-done((f32[4,64,128]{2,1,0:T(8,128)S(1)}, f32[4,64,128]{2,1,0:T(8,128)S(1)}, u32[]{:S(2)}, u32[]{:S(2)}) %collective-permute-start.37) | collective-permute-done | bytes 131104 | tf_op jit(solution)/shard_map/ppermute | solution.py:417
  164.6 2.2 %collective-permute-done.32.got_hi = f32[27,4,8,128]{3,2,1,0:T(8,128)S(1)} collective-permute-done((f32[27,4,8,128]{3,2,1,0:T(8,128)S(1)}, f32[27,4,8,128]{3,2,1,0:T(8,128)S(1)}, u32[]{:S(2)}, u32[]{:S(2)}) %collective-permute-start.32) | collective-permute-done | bytes 442400 | tf_op jit(solution)/shard_map/ppermute | solution.py:423
  166.8 1.8 %collective-permute-done.35.other_hi = f32[27,4,8,128]{3,2,1,0:T(8,128)S(1)} collective-permute-done((f32[27,4,8,128]{3,2,1,0:T(8,128)S(1)}, f32[27,4,8,128]{3,2,1,0:T(8,128)S(1)}, u32[]{:S(2)}, u32[]{:S(2)}) %collective-permute-start.35) | collective-permute-done | bytes 442400 | tf_op jit(solution)/shard_map/ppermute | solution.py:414
  168.6 8.5 %chain.1 = (f32[4,4,64,128]{3,2,1,0:T(8,128)}, f32[4,4,64,128]{3,2,1,0:T(8,128)}) custom-call(s32[2]{0:T(128)S(1)} %pad_add_fusion.where, f32[48,4,8,128]{3,2,1,0:T(8,128)S(1)} %get-tuple-element.102.sums, f32[27,4,8,128]{3,2,1,0:T(8,128)S(1)} %collective-permute-done.31.got_lo, f32[27,4,8,128]{3,2,1,0:T(8,128)S(1)} %collective-permute-done.32.got_hi, ...), custom_call_target="tpu_custom_call" | custom-call | flops 8999999488 | bytes 27000000 | tf_op jit(solution)/shard_map/chain/pallas_call | solution.py:400
  (76 shorter events, 29.3 us)
Async XLA Ops:
  0.6 7.9 %collective-permute-start.1 = (f32[4,4,64,128]{3,2,1,0:T(8,128)}, f32[4,4,64,128]{3,2,1,0:T(8,128)S(1)}, u32[]{:S(2)}, u32[]{:S(2)}) collective-permute-start(f32[4,4,64,128]{3,2,1,0:T(8,128)} %param.6), channel_id=1, source_target_pairs={{0,16},{16,0},{1,17},{17,1},{2,18},{18,2},{3,19},{19,3},{4,20},{20... | collective-permute-start | bytes 1572872 | tf_op jit(solution)/shard_map/ppermute | solution.py:414
  2.1 11.4 %collective-permute-start.6 = (f32[4,64,128]{2,1,0:T(8,128)S(1)}, f32[4,64,128]{2,1,0:T(8,128)S(1)}, u32[]{:S(2)}, u32[]{:S(2)}) collective-permute-start(f32[4,64,128]{2,1,0:T(8,128)S(1)} %broadcast_select_fusion.2), channel_id=1, source_target_pairs={{4,0},{5,1},{6,2},{7,3},{8,4},{9,5},{10,6},{11,7},{12,8},{13,9},{1... | collective-permute-start | bytes 393224 | tf_op jit(solution)/shard_map/ppermute | solution.py:423
  3.4 10.1 %collective-permute-start.5 = (f32[4,64,128]{2,1,0:T(8,128)S(1)}, f32[4,64,128]{2,1,0:T(8,128)S(1)}, u32[]{:S(2)}, u32[]{:S(2)}) collective-permute-start(f32[4,64,128]{2,1,0:T(8,128)S(1)} %broadcast_select_fusion.2), channel_id=1, source_target_pairs={{0,4},{1,5},{2,6},{3,7},{4,8},{5,9},{6,10},{7,11},{8,12},{9,13},{1... | collective-permute-start | bytes 393224 | tf_op jit(solution)/shard_map/ppermute | solution.py:420
  9.9 6.8 %collective-permute-start.4 = (f32[4,64,128]{2,1,0:T(8,128)S(1)}, f32[4,64,128]{2,1,0:T(8,128)S(1)}, u32[]{:S(2)}, u32[]{:S(2)}) collective-permute-start(f32[4,64,128]{2,1,0:T(8,128)S(1)} %get-tuple-element.110), channel_id=1, source_target_pairs={{0,3},{1,2},{2,1},{3,0},{4,7},{5,6},{6,5},{7,4},{8,11},{9,10},{10,... | collective-permute-start | bytes 393224 | tf_op jit(solution)/shard_map/ppermute | solution.py:417
  12.8 6.4 %collective-permute-start.3 = (f32[4,64,128]{2,1,0:T(8,128)S(1)}, f32[4,64,128]{2,1,0:T(8,128)S(1)}, u32[]{:S(2)}, u32[]{:S(2)}) collective-permute-start(f32[4,64,128]{2,1,0:T(8,128)S(1)} %get-tuple-element.111), channel_id=1, source_target_pairs={{0,2},{1,3},{2,0},{3,1},{4,6},{5,7},{6,4},{7,5},{8,10},{9,11},{10,... | collective-permute-start | bytes 393224 | tf_op jit(solution)/shard_map/ppermute | solution.py:417
  19.5 13.0 %collective-permute-start.11 = (f32[12,64,128]{2,1,0:T(8,128)S(1)}, f32[12,64,128]{2,1,0:T(8,128)S(1)}, u32[]{:S(2)}, u32[]{:S(2)}) collective-permute-start(f32[12,64,128]{2,1,0:T(8,128)S(1)} %pad_maximum_fusion.3.m0), channel_id=1, source_target_pairs={{0,3},{1,2},{2,1},{3,0},{4,7},{5,6},{6,5},{7,4},{8,11},{9,10},{10,... | collective-permute-start | bytes 1179656 | tf_op jit(solution)/shard_map/ppermute | solution.py:417
  21.1 18.6 %collective-permute-start.10 = (f32[12,64,128]{2,1,0:T(8,128)S(1)}, f32[12,64,128]{2,1,0:T(8,128)S(1)}, u32[]{:S(2)}, u32[]{:S(2)}) collective-permute-start(f32[12,64,128]{2,1,0:T(8,128)S(1)} %pad_maximum_fusion.3.m0), channel_id=1, source_target_pairs={{0,2},{1,3},{2,0},{3,1},{4,6},{5,7},{6,4},{7,5},{8,10},{9,11},{10,... | collective-permute-start | bytes 1179656 | tf_op jit(solution)/shard_map/ppermute | solution.py:417
  22.5 17.4 %collective-permute-start.9 = (f32[12,64,128]{2,1,0:T(8,128)S(1)}, f32[12,64,128]{2,1,0:T(8,128)S(1)}, u32[]{:S(2)}, u32[]{:S(2)}) collective-permute-start(f32[12,64,128]{2,1,0:T(8,128)S(1)} %pad_maximum_fusion.3.m0), channel_id=1, source_target_pairs={{0,1},{1,0},{2,3},{3,2},{4,5},{5,4},{6,7},{7,6},{8,9},{9,8},{10,11... | collective-permute-start | bytes 1179656 | tf_op jit(solution)/shard_map/ppermute | solution.py:417
  24.5 15.7 %collective-permute-start.7 = (f32[12,8,8,128]{3,2,1,0:T(8,128)}, f32[12,8,8,128]{3,2,1,0:T(8,128)S(1)}, u32[]{:S(2)}, u32[]{:S(2)}) collective-permute-start(f32[12,8,8,128]{3,2,1,0:T(8,128)} %get-tuple-element.61), channel_id=1, source_target_pairs={{0,4},{1,5},{2,6},{3,7},{4,8},{5,9},{6,10},{7,11},{8,12},{9,13},{1... | collective-permute-start | bytes 1179656 | tf_op jit(solution)/shard_map/ppermute | solution.py:420
  29.2 12.4 %collective-permute-start.12 = (f32[12,64,128]{2,1,0:T(8,128)S(1)}, f32[12,64,128]{2,1,0:T(8,128)S(1)}, u32[]{:S(2)}, u32[]{:S(2)}) collective-permute-start(f32[12,64,128]{2,1,0:T(8,128)S(1)} %pad_maximum_fusion.3.m0), channel_id=1, source_target_pairs={{0,16},{16,0},{1,17},{17,1},{2,18},{18,2},{3,19},{19,3},{4,20},{20... | collective-permute-start | bytes 1179656 | tf_op jit(solution)/shard_map/ppermute | solution.py:414
  32.4 10.5 %collective-permute-start.15 = (f32[12,64,128]{2,1,0:T(8,128)S(1)}, f32[12,64,128]{2,1,0:T(8,128)}, u32[]{:S(2)}, u32[]{:S(2)}) collective-permute-start(f32[12,64,128]{2,1,0:T(8,128)S(1)} %collective-permute-done.11.m3), channel_id=1, source_target_pairs={{0,16},{16,0},{1,17},{17,1},{2,18},{18,2},{3,19},{19,3},{4,20},{20... | collective-permute-start | bytes 1179656 | tf_op jit(solution)/shard_map/ppermute | solution.py:414
  40.2 13.2 %collective-permute-start.8 = (f32[12,8,8,128]{3,2,1,0:T(8,128)S(1)}, f32[12,8,8,128]{3,2,1,0:T(8,128)S(1)}, u32[]{:S(2)}, u32[]{:S(2)}) collective-permute-start(f32[12,8,8,128]{3,2,1,0:T(8,128)S(1)} %get-tuple-element.63), channel_id=1, source_target_pairs={{4,0},{5,1},{6,2},{7,3},{8,4},{9,5},{10,6},{11,7},{12,8},{13,9},{1... | collective-permute-start | bytes 1179656 | tf_op jit(solution)/shard_map/ppermute | solution.py:423
  41.6 18.3 %collective-permute-start.16 = (f32[16,8,8,128]{3,2,1,0:T(8,128)S(1)}, f32[16,8,8,128]{3,2,1,0:T(8,128)S(1)}, u32[]{:S(2)}, u32[]{:S(2)}) collective-permute-start(f32[16,8,8,128]{3,2,1,0:T(8,128)S(1)} %get-tuple-element.68.field), channel_id=1, source_target_pairs={{16,0},{17,1},{18,2},{19,3},{20,4},{21,5},{22,6},{23,7},{24,8},{25... | collective-permute-start | bytes 1572872 | tf_op jit(solution)/shard_map/ppermute | solution.py:460
  59.9 11.3 %collective-permute-start.17 = (f32[12,8,8,128]{3,2,1,0:T(8,128)S(1)}, f32[12,8,8,128]{3,2,1,0:T(8,128)S(1)}, u32[]{:S(2)}, u32[]{:S(2)}) collective-permute-start(f32[12,8,8,128]{3,2,1,0:T(8,128)S(1)} %get-tuple-element.71), channel_id=1, source_target_pairs={{0,4},{1,5},{2,6},{3,7},{4,8},{5,9},{6,10},{7,11},{8,12},{9,13},{1... | collective-permute-start | bytes 1179656 | tf_op jit(solution)/shard_map/ppermute | solution.py:420
  63.4 11.9 %collective-permute-start.18 = (f32[12,8,8,128]{3,2,1,0:T(8,128)S(1)}, f32[12,8,8,128]{3,2,1,0:T(8,128)S(1)}, u32[]{:S(2)}, u32[]{:S(2)}) collective-permute-start(f32[12,8,8,128]{3,2,1,0:T(8,128)S(1)} %get-tuple-element.72), channel_id=1, source_target_pairs={{4,0},{5,1},{6,2},{7,3},{8,4},{9,5},{10,6},{11,7},{12,8},{13,9},{1... | collective-permute-start | bytes 1179656 | tf_op jit(solution)/shard_map/ppermute | solution.py:423
  82.6 10.0 %collective-permute-start.19 = (f32[12,8,8,128]{3,2,1,0:T(8,128)S(1)}, f32[12,8,8,128]{3,2,1,0:T(8,128)S(1)}, u32[]{:S(2)}, u32[]{:S(2)}) collective-permute-start(f32[12,8,8,128]{3,2,1,0:T(8,128)S(1)} %get-tuple-element.79), channel_id=1, source_target_pairs={{0,4},{1,5},{2,6},{3,7},{4,8},{5,9},{6,10},{7,11},{8,12},{9,13},{1... | collective-permute-start | bytes 1179656 | tf_op jit(solution)/shard_map/ppermute | solution.py:420
  86.1 10.7 %collective-permute-start.20 = (f32[12,8,8,128]{3,2,1,0:T(8,128)S(1)}, f32[12,8,8,128]{3,2,1,0:T(8,128)S(1)}, u32[]{:S(2)}, u32[]{:S(2)}) collective-permute-start(f32[12,8,8,128]{3,2,1,0:T(8,128)S(1)} %get-tuple-element.81), channel_id=1, source_target_pairs={{4,0},{5,1},{6,2},{7,3},{8,4},{9,5},{10,6},{11,7},{12,8},{13,9},{1... | collective-permute-start | bytes 1179656 | tf_op jit(solution)/shard_map/ppermute | solution.py:423
  92.7 9.8 %collective-permute-start.21 = (f32[4,64,128]{2,1,0:T(8,128)S(1)}, f32[4,64,128]{2,1,0:T(8,128)S(1)}, u32[]{:S(2)}, u32[]{:S(2)}) collective-permute-start(f32[4,64,128]{2,1,0:T(8,128)S(1)} %get-tuple-element.84), channel_id=1, source_target_pairs={{0,1},{1,0},{2,3},{3,2},{4,5},{5,4},{6,7},{7,6},{8,9},{9,8},{10,11... | collective-permute-start | bytes 393224 | tf_op jit(solution)/shard_map/ppermute | solution.py:417
  93.9 8.6 %collective-permute-start.22 = (f32[4,64,128]{2,1,0:T(8,128)S(1)}, f32[4,64,128]{2,1,0:T(8,128)S(1)}, u32[]{:S(2)}, u32[]{:S(2)}) collective-permute-start(f32[4,64,128]{2,1,0:T(8,128)S(1)} %get-tuple-element.85), channel_id=1, source_target_pairs={{0,2},{1,3},{2,0},{3,1},{4,6},{5,7},{6,4},{7,5},{8,10},{9,11},{10,... | collective-permute-start | bytes 393224 | tf_op jit(solution)/shard_map/ppermute | solution.py:417
  95.6 7.0 %collective-permute-start.23 = (f32[4,64,128]{2,1,0:T(8,128)S(1)}, f32[4,64,128]{2,1,0:T(8,128)S(1)}, u32[]{:S(2)}, u32[]{:S(2)}) collective-permute-start(f32[4,64,128]{2,1,0:T(8,128)S(1)} %get-tuple-element.86), channel_id=1, source_target_pairs={{0,3},{1,2},{2,1},{3,0},{4,7},{5,6},{6,5},{7,4},{8,11},{9,10},{10,... | collective-permute-start | bytes 393224 | tf_op jit(solution)/shard_map/ppermute | solution.py:417
  102.6 14.9 %collective-permute-start.24 = (f32[16,64,128]{2,1,0:T(8,128)S(1)}, f32[16,64,128]{2,1,0:T(8,128)S(1)}, u32[]{:S(2)}, u32[]{:S(2)}) collective-permute-start(f32[16,64,128]{2,1,0:T(8,128)S(1)} %pad_maximum_fusion.1), channel_id=1, source_target_pairs={{0,16},{16,0},{1,17},{17,1},{2,18},{18,2},{3,19},{19,3},{4,20},{20... | collective-permute-start | bytes 1572872 | tf_op jit(solution)/shard_map/ppermute | solution.py:414
  102.7 14.9 %collective-permute-start.25 = (f32[15,8,8,128]{3,2,1,0:T(8,128)S(1)}, f32[15,8,8,128]{3,2,1,0:T(8,128)S(1)}, u32[]{:S(2)}, u32[]{:S(2)}) collective-permute-start(f32[15,8,8,128]{3,2,1,0:T(8,128)S(1)} %get-tuple-element.93), channel_id=1, source_target_pairs={{0,4},{1,5},{2,6},{3,7},{4,8},{5,9},{6,10},{7,11},{8,12},{9,13},{1... | collective-permute-start | bytes 1474568 | tf_op jit(solution)/shard_map/ppermute | solution.py:420
  106.5 15.2 %collective-permute-start.26 = (f32[15,8,8,128]{3,2,1,0:T(8,128)S(1)}, f32[15,8,8,128]{3,2,1,0:T(8,128)S(1)}, u32[]{:S(2)}, u32[]{:S(2)}) collective-permute-start(f32[15,8,8,128]{3,2,1,0:T(8,128)S(1)} %get-tuple-element.95), channel_id=1, source_target_pairs={{4,0},{5,1},{6,2},{7,3},{8,4},{9,5},{10,6},{11,7},{12,8},{13,9},{1... | collective-permute-start | bytes 1474568 | tf_op jit(solution)/shard_map/ppermute | solution.py:423
  133.8 10.2 %collective-permute-start.30 = (f32[16,4,8,128]{3,2,1,0:T(8,128)S(1)}, f32[16,4,8,128]{3,2,1,0:T(8,128)S(1)}, u32[]{:S(2)}, u32[]{:S(2)}) collective-permute-start(f32[16,4,8,128]{3,2,1,0:T(8,128)S(1)} %pairs.1.own), channel_id=1, source_target_pairs={{0,3},{1,2},{2,1},{3,0},{4,7},{5,6},{6,5},{7,4},{8,11},{9,10},{10,... | collective-permute-start | bytes 786440 | tf_op jit(solution)/shard_map/ppermute | solution.py:417
  136.2 12.5 %collective-permute-start.29 = (f32[16,4,8,128]{3,2,1,0:T(8,128)S(1)}, f32[16,4,8,128]{3,2,1,0:T(8,128)S(1)}, u32[]{:S(2)}, u32[]{:S(2)}) collective-permute-start(f32[16,4,8,128]{3,2,1,0:T(8,128)S(1)} %pairs.1.own), channel_id=1, source_target_pairs={{0,2},{1,3},{2,0},{3,1},{4,6},{5,7},{6,4},{7,5},{8,10},{9,11},{10,... | collective-permute-start | bytes 786440 | tf_op jit(solution)/shard_map/ppermute | solution.py:417
  136.6 12.1 %collective-permute-start.28 = (f32[16,4,8,128]{3,2,1,0:T(8,128)S(1)}, f32[16,4,8,128]{3,2,1,0:T(8,128)S(1)}, u32[]{:S(2)}, u32[]{:S(2)}) collective-permute-start(f32[16,4,8,128]{3,2,1,0:T(8,128)S(1)} %pairs.1.own), channel_id=1, source_target_pairs={{0,1},{1,0},{2,3},{3,2},{4,5},{5,4},{6,7},{7,6},{8,9},{9,8},{10,11... | collective-permute-start | bytes 786440 | tf_op jit(solution)/shard_map/ppermute | solution.py:417
  149.5 6.6 %collective-permute-start.36 = (f32[4,64,128]{2,1,0:T(8,128)S(1)}, f32[4,64,128]{2,1,0:T(8,128)S(1)}, u32[]{:S(2)}, u32[]{:S(2)}) collective-permute-start(f32[4,64,128]{2,1,0:T(8,128)S(1)} %get-tuple-element.107), channel_id=1, source_target_pairs={{0,1},{1,0},{2,3},{3,2},{4,5},{5,4},{6,7},{7,6},{8,9},{9,8},{10,11... | collective-permute-start | bytes 393224 | tf_op jit(solution)/shard_map/ppermute | solution.py:417
  151.1 13.0 %collective-permute-start.31 = (f32[27,4,8,128]{3,2,1,0:T(8,128)S(1)}, f32[27,4,8,128]{3,2,1,0:T(8,128)S(1)}, u32[]{:S(2)}, u32[]{:S(2)}) collective-permute-start(f32[27,4,8,128]{3,2,1,0:T(8,128)S(1)} %get-tuple-element.103), channel_id=1, source_target_pairs={{0,4},{1,5},{2,6},{3,7},{4,8},{5,9},{6,10},{7,11},{8,12},{9,13},{1... | collective-permute-start | bytes 1327112 | tf_op jit(solution)/shard_map/ppermute | solution.py:420
  153.6 13.2 %collective-permute-start.32 = (f32[27,4,8,128]{3,2,1,0:T(8,128)S(1)}, f32[27,4,8,128]{3,2,1,0:T(8,128)S(1)}, u32[]{:S(2)}, u32[]{:S(2)}) collective-permute-start(f32[27,4,8,128]{3,2,1,0:T(8,128)S(1)} %get-tuple-element.104), channel_id=1, source_target_pairs={{4,0},{5,1},{6,2},{7,3},{8,4},{9,5},{10,6},{11,7},{12,8},{13,9},{1... | collective-permute-start | bytes 1327112 | tf_op jit(solution)/shard_map/ppermute | solution.py:423
  155.2 11.6 %collective-permute-start.33 = (f32[48,4,8,128]{3,2,1,0:T(8,128)S(1)}, f32[48,4,8,128]{3,2,1,0:T(8,128)S(1)}, u32[]{:S(2)}, u32[]{:S(2)}) collective-permute-start(f32[48,4,8,128]{3,2,1,0:T(8,128)S(1)} %get-tuple-element.102.sums), channel_id=1, source_target_pairs={{0,16},{16,0},{1,17},{17,1},{2,18},{18,2},{3,19},{19,3},{4,20},{20... | collective-permute-start | bytes 2359304 | tf_op jit(solution)/shard_map/ppermute | solution.py:414
  155.2 8.7 %collective-permute-start.37 = (f32[4,64,128]{2,1,0:T(8,128)S(1)}, f32[4,64,128]{2,1,0:T(8,128)S(1)}, u32[]{:S(2)}, u32[]{:S(2)}) collective-permute-start(f32[4,64,128]{2,1,0:T(8,128)S(1)} %get-tuple-element.108), channel_id=1, source_target_pairs={{0,2},{1,3},{2,0},{3,1},{4,6},{5,7},{6,4},{7,5},{8,10},{9,11},{10,... | collective-permute-start | bytes 393224 | tf_op jit(solution)/shard_map/ppermute | solution.py:417
  156.1 7.9 %collective-permute-start.38 = (f32[4,64,128]{2,1,0:T(8,128)S(1)}, f32[4,64,128]{2,1,0:T(8,128)S(1)}, u32[]{:S(2)}, u32[]{:S(2)}) collective-permute-start(f32[4,64,128]{2,1,0:T(8,128)S(1)} %get-tuple-element.109), channel_id=1, source_target_pairs={{0,3},{1,2},{2,1},{3,0},{4,7},{5,6},{6,5},{7,4},{8,11},{9,10},{10,... | collective-permute-start | bytes 393224 | tf_op jit(solution)/shard_map/ppermute | solution.py:417
  (12 other events, 136.3 us)
